TPU v7x, 32 devices: a whole 2x2x4 slice. The times are simulated.
32 devices in a mesh: frag: 2 (over x), col: 16 (over z, y, core).
Axes of the slice: x: 2, y: 2, z: 4, core: 2. Of those that a mesh axis runs over, the one named last changes fastest.
Arguments:
- amplitudes: bfloat16 [64, 256, 256], P(('frag', 'col')), parts along dimension 0, may hold values from -6 to 6
- integrals: bfloat16 [64, 256, 256], P(('frag', 'col')), parts along dimension 0, may hold values from -6 to 6
- energies: float32 [64, 256], P(('frag', 'col')), parts along dimension 0, may hold values from 0.5 to 4
- pno_size: int32 [64], P(('frag', 'col')), parts along dimension 0, may hold values from 128 to 256, as said below
- subspace_transfers: bfloat16 [2048, 256, 256], P(('frag', 'col')), parts along dimension 0, may hold values from -0.375 to 0.375
- tile_source: int32 [2048], P(('frag', 'col')), parts along dimension 0, may hold values from 0 to 15
- tile_owner: int32 [2048], P(('frag', 'col')), parts along dimension 0, may hold values from 0 to 15, as said below
- dispatch_table: int32 [32, 16], P('frag'), parts along dimension 0, may hold values from -1 to 1, as said below
- result_list: int32 [32, 16], P('frag'), parts along dimension 0, may hold values from -1 to 1, as said below
Outputs:
- residual: float32 [64, 256, 256], P(('frag', 'col')), parts along dimension 0
There are 2 independent parts, one for each index of `frag`. A program takes and returns all parts, laid end to end along the dimension named above; each array names one. Nothing has to cross between parts.
Inputs may be any that keep to these rules, and one draw needn't show every extreme that they name: `pno_size`: each pair keeps either 256/2 or 256 PNOs. `dispatch_table`: -1 marks a device that couples to no pair of that source device. `result_list`: -1 marks no target pair; entry [d, o] is -1 unless (o - d) mod 16 lies in 1 to 8. `tile_owner`: A tile of device d has an owner o with (o - d) mod 16 in 1 to 8; the first tile of each device has the owner 16/2 away.
All inputs are finite; a program needn't handle non-finite values.
Results may differ from a plain program's by a relative error of at most 0.0075.
Values may be sent and summed in bfloat16 or wider, within the bound.
No kernel may reach another device: no remote copies, remote signals or barrier semaphores. Data moves between devices by JAX's collectives and lax.ppermute only.
A program may use at most 128 MiB of HBM per device.

v0:
```python
import functools

import jax
import jax.numpy as jnp
from jax import lax
from jax.experimental import pallas as pl
from jax.experimental.pallas import tpu as pltpu
from jax.sharding import PartitionSpec as P

GROUP = 4
UNROLL = 8

VMEM = functools.partial(pl.BlockSpec, memory_space=pltpu.VMEM)
SMEM = functools.partial(pl.BlockSpec, memory_space=pltpu.SMEM)
HBM = functools.partial(pl.BlockSpec, memory_space=pl.ANY)


def inside(size, shape):
    rows = lax.broadcasted_iota(jnp.int32, shape, 0)
    lanes = lax.broadcasted_iota(jnp.int32, shape, 1)
    return (rows < size) & (lanes < size)


def mask_kernel(size_ref, amplitude_ref, masked_ref):
    for p in range(masked_ref.shape[0]):
        held = inside(size_ref[p], masked_ref.shape[1:])
        value = jnp.where(held, amplitude_ref[p].astype(jnp.float32), 0.0)
        masked_ref[p] = value.astype(masked_ref.dtype)


def base_kernel(size_ref, energy_ref, integral_ref, masked_ref, base_ref):
    shape = base_ref.shape[1:]
    for p in range(base_ref.shape[0]):
        across = jnp.broadcast_to(energy_ref[p : p + 1, :], shape)
        denominator = across.T + across
        value = integral_ref[p].astype(jnp.float32) + denominator * masked_ref[p].astype(jnp.float32)
        base_ref[p] = jnp.where(inside(size_ref[p], shape), value, 0.0)


def list_kernel(
    columns, pairs, me_ref, source_ref, owner_ref, dispatch_ref, result_ref, list_ref, pair_ref
):
    tiles = source_ref.shape[0]
    depth = columns // GROUP
    half = depth // 2
    me = me_ref[0]
    z, g = me // GROUP, me % GROUP

    def fill(i, _):
        list_ref[0, i] = 0
        list_ref[1, i] = 0
        list_ref[2, i] = columns // 2
        return 0

    lax.fori_loop(0, tiles, fill, 0)

    def visit(t, count):
        s, o = source_ref[t], owner_ref[t]
        pair = dispatch_ref[s, me]
        live = (pair >= 0) & (result_ref[me, o] >= 0)

        @pl.when(live)
        def _():
            far = (s // GROUP - z + depth) % depth
            ahead = (o // GROUP - z + depth) % half
            list_ref[0, count] = t
            list_ref[1, count] = (far * GROUP + (g ^ (s % GROUP))) * pairs + jnp.maximum(pair, 0)
            list_ref[2, count] = ahead * GROUP + (g ^ (o % GROUP))

        return count + live.astype(jnp.int32)

    count = lax.fori_loop(0, tiles, visit, jnp.int32(0))
    list_ref[3, 0] = count
    for steps in range(half + 1):
        for m in range(GROUP):
            pair_ref[steps, m] = result_ref[z * GROUP + (g ^ m), (z + steps) % depth * GROUP + g]


def tiles_kernel(list_ref, masked_ref, transfer_ref, block_ref, held, total, arrived):
    count = list_ref[3, 0]
    steps = (count + UNROLL - 1) // UNROLL

    def copy(i):
        return pltpu.make_async_copy(transfer_ref.at[list_ref[0, i]], held.at[i], arrived.at[i])

    def fetch(i, _):
        copy(i).start()
        return 0

    lax.fori_loop(0, steps * UNROLL, fetch, 0)
    total[...] = jnp.zeros_like(total)

    def step(n, _):
        places = [n * UNROLL + u for u in range(UNROLL)]
        for i in places:
            copy(i).wait()
        halves = [
            jnp.dot(held[i], masked_ref[list_ref[1, i]], preferred_element_type=jnp.float32)
            for i in places
        ]
        for i, half in zip(places, halves):
            total[list_ref[2, i]] += lax.dot_general(
                half.astype(jnp.bfloat16),
                held[i],
                (((1,), (1,)), ((), ())),
                preferred_element_type=jnp.float32,
            )
        return 0

    lax.fori_loop(0, steps, step, 0)
    for b in range(block_ref.shape[0]):
        block_ref[b] = total[b].astype(block_ref.dtype)


def shards(
    amplitudes,
    integrals,
    energies,
    pno_size,
    subspace_transfers,
    tile_source,
    tile_owner,
    dispatch_table,
    result_list,
):
    pairs, width = amplitudes.shape[:2]
    tiles = subspace_transfers.shape[0]
    columns = lax.axis_size("col")
    depth = columns // GROUP
    half = depth // 2
    me = lax.axis_index("col").astype(jnp.int32)
    z, g = me // GROUP, me % GROUP

    def swap(value, m):
        return lax.ppermute(value, "col", [(i, i ^ m) for i in range(columns)])

    def ahead(value, steps):
        return lax.ppermute(
            value, "col", [(i, (i + steps * GROUP) % columns) for i in range(columns)]
        )

    masked = pl.pallas_call(
        mask_kernel,
        out_shape=jax.ShapeDtypeStruct(amplitudes.shape, jnp.bfloat16),
        in_specs=[SMEM(), VMEM()],
        out_specs=VMEM(),
        name="mask",
    )(pno_size, amplitudes)

    lane = [masked] + [ahead(masked, -far) for far in range(1, depth)]
    across = [swap(part, 2) for part in lane]
    both = [jnp.stack([a, b]) for a, b in zip(lane, across)]
    other = [swap(part, 1) for part in both]
    everyone = jnp.stack(
        [jnp.stack([a[0], b[0], a[1], b[1]]) for a, b in zip(both, other)]
    ).reshape(columns * pairs, width, width)

    tile_list, fed = pl.pallas_call(
        functools.partial(list_kernel, columns, pairs),
        out_shape=[
            jax.ShapeDtypeStruct((4, tiles), jnp.int32),
            jax.ShapeDtypeStruct((half + 1, GROUP), jnp.int32),
        ],
        in_specs=[SMEM()] * 5,
        out_specs=[SMEM(), SMEM()],
        name="tile_list",
    )(me[None], tile_source, tile_owner, dispatch_table, result_list)

    blocks = pl.pallas_call(
        tiles_kernel,
        out_shape=jax.ShapeDtypeStruct((columns // 2, width, width), jnp.bfloat16),
        in_specs=[SMEM(), VMEM(), HBM()],
        out_specs=VMEM(),
        scratch_shapes=[
            pltpu.VMEM((tiles, width, width), jnp.bfloat16),
            pltpu.VMEM((columns // 2 + 1, width, width), jnp.float32),
            pltpu.SemaphoreType.DMA((tiles,)),
        ],
        compiler_params=pltpu.CompilerParams(vmem_limit_bytes=48 * 2**20),
        cost_estimate=pl.CostEstimate(
            flops=4 * tiles * width**3, bytes_accessed=2 * tiles * width**2, transcendentals=0
        ),
        name="tiles",
    )(tile_list, everyone, subspace_transfers)

    near = (g ^ jnp.arange(GROUP, dtype=jnp.int32)) < g
    stays = jnp.where(near, fed[0], -1)
    onward = jnp.concatenate([jnp.where(near, -1, fed[half])[None], fed[1:half]])
    pair_ids = jnp.arange(pairs, dtype=jnp.int32)

    def by_pair(parts, fed_pairs):
        chosen = (fed_pairs[:, None] == pair_ids)[:, :, None, None]
        terms = [jnp.where(chosen[m], parts[m].astype(jnp.float32), 0.0) for m in range(GROUP)]
        return functools.reduce(jnp.add, terms)

    coupled = []
    for row in range(half):
        block = [blocks[row * GROUP + m] for m in range(GROUP)]
        block = [block[0]] + [swap(block[m], m) for m in range(1, GROUP)]
        sums = by_pair(block, onward[row]).astype(jnp.bfloat16)
        if row == 0:
            coupled.append(by_pair(block, stays))
        coupled.append(ahead(sums, row if row else half))

    base = pl.pallas_call(
        base_kernel,
        out_shape=jax.ShapeDtypeStruct(amplitudes.shape, jnp.float32),
        in_specs=[SMEM(), VMEM(), VMEM(), VMEM()],
        out_specs=VMEM(),
        name="base",
    )(pno_size, energies, integrals, masked)

    total = functools.reduce(jnp.add, [part.astype(jnp.float32) for part in coupled], base)
    lanes = jnp.arange(width, dtype=jnp.int32)
    held = lanes[None, :] < pno_size[:, None]
    return jnp.where(held[:, :, None] & held[:, None, :], total, 0.0)


def solution(mesh):
    placed = (
        P(("frag", "col"), None, None),
        P(("frag", "col"), None, None),
        P(("frag", "col"), None),
        P(("frag", "col")),
        P(("frag", "col"), None, None),
        P(("frag", "col")),
        P(("frag", "col")),
        P("frag", None),
        P("frag", None),
    )
    return jax.shard_map(
        shards,
        mesh=mesh,
        in_specs=placed,
        out_specs=P(("frag", "col"), None, None),
        check_vma=False,
    )
```

profile of v0, /device:TPU:0, one launch (start us, length us, event | category | flops | bytes accessed | tf_op | source)
XLA Modules:
  0.0 83.4 jit_solution(2170692218574380585)
XLA Ops:
  0.0 1.7 %mask.1.masked_ref = bf16[2,256,256]{2,1,0:T(8,128)(2,1)} custom-call(s32[2]{0:T(128)} %size_ref.3, bf16[2,256,256]{2,1,0:T(8,128)(2,1)} %amplitude_ref.1), custom_call_target="tpu_custom_call" | custom-call | tf_op jit(solution)/shard_map/mask/pallas_call | solution.py:142
  1.7 5.0 %collective-permute-start.2 = (bf16[2,256,256]{2,1,0:T(8,128)(2,1)}, bf16[2,256,256]{2,1,0:T(8,128)(2,1)S(1)}, u32[]{:S(2)}, u32[]{:S(2)}) collective-permute-start(bf16[2,256,256]{2,1,0:T(8,128)(2,1)} %mask.1.masked_ref), channel_id=1, source_target_pairs={{0,12},{1,13},{2,14},{3,15},{4,0},{5,1},{6,2},{7,3},{8,4},{9,5},{1... | collective-permute-start | bytes 786440 | tf_op jit(solution)/shard_map/ppermute | solution.py:138
  6.8 0.0 collective-permute-start.5
  6.8 1.0 %collective-permute-start.8 = (bf16[2,256,256]{2,1,0:T(8,128)(2,1)}, bf16[2,256,256]{2,1,0:T(8,128)(2,1)S(1)}, u32[]{:S(2)}, u32[]{:S(2)}) collective-permute-start(bf16[2,256,256]{2,1,0:T(8,128)(2,1)} %mask.1.masked_ref), channel_id=1, source_target_pairs={{0,4},{1,5},{2,6},{3,7},{4,8},{5,9},{6,10},{7,11},{8,12},{9,13},{1... | collective-permute-start | bytes 786440 | tf_op jit(solution)/shard_map/ppermute | solution.py:138
  7.8 1.5 %collective-permute-start = (bf16[2,256,256]{2,1,0:T(8,128)(2,1)}, bf16[2,256,256]{2,1,0:T(8,128)(2,1)S(1)}, u32[]{:S(2)}, u32[]{:S(2)}) collective-permute-start(bf16[2,256,256]{2,1,0:T(8,128)(2,1)} %mask.1.masked_ref), channel_id=1, source_target_pairs={{0,2},{1,3},{2,0},{3,1},{4,6},{5,7},{6,4},{7,5},{8,10},{9,11},{10,... | collective-permute-start | bytes 786440 | tf_op jit(solution)/shard_map/ppermute | solution.py:135
  9.3 4.2 %tile_list.1 = (s32[4,64]{1,0:T(4,128)}, s32[3,4]{1,0:T(4,128)}) custom-call(s32[1]{0:T(128)} %bitcast.me_ref, s32[64]{0:T(128)} %source_ref.1, s32[64]{0:T(128)} %owner_ref.1, s32[16,16]{1,0:T(8,128)} %dispatch_ref.1, s32[16,16]{1,0:T(8,128)} %result_ref.1), custom_call_target="tpu_custom_call" | custom-call | tf_op jit(solution)/shard_map/tile_list/pallas_call | solution.py:158
  13.5 0.7 slice_bitcast_fusion.20
  14.2 0.8 compare_select_fusion.1
  14.9 0.1 iota_compare_fusion.1
  15.0 0.0 collective-permute-done.2
  15.0 0.6 collective-permute-start.3
  15.6 0.0 collective-permute-done
  15.6 1.0 %pad_maximum_fusion.1 = bf16[2,2,256,256]{3,2,1,0:T(8,128)(2,1)S(1)} fusion(bf16[1,2,256,256]{3,2,1,0:T(8,128)(2,1)S(1)} %bitcast.79, bf16[1,2,256,256]{3,2,1,0:T(8,128)(2,1)} %bitcast.71), kind=kLoop, calls=%fused_computation.5 | loop fusion | flops 262144 | bytes 1048576 | tf_op jit(solution)/shard_map/stack | solution.py:152
  16.6 0.1 collective-permute-start.1
  16.7 12.6 %collective-permute-done.5 = bf16[2,256,256]{2,1,0:T(8,128)(2,1)S(1)} collective-permute-done((bf16[2,256,256]{2,1,0:T(8,128)(2,1)}, bf16[2,256,256]{2,1,0:T(8,128)(2,1)S(1)}, u32[]{:S(2)}, u32[]{:S(2)}) %collective-permute-start.5) | collective-permute-done | bytes 262176 | tf_op jit(solution)/shard_map/ppermute | solution.py:138
  29.3 1.5 %collective-permute-start.6 = (bf16[2,256,256]{2,1,0:T(8,128)(2,1)S(1)}, bf16[2,256,256]{2,1,0:T(8,128)(2,1)S(1)}, u32[]{:S(2)}, u32[]{:S(2)}) collective-permute-start(bf16[2,256,256]{2,1,0:T(8,128)(2,1)S(1)} %collective-permute-done.5), channel_id=1, source_target_pairs={{0,2},{1,3},{2,0},{3,1},{4,6},{5,7},{6,4},{7,5},{8,10},{9,11},{10,... | collective-permute-start | bytes 786440 | tf_op jit(solution)/shard_map/ppermute | solution.py:135
  30.8 0.0 collective-permute-done.8
  30.8 0.5 collective-permute-start.9
  31.3 0.1 iota_compare_fusion
  31.4 0.0 collective-permute-done.3
  31.4 0.1 pad_maximum_fusion.2
  31.5 0.1 collective-permute-start.4
  31.5 7.0 %collective-permute-done.6 = bf16[2,256,256]{2,1,0:T(8,128)(2,1)S(1)} collective-permute-done((bf16[2,256,256]{2,1,0:T(8,128)(2,1)S(1)}, bf16[2,256,256]{2,1,0:T(8,128)(2,1)S(1)}, u32[]{:S(2)}, u32[]{:S(2)}) %collective-permute-start.6) | collective-permute-done | bytes 262176 | tf_op jit(solution)/shard_map/ppermute | solution.py:135
  38.5 0.1 pad_maximum_fusion.3
  38.6 0.1 collective-permute-start.7
  38.7 3.4 %collective-permute-done.9 = bf16[2,256,256]{2,1,0:T(8,128)(2,1)S(1)} collective-permute-done((bf16[2,256,256]{2,1,0:T(8,128)(2,1)S(1)}, bf16[2,256,256]{2,1,0:T(8,128)(2,1)S(1)}, u32[]{:S(2)}, u32[]{:S(2)}) %collective-permute-start.9) | collective-permute-done | bytes 262176 | tf_op jit(solution)/shard_map/ppermute | solution.py:135
  42.1 0.1 pad_maximum_fusion.4
  42.1 0.1 collective-permute-start.10
  42.2 0.0 collective-permute-done.1
  42.3 0.0 copy-done.1
  42.3 0.1 maximum_bitcast_fusion
  42.4 0.0 collective-permute-done.4
  42.5 0.1 maximum_bitcast_fusion.1
  42.6 0.0 collective-permute-done.7
  42.7 0.1 maximum_bitcast_fusion.2
  42.8 1.3 %collective-permute-done.10 = bf16[2,2,256,256]{3,2,1,0:T(8,128)(2,1)S(1)} collective-permute-done((bf16[2,2,256,256]{3,2,1,0:T(8,128)(2,1)S(1)}, bf16[2,2,256,256]{3,2,1,0:T(8,128)(2,1)S(1)}, u32[]{:S(2)}, u32[]{:S(2)}) %collective-permute-start.10) | collective-permute-done | bytes 524320 | tf_op jit(solution)/shard_map/ppermute | solution.py:135
  44.2 0.1 maximum_bitcast_fusion.3
  44.3 0.0 copy-start
  44.3 0.6 pad_maximum_fusion
  44.9 0.1 copy-done
  45.0 6.4 %tiles.1 = bf16[8,256,256]{2,1,0:T(8,128)(2,1)S(1)} custom-call(s32[4,64]{1,0:T(4,128)S(1)} %copy-done, bf16[32,256,256]{2,1,0:T(8,128)(2,1)S(1)} %bitcast.70, bf16[64,256,256]{2,1,0:T(8,128)(2,1)} %transfer_ref.1), custom_call_target="tpu_custom_call" | custom-call | flops 4294967296 | bytes 8388608 | tf_op jit(solution)/shard_map/tiles/pallas_call | solution.py:169
  51.4 0.0 copy-start.2
  51.4 0.1 fusion.1
  51.5 0.1 collective-permute-start.11
  51.6 0.8 collective-permute-start.12
  52.4 1.1 %collective-permute-start.13 = (bf16[256,256]{1,0:T(8,128)(2,1)S(1)}, bf16[256,256]{1,0:T(8,128)(2,1)S(1)}, u32[]{:S(2)}, u32[]{:S(2)}) collective-permute-start(bf16[256,256]{1,0:T(8,128)(2,1)S(1)} %get-tuple-element.14), channel_id=1, source_target_pairs={{0,3},{1,2},{2,1},{3,0},{4,7},{5,6},{6,5},{7,4},{8,11},{9,10},{10,... | collective-permute-start | bytes 393224 | tf_op jit(solution)/shard_map/ppermute | solution.py:135
  53.5 0.4 collective-permute-start.15
  53.9 0.7 collective-permute-start.16
  54.6 0.0 collective-permute-done.11
  54.6 0.8 collective-permute-start.17
  55.4 2.5 %collective-permute-done.12 = bf16[256,256]{1,0:T(8,128)(2,1)S(1)} collective-permute-done((bf16[256,256]{1,0:T(8,128)(2,1)S(1)}, bf16[256,256]{1,0:T(8,128)(2,1)S(1)}, u32[]{:S(2)}, u32[]{:S(2)}) %collective-permute-start.12) | collective-permute-done | bytes 131104 | tf_op jit(solution)/shard_map/ppermute | solution.py:135
  58.0 1.9 %collective-permute-done.13 = bf16[256,256]{1,0:T(8,128)(2,1)S(1)} collective-permute-done((bf16[256,256]{1,0:T(8,128)(2,1)S(1)}, bf16[256,256]{1,0:T(8,128)(2,1)S(1)}, u32[]{:S(2)}, u32[]{:S(2)}) %collective-permute-start.13) | collective-permute-done | bytes 131104 | tf_op jit(solution)/shard_map/ppermute | solution.py:135
  59.9 0.2 add_convert_fusion.1
  60.1 1.3 %collective-permute-start.14 = (bf16[2,256,256]{2,1,0:T(8,128)(2,1)S(1)}, bf16[2,256,256]{2,1,0:T(8,128)(2,1)S(1)}, u32[]{:S(2)}, u32[]{:S(2)}) collective-permute-start(bf16[2,256,256]{2,1,0:T(8,128)(2,1)S(1)} %add_convert_fusion.1), channel_id=1, source_target_pairs={{0,8},{1,9},{2,10},{3,11},{4,12},{5,13},{6,14},{7,15},{8,0},{9,1},... | collective-permute-start | bytes 786440 | tf_op jit(solution)/shard_map/ppermute | solution.py:138
  61.4 0.0 collective-permute-done.15
  61.4 2.1 %collective-permute-done.16 = bf16[256,256]{1,0:T(8,128)(2,1)S(1)} collective-permute-done((bf16[256,256]{1,0:T(8,128)(2,1)S(1)}, bf16[256,256]{1,0:T(8,128)(2,1)S(1)}, u32[]{:S(2)}, u32[]{:S(2)}) %collective-permute-start.16) | collective-permute-done | bytes 131104 | tf_op jit(solution)/shard_map/ppermute | solution.py:135
  63.6 1.9 %collective-permute-done.17 = bf16[256,256]{1,0:T(8,128)(2,1)S(1)} collective-permute-done((bf16[256,256]{1,0:T(8,128)(2,1)S(1)}, bf16[256,256]{1,0:T(8,128)(2,1)S(1)}, u32[]{:S(2)}, u32[]{:S(2)}) %collective-permute-start.17) | collective-permute-done | bytes 131104 | tf_op jit(solution)/shard_map/ppermute | solution.py:135
  65.5 0.2 add_convert_fusion
  65.7 2.7 %collective-permute-start.18 = (bf16[2,256,256]{2,1,0:T(8,128)(2,1)S(1)}, bf16[2,256,256]{2,1,0:T(8,128)(2,1)S(1)}, u32[]{:S(2)}, u32[]{:S(2)}) collective-permute-start(bf16[2,256,256]{2,1,0:T(8,128)(2,1)S(1)} %add_convert_fusion), channel_id=1, source_target_pairs={{0,4},{1,5},{2,6},{3,7},{4,8},{5,9},{6,10},{7,11},{8,12},{9,13},{1... | collective-permute-start | bytes 786440 | tf_op jit(solution)/shard_map/ppermute | solution.py:138
  68.4 0.1 iota_compare_fusion.3
  68.4 2.0 %base.1 = f32[2,256,256]{2,1,0:T(8,128)} custom-call(s32[2]{0:T(128)} %size_ref.3, f32[2,256]{1,0:T(2,128)} %energy_ref.1, bf16[2,256,256]{2,1,0:T(8,128)(2,1)} %integral_ref.1, bf16[2,256,256]{2,1,0:T(8,128)(2,1)} %mask.1.masked_ref), custom_call_target="tpu_custom_call" | custom-call | tf_op jit(solution)/shard_map/base/pallas_call | solution.py:205
  70.5 10.7 %collective-permute-done.14 = bf16[2,256,256]{2,1,0:T(8,128)(2,1)S(1)} collective-permute-done((bf16[2,256,256]{2,1,0:T(8,128)(2,1)S(1)}, bf16[2,256,256]{2,1,0:T(8,128)(2,1)S(1)}, u32[]{:S(2)}, u32[]{:S(2)}) %collective-permute-start.14) | collective-permute-done | bytes 262176 | tf_op jit(solution)/shard_map/ppermute | solution.py:138
  81.2 0.0 collective-permute-done.18
  81.2 2.2 %add_select_fusion = f32[2,256,256]{2,1,0:T(8,128)} fusion(bf16[2,256,256]{2,1,0:T(8,128)(2,1)S(1)} %collective-permute-done.18, bf16[2,256,256]{2,1,0:T(8,128)(2,1)S(1)} %collective-permute-done.14, f32[2,256,256]{2,1,0:T(8,128)} %base.1, f32[256,256]{1,0:T(8,128)S(1)} %convert_element_type.50, f32[256,256]{1,0:T(8,128)S(1)} %convert_element_type.49, ...), kind=kLoop, calls=%fused_computation.9 | loop fusion | flops 1835008 | bytes 2621960 | tf_op jit(solution)/shard_map/jit(_where)/select_n | solution.py:216
  (15 shorter events, 0.3 us)
Async XLA Ops:
  1.7 40.6 %copy-start.1 = (bf16[2,256,256]{2,1,0:T(8,128)(2,1)S(1)}, bf16[2,256,256]{2,1,0:T(8,128)(2,1)}, u32[]{:S(2)}) copy-start(bf16[2,256,256]{2,1,0:T(8,128)(2,1)} %mask.1.masked_ref) | copy-start | bytes 786436
  1.7 13.3 %collective-permute-start.2 = (bf16[2,256,256]{2,1,0:T(8,128)(2,1)}, bf16[2,256,256]{2,1,0:T(8,128)(2,1)S(1)}, u32[]{:S(2)}, u32[]{:S(2)}) collective-permute-start(bf16[2,256,256]{2,1,0:T(8,128)(2,1)} %mask.1.masked_ref), channel_id=1, source_target_pairs={{0,12},{1,13},{2,14},{3,15},{4,0},{5,1},{6,2},{7,3},{8,4},{9,5},{1... | collective-permute-start | bytes 786440 | tf_op jit(solution)/shard_map/ppermute | solution.py:138
  6.8 22.5 %collective-permute-start.5 = (bf16[2,256,256]{2,1,0:T(8,128)(2,1)}, bf16[2,256,256]{2,1,0:T(8,128)(2,1)S(1)}, u32[]{:S(2)}, u32[]{:S(2)}) collective-permute-start(bf16[2,256,256]{2,1,0:T(8,128)(2,1)} %mask.1.masked_ref), channel_id=1, source_target_pairs={{0,8},{1,9},{2,10},{3,11},{4,12},{5,13},{6,14},{7,15},{8,0},{9,1},... | collective-permute-start | bytes 786440 | tf_op jit(solution)/shard_map/ppermute | solution.py:138
  6.8 24.0 %collective-permute-start.8 = (bf16[2,256,256]{2,1,0:T(8,128)(2,1)}, bf16[2,256,256]{2,1,0:T(8,128)(2,1)S(1)}, u32[]{:S(2)}, u32[]{:S(2)}) collective-permute-start(bf16[2,256,256]{2,1,0:T(8,128)(2,1)} %mask.1.masked_ref), channel_id=1, source_target_pairs={{0,4},{1,5},{2,6},{3,7},{4,8},{5,9},{6,10},{7,11},{8,12},{9,13},{1... | collective-permute-start | bytes 786440 | tf_op jit(solution)/shard_map/ppermute | solution.py:138
  7.8 7.8 %collective-permute-start = (bf16[2,256,256]{2,1,0:T(8,128)(2,1)}, bf16[2,256,256]{2,1,0:T(8,128)(2,1)S(1)}, u32[]{:S(2)}, u32[]{:S(2)}) collective-permute-start(bf16[2,256,256]{2,1,0:T(8,128)(2,1)} %mask.1.masked_ref), channel_id=1, source_target_pairs={{0,2},{1,3},{2,0},{3,1},{4,6},{5,7},{6,4},{7,5},{8,10},{9,11},{10,... | collective-permute-start | bytes 786440 | tf_op jit(solution)/shard_map/ppermute | solution.py:135
  15.0 16.4 %collective-permute-start.3 = (bf16[2,256,256]{2,1,0:T(8,128)(2,1)S(1)}, bf16[2,256,256]{2,1,0:T(8,128)(2,1)S(1)}, u32[]{:S(2)}, u32[]{:S(2)}) collective-permute-start(bf16[2,256,256]{2,1,0:T(8,128)(2,1)S(1)} %collective-permute-done.2), channel_id=1, source_target_pairs={{0,2},{1,3},{2,0},{3,1},{4,6},{5,7},{6,4},{7,5},{8,10},{9,11},{10,... | collective-permute-start | bytes 786440 | tf_op jit(solution)/shard_map/ppermute | solution.py:135
  16.6 25.6 %collective-permute-start.1 = (bf16[2,2,256,256]{3,2,1,0:T(8,128)(2,1)S(1)}, bf16[2,2,256,256]{3,2,1,0:T(8,128)(2,1)S(1)}, u32[]{:S(2)}, u32[]{:S(2)}) collective-permute-start(bf16[2,2,256,256]{3,2,1,0:T(8,128)(2,1)S(1)} %pad_maximum_fusion.1), channel_id=1, source_target_pairs={{0,1},{1,0},{2,3},{3,2},{4,5},{5,4},{6,7},{7,6},{8,9},{9,8},{10,11... | collective-permute-start | bytes 1572872 | tf_op jit(solution)/shard_map/ppermute | solution.py:135
  29.3 9.2 %collective-permute-start.6 = (bf16[2,256,256]{2,1,0:T(8,128)(2,1)S(1)}, bf16[2,256,256]{2,1,0:T(8,128)(2,1)S(1)}, u32[]{:S(2)}, u32[]{:S(2)}) collective-permute-start(bf16[2,256,256]{2,1,0:T(8,128)(2,1)S(1)} %collective-permute-done.5), channel_id=1, source_target_pairs={{0,2},{1,3},{2,0},{3,1},{4,6},{5,7},{6,4},{7,5},{8,10},{9,11},{10,... | collective-permute-start | bytes 786440 | tf_op jit(solution)/shard_map/ppermute | solution.py:135
  30.8 11.3 %collective-permute-start.9 = (bf16[2,256,256]{2,1,0:T(8,128)(2,1)S(1)}, bf16[2,256,256]{2,1,0:T(8,128)(2,1)S(1)}, u32[]{:S(2)}, u32[]{:S(2)}) collective-permute-start(bf16[2,256,256]{2,1,0:T(8,128)(2,1)S(1)} %collective-permute-done.8), channel_id=1, source_target_pairs={{0,2},{1,3},{2,0},{3,1},{4,6},{5,7},{6,4},{7,5},{8,10},{9,11},{10,... | collective-permute-start | bytes 786440 | tf_op jit(solution)/shard_map/ppermute | solution.py:135
  31.5 11.0 %collective-permute-start.4 = (bf16[2,2,256,256]{3,2,1,0:T(8,128)(2,1)S(1)}, bf16[2,2,256,256]{3,2,1,0:T(8,128)(2,1)S(1)}, u32[]{:S(2)}, u32[]{:S(2)}) collective-permute-start(bf16[2,2,256,256]{3,2,1,0:T(8,128)(2,1)S(1)} %pad_maximum_fusion.2), channel_id=1, source_target_pairs={{0,1},{1,0},{2,3},{3,2},{4,5},{5,4},{6,7},{7,6},{8,9},{9,8},{10,11... | collective-permute-start | bytes 1572872 | tf_op jit(solution)/shard_map/ppermute | solution.py:135
  38.6 4.0 %collective-permute-start.7 = (bf16[2,2,256,256]{3,2,1,0:T(8,128)(2,1)S(1)}, bf16[2,2,256,256]{3,2,1,0:T(8,128)(2,1)S(1)}, u32[]{:S(2)}, u32[]{:S(2)}) collective-permute-start(bf16[2,2,256,256]{3,2,1,0:T(8,128)(2,1)S(1)} %pad_maximum_fusion.3), channel_id=1, source_target_pairs={{0,1},{1,0},{2,3},{3,2},{4,5},{5,4},{6,7},{7,6},{8,9},{9,8},{10,11... | collective-permute-start | bytes 1572872 | tf_op jit(solution)/shard_map/ppermute | solution.py:135
  42.1 2.0 %collective-permute-start.10 = (bf16[2,2,256,256]{3,2,1,0:T(8,128)(2,1)S(1)}, bf16[2,2,256,256]{3,2,1,0:T(8,128)(2,1)S(1)}, u32[]{:S(2)}, u32[]{:S(2)}) collective-permute-start(bf16[2,2,256,256]{3,2,1,0:T(8,128)(2,1)S(1)} %pad_maximum_fusion.4), channel_id=1, source_target_pairs={{0,1},{1,0},{2,3},{3,2},{4,5},{5,4},{6,7},{7,6},{8,9},{9,8},{10,11... | collective-permute-start | bytes 1572872 | tf_op jit(solution)/shard_map/ppermute | solution.py:135
  44.3 0.7 copy-start
  51.4 17.0 %copy-start.2 = (s32[2]{0:T(128)S(1)}, s32[2]{0:T(128)}, u32[]{:S(2)}) copy-start(s32[2]{0:T(128)} %size_ref.3) | copy-start | bytes 28
  51.5 3.1 %collective-permute-start.11 = (bf16[256,256]{1,0:T(8,128)(2,1)S(1)}, bf16[256,256]{1,0:T(8,128)(2,1)S(1)}, u32[]{:S(2)}, u32[]{:S(2)}) collective-permute-start(bf16[256,256]{1,0:T(8,128)(2,1)S(1)} %get-tuple-element.16), channel_id=1, source_target_pairs={{0,1},{1,0},{2,3},{3,2},{4,5},{5,4},{6,7},{7,6},{8,9},{9,8},{10,11... | collective-permute-start | bytes 393224 | tf_op jit(solution)/shard_map/ppermute | solution.py:135
  51.6 6.4 %collective-permute-start.12 = (bf16[256,256]{1,0:T(8,128)(2,1)S(1)}, bf16[256,256]{1,0:T(8,128)(2,1)S(1)}, u32[]{:S(2)}, u32[]{:S(2)}) collective-permute-start(bf16[256,256]{1,0:T(8,128)(2,1)S(1)} %get-tuple-element.15), channel_id=1, source_target_pairs={{0,2},{1,3},{2,0},{3,1},{4,6},{5,7},{6,4},{7,5},{8,10},{9,11},{10,... | collective-permute-start | bytes 393224 | tf_op jit(solution)/shard_map/ppermute | solution.py:135
  52.4 7.5 %collective-permute-start.13 = (bf16[256,256]{1,0:T(8,128)(2,1)S(1)}, bf16[256,256]{1,0:T(8,128)(2,1)S(1)}, u32[]{:S(2)}, u32[]{:S(2)}) collective-permute-start(bf16[256,256]{1,0:T(8,128)(2,1)S(1)} %get-tuple-element.14), channel_id=1, source_target_pairs={{0,3},{1,2},{2,1},{3,0},{4,7},{5,6},{6,5},{7,4},{8,11},{9,10},{10,... | collective-permute-start | bytes 393224 | tf_op jit(solution)/shard_map/ppermute | solution.py:135
  53.5 7.9 %collective-permute-start.15 = (bf16[256,256]{1,0:T(8,128)(2,1)S(1)}, bf16[256,256]{1,0:T(8,128)(2,1)S(1)}, u32[]{:S(2)}, u32[]{:S(2)}) collective-permute-start(bf16[256,256]{1,0:T(8,128)(2,1)S(1)} %get-tuple-element.12), channel_id=1, source_target_pairs={{0,1},{1,0},{2,3},{3,2},{4,5},{5,4},{6,7},{7,6},{8,9},{9,8},{10,11... | collective-permute-start | bytes 393224 | tf_op jit(solution)/shard_map/ppermute | solution.py:135
  53.9 9.7 %collective-permute-start.16 = (bf16[256,256]{1,0:T(8,128)(2,1)S(1)}, bf16[256,256]{1,0:T(8,128)(2,1)S(1)}, u32[]{:S(2)}, u32[]{:S(2)}) collective-permute-start(bf16[256,256]{1,0:T(8,128)(2,1)S(1)} %get-tuple-element.11), channel_id=1, source_target_pairs={{0,2},{1,3},{2,0},{3,1},{4,6},{5,7},{6,4},{7,5},{8,10},{9,11},{10,... | collective-permute-start | bytes 393224 | tf_op jit(solution)/shard_map/ppermute | solution.py:135
  54.6 10.9 %collective-permute-start.17 = (bf16[256,256]{1,0:T(8,128)(2,1)S(1)}, bf16[256,256]{1,0:T(8,128)(2,1)S(1)}, u32[]{:S(2)}, u32[]{:S(2)}) collective-permute-start(bf16[256,256]{1,0:T(8,128)(2,1)S(1)} %get-tuple-element.10), channel_id=1, source_target_pairs={{0,3},{1,2},{2,1},{3,0},{4,7},{5,6},{6,5},{7,4},{8,11},{9,10},{10,... | collective-permute-start | bytes 393224 | tf_op jit(solution)/shard_map/ppermute | solution.py:135
  60.1 21.1 %collective-permute-start.14 = (bf16[2,256,256]{2,1,0:T(8,128)(2,1)S(1)}, bf16[2,256,256]{2,1,0:T(8,128)(2,1)S(1)}, u32[]{:S(2)}, u32[]{:S(2)}) collective-permute-start(bf16[2,256,256]{2,1,0:T(8,128)(2,1)S(1)} %add_convert_fusion.1), channel_id=1, source_target_pairs={{0,8},{1,9},{2,10},{3,11},{4,12},{5,13},{6,14},{7,15},{8,0},{9,1},... | collective-permute-start | bytes 786440 | tf_op jit(solution)/shard_map/ppermute | solution.py:138
  65.7 15.5 %collective-permute-start.18 = (bf16[2,256,256]{2,1,0:T(8,128)(2,1)S(1)}, bf16[2,256,256]{2,1,0:T(8,128)(2,1)S(1)}, u32[]{:S(2)}, u32[]{:S(2)}) collective-permute-start(bf16[2,256,256]{2,1,0:T(8,128)(2,1)S(1)} %add_convert_fusion), channel_id=1, source_target_pairs={{0,4},{1,5},{2,6},{3,7},{4,8},{5,9},{6,10},{7,11},{8,12},{9,13},{1... | collective-permute-start | bytes 786440 | tf_op jit(solution)/shard_map/ppermute | solution.py:138
where the time goes:
time: 84.3 us; the launch traced here: 83.4 us
  waiting for transfers between devices  43.5 us (52%)
  starting transfers between devices  18.3 us (22%)
  Pallas kernels  14.4 us (17%)
  other arithmetic  6.01 us (7%)
  local copies, waits for them, and re-layouts  0.95 us (1%)
    ppermute x5, waiting for transfers between devices, ahead(): lax.ppermute(value, 'col', [(i, (i + steps * GROUP) % columns) for i in r...  23.3 us
    ppermute x14, waiting for transfers between devices, swap(): return lax.ppermute(value, 'col', [(i, i ^ m) for i in range(columns)])  20.2 us
    ppermute x5, starting transfers between devices, ahead(): lax.ppermute(value, 'col', [(i, (i + steps * GROUP) % columns) for i in r...  10 us
    ppermute x14, starting transfers between devices, swap(): return lax.ppermute(value, 'col', [(i, i ^ m) for i in range(columns)])  8.26 us
    pallas_call x1, Pallas kernels, shards(): pl.pallas_call(tiles_kernel, out_shape=jax.ShapeDtypeStruct((columns // 2...  6.41 us
    pallas_call x1, Pallas kernels, shards(): pl.pallas_call(functools.partial(list_kernel, columns, pairs), out_shape=...  4.19 us
    select_n x1, other arithmetic, shards(): return jnp.where(held[:, :, None] & held[:, None, :], total, 0.0)  2.16 us
    pallas_call x1, Pallas kernels, shards(): pl.pallas_call(base_kernel, out_shape=jax.ShapeDtypeStruct(amplitudes.sha...  2.05 us
  transfers between devices with their start and end apart: 19, of which 9 were waited for; matrix products, arithmetic and copies ran while one was open for 5% of the time, Pallas kernels for 7%

commit v1 on v0

--- a/solution.py
+++ b/solution.py
@@ -46,62 +46,61 @@
     me = me_ref[0]
     z, g = me // GROUP, me % GROUP
 
-    def fill(i, _):
-        list_ref[0, i] = 0
-        list_ref[1, i] = 0
-        list_ref[2, i] = columns // 2
-        return 0
-
-    lax.fori_loop(0, tiles, fill, 0)
-
-    def visit(t, count):
+    def visit(t, counts):
         s, o = source_ref[t], owner_ref[t]
         pair = dispatch_ref[s, me]
         live = (pair >= 0) & (result_ref[me, o] >= 0)
+        row = (o // GROUP - z + depth) % half
+        later = (row > 0).astype(jnp.int32)
+        count = jnp.where(row > 0, counts[1], counts[0])
 
         @pl.when(live)
         def _():
-            far = (s // GROUP - z + depth) % depth
-            ahead = (o // GROUP - z + depth) % half
-            list_ref[0, count] = t
-            list_ref[1, count] = (far * GROUP + (g ^ (s % GROUP))) * pairs + jnp.maximum(pair, 0)
-            list_ref[2, count] = ahead * GROUP + (g ^ (o % GROUP))
-
-        return count + live.astype(jnp.int32)
-
-    count = lax.fori_loop(0, tiles, visit, jnp.int32(0))
-    list_ref[3, 0] = count
+            list_ref[later, 0, count] = t
+            list_ref[later, 1, count] = (me ^ s) * pairs + jnp.maximum(pair, 0)
+            list_ref[later, 2, count] = (row - later) * GROUP + (g ^ (o % GROUP))
+
+        one = live.astype(jnp.int32)
+        return counts[0] + one * (1 - later), counts[1] + one * later
+
+    counts = lax.fori_loop(0, tiles, visit, (jnp.int32(0), jnp.int32(0)))
+    for part in range(2):
+        count = counts[part]
+        spare = GROUP * (half - 1 if part else 1)
+
+        def fill(i, _):
+            list_ref[part, 0, i] = 0
+            list_ref[part, 1, i] = 0
+            list_ref[part, 2, i] = spare
+            return 0
+
+        lax.fori_loop(count, (count + UNROLL - 1) // UNROLL * UNROLL, fill, 0)
+        list_ref[part, 3, 0] = count
     for steps in range(half + 1):
         for m in range(GROUP):
             pair_ref[steps, m] = result_ref[z * GROUP + (g ^ m), (z + steps) % depth * GROUP + g]
 
 
-def tiles_kernel(list_ref, masked_ref, transfer_ref, block_ref, held, total, arrived):
-    count = list_ref[3, 0]
-    steps = (count + UNROLL - 1) // UNROLL
-
-    def copy(i):
-        return pltpu.make_async_copy(transfer_ref.at[list_ref[0, i]], held.at[i], arrived.at[i])
-
-    def fetch(i, _):
-        copy(i).start()
-        return 0
-
-    lax.fori_loop(0, steps * UNROLL, fetch, 0)
+def tiles_kernel(part, list_ref, masked_ref, transfer_ref, *refs):
+    block_ref, total = refs[-2:]
+    steps = (list_ref[part, 3, 0] + UNROLL - 1) // UNROLL
     total[...] = jnp.zeros_like(total)
 
     def step(n, _):
         places = [n * UNROLL + u for u in range(UNROLL)]
-        for i in places:
-            copy(i).wait()
+        tiles = [list_ref[part, 0, i] for i in places]
         halves = [
-            jnp.dot(held[i], masked_ref[list_ref[1, i]], preferred_element_type=jnp.float32)
-            for i in places
+            jnp.dot(
+                transfer_ref[t],
+                masked_ref[list_ref[part, 1, i]],
+                preferred_element_type=jnp.float32,
+            )
+            for i, t in zip(places, tiles)
         ]
-        for i, half in zip(places, halves):
-            total[list_ref[2, i]] += lax.dot_general(
+        for i, t, half in zip(places, tiles, halves):
+            total[list_ref[part, 2, i]] += lax.dot_general(
                 half.astype(jnp.bfloat16),
-                held[i],
+                transfer_ref[t],
                 (((1,), (1,)), ((), ())),
                 preferred_element_type=jnp.float32,
             )
@@ -147,18 +146,25 @@
         name="mask",
     )(pno_size, amplitudes)
 
-    lane = [masked] + [ahead(masked, -far) for far in range(1, depth)]
-    across = [swap(part, 2) for part in lane]
-    both = [jnp.stack([a, b]) for a, b in zip(lane, across)]
-    other = [swap(part, 1) for part in both]
-    everyone = jnp.stack(
-        [jnp.stack([a[0], b[0], a[1], b[1]]) for a, b in zip(both, other)]
-    ).reshape(columns * pairs, width, width)
+    lane, across = [masked] + [None] * (depth - 1), [None] * depth
+    for x in range(1, depth, 2):
+        lane[x] = swap(masked, x * GROUP)
+        across[x - 1 if x == 1 else x] = swap(lane[x - 1 if x == 1 else x], 2)
+    across[1] = swap(lane[1], 2)
+    for x in range(2, depth, 2):
+        lane[x] = swap(lane[x + 1], GROUP)
+        across[x] = jnp.concatenate(
+            [swap(lane[x][: pairs // 2], 2), swap(across[x + 1][pairs // 2 :], GROUP)]
+        )
+    everyone = []
+    for x in range(depth):
+        everyone += [lane[x], swap(lane[x], 1), across[x], swap(across[x], 1)]
+    everyone = jnp.concatenate(everyone)
 
     tile_list, fed = pl.pallas_call(
         functools.partial(list_kernel, columns, pairs),
         out_shape=[
-            jax.ShapeDtypeStruct((4, tiles), jnp.int32),
+            jax.ShapeDtypeStruct((2, 4, tiles + UNROLL), jnp.int32),
             jax.ShapeDtypeStruct((half + 1, GROUP), jnp.int32),
         ],
         in_specs=[SMEM()] * 5,
@@ -166,22 +172,26 @@
         name="tile_list",
     )(me[None], tile_source, tile_owner, dispatch_table, result_list)
 
-    blocks = pl.pallas_call(
-        tiles_kernel,
-        out_shape=jax.ShapeDtypeStruct((columns // 2, width, width), jnp.bfloat16),
-        in_specs=[SMEM(), VMEM(), HBM()],
-        out_specs=VMEM(),
-        scratch_shapes=[
-            pltpu.VMEM((tiles, width, width), jnp.bfloat16),
-            pltpu.VMEM((columns // 2 + 1, width, width), jnp.float32),
-            pltpu.SemaphoreType.DMA((tiles,)),
-        ],
-        compiler_params=pltpu.CompilerParams(vmem_limit_bytes=48 * 2**20),
-        cost_estimate=pl.CostEstimate(
-            flops=4 * tiles * width**3, bytes_accessed=2 * tiles * width**2, transcendentals=0
-        ),
-        name="tiles",
-    )(tile_list, everyone, subspace_transfers)
+    def sums_of(part, rows, *after):
+        return pl.pallas_call(
+            functools.partial(tiles_kernel, part),
+            out_shape=jax.ShapeDtypeStruct((rows * GROUP, width, width), jnp.bfloat16),
+            in_specs=[SMEM(), VMEM(), VMEM()] + [HBM()] * len(after),
+            out_specs=VMEM(),
+            scratch_shapes=[pltpu.VMEM((rows * GROUP + 1, width, width), jnp.float32)],
+            compiler_params=pltpu.CompilerParams(vmem_limit_bytes=16 * 2**20),
+            cost_estimate=pl.CostEstimate(
+                flops=2 * tiles * width**3, bytes_accessed=tiles * width**2, transcendentals=0
+            ),
+            name="tiles",
+        )(tile_list, everyone, subspace_transfers, *after)
+
+    def spread(block):
+        return [block[0]] + [swap(block[m], m) for m in range(1, GROUP)]
+
+    first = spread(sums_of(0, 1))
+    others = sums_of(1, half - 1, first[1])
+    rows = [first] + [spread(others[i * GROUP : (i + 1) * GROUP]) for i in range(half - 1)]
 
     near = (g ^ jnp.arange(GROUP, dtype=jnp.int32)) < g
     stays = jnp.where(near, fed[0], -1)
@@ -194,9 +204,7 @@
         return functools.reduce(jnp.add, terms)
 
     coupled = []
-    for row in range(half):
-        block = [blocks[row * GROUP + m] for m in range(GROUP)]
-        block = [block[0]] + [swap(block[m], m) for m in range(1, GROUP)]
+    for row, block in enumerate(rows):
         sums = by_pair(block, onward[row]).astype(jnp.bfloat16)
         if row == 0:
             coupled.append(by_pair(block, stays))

time: 84.3 us -> 75.2 us (0.89)
  waiting for transfers between devices: 43.5 us -> 30.8 us
  starting transfers between devices: 18.3 us -> 23 us
  other arithmetic: 6.01 us -> 3.77 us
  local copies, waits for them, and re-layouts: 0.95 us -> 1.99 us
    ppermute x5 -> x2, waiting for transfers between devices: 23.3 us -> 10.1 us  [ahead(): lax.ppermute(value, 'col', [(i, (i + steps * GROUP) % columns) for i in r...]
    ppermute x14 -> x22, starting transfers between devices: 8.26 us -> 16.4 us  [swap(): return lax.ppermute(value, 'col', [(i, i ^ m) for i in range(columns)])]
    ppermute x5 -> x2, starting transfers between devices: 10 us -> 6.65 us  [ahead(): lax.ppermute(value, 'col', [(i, (i + steps * GROUP) % columns) for i in r...]
    another operation x9 -> x0, other arithmetic: 2.26 us -> none  [the longest x4 1.15 us: shards(): both = [jnp.stack([a, b]) for a, b in zip(lane, across)]]
    unnamed x6 -> x22, local copies, waits for them, and re-layouts: 0.1 us -> 1.25 us
    pallas_call x1 -> x2, Pallas kernels: 6.41 us -> 7.01 us  [sums_of(): pl.pallas_call(functools.partial(tiles_kernel, part), out_shape=jax.Shape...]
    ppermute x14 -> x22, waiting for transfers between devices: 20.2 us -> 20.8 us  [swap(): return lax.ppermute(value, 'col', [(i, i ^ m) for i in range(columns)])]
  transfers between devices with their start and end apart: 19 -> 24, of which waited for: 9 -> 10; matrix products, arithmetic and copies ran while one was open for 5% -> 5% of each run, Pallas kernels for 7% -> 13%
where the time goes in v1:
time: 75.2 us; the launch traced here: 74.4 us
  waiting for transfers between devices  30.8 us (41%)
  starting transfers between devices  23 us (31%)
  Pallas kernels  14.4 us (19%)
  other arithmetic  3.77 us (5%)
  local copies, waits for them, and re-layouts  1.99 us (3%)
    ppermute x22, waiting for transfers between devices, swap(): return lax.ppermute(value, 'col', [(i, i ^ m) for i in range(columns)])  20.8 us
    ppermute x22, starting transfers between devices, swap(): return lax.ppermute(value, 'col', [(i, i ^ m) for i in range(columns)])  16.4 us
    ppermute x2, waiting for transfers between devices, ahead(): lax.ppermute(value, 'col', [(i, (i + steps * GROUP) % columns) for i in r...  10.1 us
    pallas_call x2, Pallas kernels, sums_of(): pl.pallas_call(functools.partial(tiles_kernel, part), out_shape=jax.Shape...  7.01 us
    ppermute x2, starting transfers between devices, ahead(): lax.ppermute(value, 'col', [(i, (i + steps * GROUP) % columns) for i in r...  6.65 us
    pallas_call x1, Pallas kernels, shards(): pl.pallas_call(functools.partial(list_kernel, columns, pairs), out_shape=...  3.65 us
    select_n x1, other arithmetic, shards(): return jnp.where(held[:, :, None] & held[:, None, :], total, 0.0)  2.16 us
    pallas_call x1, Pallas kernels, shards(): pl.pallas_call(base_kernel, out_shape=jax.ShapeDtypeStruct(amplitudes.sha...  2.05 us
  transfers between devices with their start and end apart: 24, of which 10 were waited for; matrix products, arithmetic and copies ran while one was open for 5% of the time, Pallas kernels for 13%

profile of v1, /device:TPU:0, one launch (start us, length us, event | category | flops | bytes accessed | tf_op | source)
XLA Modules:
  0.0 74.4 jit_solution(783244606272129277)
XLA Ops:
  0.0 1.7 %mask.1.masked_ref = bf16[2,256,256]{2,1,0:T(8,128)(2,1)} custom-call(s32[2]{0:T(128)} %size_ref.3, bf16[2,256,256]{2,1,0:T(8,128)(2,1)} %amplitude_ref.1), custom_call_target="tpu_custom_call" | custom-call | tf_op jit(solution)/shard_map/mask/pallas_call | solution.py:141
  1.7 0.5 collective-permute-start
  2.2 2.5 %collective-permute-start.1 = (bf16[2,256,256]{2,1,0:T(8,128)(2,1)}, bf16[2,256,256]{2,1,0:T(8,128)(2,1)S(1)}, u32[]{:S(2)}, u32[]{:S(2)}) collective-permute-start(bf16[2,256,256]{2,1,0:T(8,128)(2,1)} %mask.1.masked_ref), channel_id=1, source_target_pairs={{0,2},{1,3},{2,0},{3,1},{4,6},{5,7},{6,4},{7,5},{8,10},{9,11},{10,... | collective-permute-start | bytes 786440 | tf_op jit(solution)/shard_map/ppermute | solution.py:134
  4.7 1.6 %collective-permute-start.3 = (bf16[2,256,256]{2,1,0:T(8,128)(2,1)}, bf16[2,256,256]{2,1,0:T(8,128)(2,1)S(1)}, u32[]{:S(2)}, u32[]{:S(2)}) collective-permute-start(bf16[2,256,256]{2,1,0:T(8,128)(2,1)} %mask.1.masked_ref), channel_id=1, source_target_pairs={{0,4},{1,5},{2,6},{3,7},{4,0},{5,1},{6,2},{7,3},{8,12},{9,13},{10,... | collective-permute-start | bytes 786440 | tf_op jit(solution)/shard_map/ppermute | solution.py:134
  6.3 2.5 %collective-permute-start.7 = (bf16[2,256,256]{2,1,0:T(8,128)(2,1)}, bf16[2,256,256]{2,1,0:T(8,128)(2,1)S(1)}, u32[]{:S(2)}, u32[]{:S(2)}) collective-permute-start(bf16[2,256,256]{2,1,0:T(8,128)(2,1)} %mask.1.masked_ref), channel_id=1, source_target_pairs={{0,12},{1,13},{2,14},{3,15},{4,8},{5,9},{6,10},{7,11},{8,4},{9,5},... | collective-permute-start | bytes 786440 | tf_op jit(solution)/shard_map/ppermute | solution.py:134
  8.7 3.6 %tile_list.1 = (s32[2,4,72]{2,1,0:T(4,128)}, s32[3,4]{1,0:T(4,128)}) custom-call(s32[1]{0:T(128)} %bitcast.me_ref, s32[64]{0:T(128)} %source_ref.1, s32[64]{0:T(128)} %owner_ref.1, s32[16,16]{1,0:T(8,128)} %dispatch_ref.1, s32[16,16]{1,0:T(8,128)} %result_ref.1), custom_call_target="tpu_custom_call" | custom-call | tf_op jit(solution)/shard_map/tile_list/pallas_call | solution.py:164
  12.4 0.7 slice_bitcast_fusion.20
  13.1 0.7 %compare_select_fusion.1 = (s32[4]{0:T(128)S(1)}, s32[4]{0:T(128)S(1)}) fusion(s32[3,4]{1,0:T(4,128)} %get-tuple-element.7, s32[]{:T(128)S(6)} %select_n.64), kind=kLoop, calls=%fused_computation.48 | loop fusion | flops 16 | bytes 68 | tf_op jit(solution)/shard_map/jit(_where)/select_n | solution.py:197
  13.8 0.1 iota_compare_fusion.1
  13.9 0.1 iota_compare_fusion
  14.0 7.1 %collective-permute-done.7 = bf16[2,256,256]{2,1,0:T(8,128)(2,1)S(1)} collective-permute-done((bf16[2,256,256]{2,1,0:T(8,128)(2,1)}, bf16[2,256,256]{2,1,0:T(8,128)(2,1)S(1)}, u32[]{:S(2)}, u32[]{:S(2)}) %collective-permute-start.7) | collective-permute-done | bytes 262176 | tf_op jit(solution)/shard_map/ppermute | solution.py:134
  21.1 0.6 collective-permute-start.8
  21.7 0.5 collective-permute-start.11
  22.2 0.0 collective-permute-done.1
  22.2 0.0 collective-permute-start.2
  22.2 1.0 %constant_dynamic-update-slice_fusion.16 = bf16[32,256,256]{2,1,0:T(8,128)(2,1)S(1)} fusion(bf16[2,256,256]{2,1,0:T(8,128)(2,1)} %mask.1.masked_ref), kind=kLoop, calls=%fused_computation.30 | loop fusion | bytes 524288
  23.2 0.0 collective-permute-done.3
  23.2 0.6 collective-permute-start.4
  23.8 0.0 collective-permute-done
  23.8 1.5 %collective-permute-start.5 = (bf16[2,256,256]{2,1,0:T(8,128)(2,1)S(1)}, bf16[2,256,256]{2,1,0:T(8,128)(2,1)S(1)}, u32[]{:S(2)}, u32[]{:S(2)}) collective-permute-start(bf16[2,256,256]{2,1,0:T(8,128)(2,1)S(1)} %collective-permute-done.3), channel_id=1, source_target_pairs={{0,2},{1,3},{2,0},{3,1},{4,6},{5,7},{6,4},{7,5},{8,10},{9,11},{10,... | collective-permute-start | bytes 786440 | tf_op jit(solution)/shard_map/ppermute | solution.py:134
  25.3 0.0 copy-start
  25.4 3.3 %collective-permute-done.8 = bf16[2,256,256]{2,1,0:T(8,128)(2,1)S(1)} collective-permute-done((bf16[2,256,256]{2,1,0:T(8,128)(2,1)S(1)}, bf16[2,256,256]{2,1,0:T(8,128)(2,1)S(1)}, u32[]{:S(2)}, u32[]{:S(2)}) %collective-permute-start.8) | collective-permute-done | bytes 262176 | tf_op jit(solution)/shard_map/ppermute | solution.py:134
  28.7 0.0 collective-permute-start.14
  28.7 2.2 %collective-permute-done.11 = bf16[2,256,256]{2,1,0:T(8,128)(2,1)S(1)} collective-permute-done((bf16[2,256,256]{2,1,0:T(8,128)(2,1)S(1)}, bf16[2,256,256]{2,1,0:T(8,128)(2,1)S(1)}, u32[]{:S(2)}, u32[]{:S(2)}) %collective-permute-start.11) | collective-permute-done | bytes 262176 | tf_op jit(solution)/shard_map/ppermute | solution.py:134
  30.8 0.0 collective-permute-start.10
  30.9 0.0 collective-permute-done.2
  30.9 1.6 %collective-permute-start.12 = (bf16[1,256,256]{2,1,0:T(8,128)(2,1)S(1)}, bf16[1,256,256]{2,1,0:T(8,128)(2,1)S(1)}, u32[]{:S(2)}, u32[]{:S(2)}) collective-permute-start(bf16[1,256,256]{2,1,0:T(8,128)(2,1)S(1)} %slice.113), channel_id=1, source_target_pairs={{0,4},{1,5},{2,6},{3,7},{4,0},{5,1},{6,2},{7,3},{8,12},{9,13},{10,... | collective-permute-start | bytes 393224 | tf_op jit(solution)/shard_map/ppermute | solution.py:134
  32.5 0.0 collective-permute-done.4
  32.5 0.1 collective-permute-start.9
  32.6 3.1 %collective-permute-done.5 = bf16[2,256,256]{2,1,0:T(8,128)(2,1)S(1)} collective-permute-done((bf16[2,256,256]{2,1,0:T(8,128)(2,1)S(1)}, bf16[2,256,256]{2,1,0:T(8,128)(2,1)S(1)}, u32[]{:S(2)}, u32[]{:S(2)}) %collective-permute-start.5) | collective-permute-done | bytes 262176 | tf_op jit(solution)/shard_map/ppermute | solution.py:134
  35.7 0.0 collective-permute-start.6
  35.7 1.4 %collective-permute-done.10 = bf16[1,256,256]{2,1,0:T(8,128)(2,1)S(1)} collective-permute-done((bf16[1,256,256]{2,1,0:T(8,128)(2,1)S(1)}, bf16[1,256,256]{2,1,0:T(8,128)(2,1)S(1)}, u32[]{:S(2)}, u32[]{:S(2)}) %collective-permute-start.10) | collective-permute-done | bytes 131104 | tf_op jit(solution)/shard_map/ppermute | solution.py:134
  37.1 0.0 collective-permute-start.15
  37.1 0.0 collective-permute-done.12
  37.1 0.6 collective-permute-start.13
  37.7 0.0 collective-permute-done.6
  37.7 0.0 collective-permute-done.9
  37.8 1.2 %collective-permute-done.13 = bf16[2,256,256]{2,1,0:T(8,128)(2,1)S(1)} collective-permute-done((bf16[2,256,256]{2,1,0:T(8,128)(2,1)S(1)}, bf16[2,256,256]{2,1,0:T(8,128)(2,1)S(1)}, u32[]{:S(2)}, u32[]{:S(2)}) %collective-permute-start.13) | collective-permute-done | bytes 262176 | tf_op jit(solution)/shard_map/ppermute | solution.py:134
  39.0 0.0 collective-permute-done.14
  39.1 0.0 collective-permute-done.15
  39.2 3.1 %tiles.2 = bf16[4,256,256]{2,1,0:T(8,128)(2,1)S(1)} custom-call(s32[2,4,72]{2,1,0:T(4,128)S(1)} %copy-done.1, bf16[32,256,256]{2,1,0:T(8,128)(2,1)S(1)} %constant_dynamic-update-slice_fusion.masked_ref, bf16[64,256,256]{2,1,0:T(8,128)(2,1)S(1)} %copy-done), custom_call_target="tpu_custom_call" | custom-call | flops 2147483648 | bytes 4194304 | tf_op jit(solution)/shard_map/tiles/pallas_call | solution.py:176
  42.3 0.3 collective-permute-start.16
  42.7 0.6 collective-permute-start.17
  43.2 1.1 %collective-permute-start.18 = (bf16[256,256]{1,0:T(8,128)(2,1)S(1)}, bf16[256,256]{1,0:T(8,128)(2,1)S(1)}, u32[]{:S(2)}, u32[]{:S(2)}) collective-permute-start(bf16[256,256]{1,0:T(8,128)(2,1)S(1)} %get-tuple-element.10), channel_id=1, source_target_pairs={{0,3},{1,2},{2,1},{3,0},{4,7},{5,6},{6,5},{7,4},{8,11},{9,10},{10,... | collective-permute-start | bytes 393224 | tf_op jit(solution)/shard_map/ppermute | solution.py:134
  44.4 0.0 collective-permute-done.16.refs_0_
  44.4 3.9 %tiles.3 = bf16[4,256,256]{2,1,0:T(8,128)(2,1)S(1)} custom-call(s32[2,4,72]{2,1,0:T(4,128)S(1)} %copy-done.1, bf16[32,256,256]{2,1,0:T(8,128)(2,1)S(1)} %constant_dynamic-update-slice_fusion.masked_ref, bf16[64,256,256]{2,1,0:T(8,128)(2,1)S(1)} %copy-done, bf16[256,256]{1,0:T(8,128)(2,1)S(1)} %collective-permute-done.16.refs_0_), custom_call_target="tpu_custom_call" | custom-call | flops 2147483648 | bytes 4194304 | tf_op jit(solution)/shard_map/tiles/pallas_call | solution.py:176
  48.3 0.0 copy-start.2
  48.3 0.1 collective-permute-start.20
  48.4 0.1 collective-permute-start.21
  48.5 1.8 %collective-permute-start.22 = (bf16[256,256]{1,0:T(8,128)(2,1)S(1)}, bf16[256,256]{1,0:T(8,128)(2,1)S(1)}, u32[]{:S(2)}, u32[]{:S(2)}) collective-permute-start(bf16[256,256]{1,0:T(8,128)(2,1)S(1)} %get-tuple-element.14), channel_id=1, source_target_pairs={{0,3},{1,2},{2,1},{3,0},{4,7},{5,6},{6,5},{7,4},{8,11},{9,10},{10,... | collective-permute-start | bytes 393224 | tf_op jit(solution)/shard_map/ppermute | solution.py:134
  50.3 0.0 collective-permute-done.17
  50.3 0.2 collective-permute-done.18
  50.6 0.2 add_convert_fusion.1
  50.8 3.5 %collective-permute-start.19 = (bf16[2,256,256]{2,1,0:T(8,128)(2,1)S(1)}, bf16[2,256,256]{2,1,0:T(8,128)(2,1)S(1)}, u32[]{:S(2)}, u32[]{:S(2)}) collective-permute-start(bf16[2,256,256]{2,1,0:T(8,128)(2,1)S(1)} %add_convert_fusion.1), channel_id=1, source_target_pairs={{0,8},{1,9},{2,10},{3,11},{4,12},{5,13},{6,14},{7,15},{8,0},{9,1},... | collective-permute-start | bytes 786440 | tf_op jit(solution)/shard_map/ppermute | solution.py:137
  54.3 0.0 collective-permute-done.20
  54.3 0.4 collective-permute-done.21
  54.8 1.9 %collective-permute-done.22 = bf16[256,256]{1,0:T(8,128)(2,1)S(1)} collective-permute-done((bf16[256,256]{1,0:T(8,128)(2,1)S(1)}, bf16[256,256]{1,0:T(8,128)(2,1)S(1)}, u32[]{:S(2)}, u32[]{:S(2)}) %collective-permute-start.22) | collective-permute-done | bytes 131104 | tf_op jit(solution)/shard_map/ppermute | solution.py:134
  56.7 0.2 add_convert_fusion
  56.9 3.1 %collective-permute-start.23 = (bf16[2,256,256]{2,1,0:T(8,128)(2,1)S(1)}, bf16[2,256,256]{2,1,0:T(8,128)(2,1)S(1)}, u32[]{:S(2)}, u32[]{:S(2)}) collective-permute-start(bf16[2,256,256]{2,1,0:T(8,128)(2,1)S(1)} %add_convert_fusion), channel_id=1, source_target_pairs={{0,4},{1,5},{2,6},{3,7},{4,8},{5,9},{6,10},{7,11},{8,12},{9,13},{1... | collective-permute-start | bytes 786440 | tf_op jit(solution)/shard_map/ppermute | solution.py:137
  60.0 0.1 iota_compare_fusion.3
  60.1 2.0 %base.1 = f32[2,256,256]{2,1,0:T(8,128)} custom-call(s32[2]{0:T(128)} %size_ref.3, f32[2,256]{1,0:T(2,128)} %energy_ref.1, bf16[2,256,256]{2,1,0:T(8,128)(2,1)} %integral_ref.1, bf16[2,256,256]{2,1,0:T(8,128)(2,1)} %mask.1.masked_ref), custom_call_target="tpu_custom_call" | custom-call | tf_op jit(solution)/shard_map/base/pallas_call | solution.py:213
  62.2 10.1 %collective-permute-done.19 = bf16[2,256,256]{2,1,0:T(8,128)(2,1)S(1)} collective-permute-done((bf16[2,256,256]{2,1,0:T(8,128)(2,1)S(1)}, bf16[2,256,256]{2,1,0:T(8,128)(2,1)S(1)}, u32[]{:S(2)}, u32[]{:S(2)}) %collective-permute-start.19) | collective-permute-done | bytes 262176 | tf_op jit(solution)/shard_map/ppermute | solution.py:137
  72.2 0.0 collective-permute-done.23
  72.2 2.2 %add_select_fusion = f32[2,256,256]{2,1,0:T(8,128)} fusion(bf16[2,256,256]{2,1,0:T(8,128)(2,1)S(1)} %collective-permute-done.23, bf16[2,256,256]{2,1,0:T(8,128)(2,1)S(1)} %collective-permute-done.19, f32[2,256,256]{2,1,0:T(8,128)} %base.1, f32[256,256]{1,0:T(8,128)S(1)} %convert_element_type.50, f32[256,256]{1,0:T(8,128)S(1)} %convert_element_type.49, ...), kind=kLoop, calls=%fused_computation | loop fusion | flops 1835008 | bytes 2621960 | tf_op jit(solution)/shard_map/jit(_where)/select_n | solution.py:224
  (34 shorter events, 0.6 us)
Async XLA Ops:
  1.7 22.0 %collective-permute-start = (bf16[2,256,256]{2,1,0:T(8,128)(2,1)}, bf16[2,256,256]{2,1,0:T(8,128)(2,1)S(1)}, u32[]{:S(2)}, u32[]{:S(2)}) collective-permute-start(bf16[2,256,256]{2,1,0:T(8,128)(2,1)} %mask.1.masked_ref), channel_id=1, source_target_pairs={{0,1},{1,0},{2,3},{3,2},{4,5},{5,4},{6,7},{7,6},{8,9},{9,8},{10,11... | collective-permute-start | bytes 786440 | tf_op jit(solution)/shard_map/ppermute | solution.py:134
  2.2 20.0 %collective-permute-start.1 = (bf16[2,256,256]{2,1,0:T(8,128)(2,1)}, bf16[2,256,256]{2,1,0:T(8,128)(2,1)S(1)}, u32[]{:S(2)}, u32[]{:S(2)}) collective-permute-start(bf16[2,256,256]{2,1,0:T(8,128)(2,1)} %mask.1.masked_ref), channel_id=1, source_target_pairs={{0,2},{1,3},{2,0},{3,1},{4,6},{5,7},{6,4},{7,5},{8,10},{9,11},{10,... | collective-permute-start | bytes 786440 | tf_op jit(solution)/shard_map/ppermute | solution.py:134
  4.7 18.5 %collective-permute-start.3 = (bf16[2,256,256]{2,1,0:T(8,128)(2,1)}, bf16[2,256,256]{2,1,0:T(8,128)(2,1)S(1)}, u32[]{:S(2)}, u32[]{:S(2)}) collective-permute-start(bf16[2,256,256]{2,1,0:T(8,128)(2,1)} %mask.1.masked_ref), channel_id=1, source_target_pairs={{0,4},{1,5},{2,6},{3,7},{4,0},{5,1},{6,2},{7,3},{8,12},{9,13},{10,... | collective-permute-start | bytes 786440 | tf_op jit(solution)/shard_map/ppermute | solution.py:134
  6.3 14.8 %collective-permute-start.7 = (bf16[2,256,256]{2,1,0:T(8,128)(2,1)}, bf16[2,256,256]{2,1,0:T(8,128)(2,1)S(1)}, u32[]{:S(2)}, u32[]{:S(2)}) collective-permute-start(bf16[2,256,256]{2,1,0:T(8,128)(2,1)} %mask.1.masked_ref), channel_id=1, source_target_pairs={{0,12},{1,13},{2,14},{3,15},{4,8},{5,9},{6,10},{7,11},{8,4},{9,5},... | collective-permute-start | bytes 786440 | tf_op jit(solution)/shard_map/ppermute | solution.py:134
  21.1 7.6 %collective-permute-start.8 = (bf16[2,256,256]{2,1,0:T(8,128)(2,1)S(1)}, bf16[2,256,256]{2,1,0:T(8,128)(2,1)S(1)}, u32[]{:S(2)}, u32[]{:S(2)}) collective-permute-start(bf16[2,256,256]{2,1,0:T(8,128)(2,1)S(1)} %collective-permute-done.7), channel_id=1, source_target_pairs={{0,4},{1,5},{2,6},{3,7},{4,0},{5,1},{6,2},{7,3},{8,12},{9,13},{10,... | collective-permute-start | bytes 786440 | tf_op jit(solution)/shard_map/ppermute | solution.py:134
  21.7 9.1 %collective-permute-start.11 = (bf16[2,256,256]{2,1,0:T(8,128)(2,1)S(1)}, bf16[2,256,256]{2,1,0:T(8,128)(2,1)S(1)}, u32[]{:S(2)}, u32[]{:S(2)}) collective-permute-start(bf16[2,256,256]{2,1,0:T(8,128)(2,1)S(1)} %collective-permute-done.7), channel_id=1, source_target_pairs={{0,2},{1,3},{2,0},{3,1},{4,6},{5,7},{6,4},{7,5},{8,10},{9,11},{10,... | collective-permute-start | bytes 786440 | tf_op jit(solution)/shard_map/ppermute | solution.py:134
  22.2 8.6 %collective-permute-start.2 = (bf16[2,256,256]{2,1,0:T(8,128)(2,1)S(1)}, bf16[2,256,256]{2,1,0:T(8,128)(2,1)S(1)}, u32[]{:S(2)}, u32[]{:S(2)}) collective-permute-start(bf16[2,256,256]{2,1,0:T(8,128)(2,1)S(1)} %collective-permute-done.1), channel_id=1, source_target_pairs={{0,1},{1,0},{2,3},{3,2},{4,5},{5,4},{6,7},{7,6},{8,9},{9,8},{10,11... | collective-permute-start | bytes 786440 | tf_op jit(solution)/shard_map/ppermute | solution.py:134
  23.2 9.3 %collective-permute-start.4 = (bf16[2,256,256]{2,1,0:T(8,128)(2,1)S(1)}, bf16[2,256,256]{2,1,0:T(8,128)(2,1)S(1)}, u32[]{:S(2)}, u32[]{:S(2)}) collective-permute-start(bf16[2,256,256]{2,1,0:T(8,128)(2,1)S(1)} %collective-permute-done.3), channel_id=1, source_target_pairs={{0,1},{1,0},{2,3},{3,2},{4,5},{5,4},{6,7},{7,6},{8,9},{9,8},{10,11... | collective-permute-start | bytes 786440 | tf_op jit(solution)/shard_map/ppermute | solution.py:134
  23.8 11.9 %collective-permute-start.5 = (bf16[2,256,256]{2,1,0:T(8,128)(2,1)S(1)}, bf16[2,256,256]{2,1,0:T(8,128)(2,1)S(1)}, u32[]{:S(2)}, u32[]{:S(2)}) collective-permute-start(bf16[2,256,256]{2,1,0:T(8,128)(2,1)S(1)} %collective-permute-done.3), channel_id=1, source_target_pairs={{0,2},{1,3},{2,0},{3,1},{4,6},{5,7},{6,4},{7,5},{8,10},{9,11},{10,... | collective-permute-start | bytes 786440 | tf_op jit(solution)/shard_map/ppermute | solution.py:134
  25.3 13.9 %copy-start.1 = (s32[2,4,72]{2,1,0:T(4,128)S(1)}, s32[2,4,72]{2,1,0:T(4,128)}, u32[]{:S(2)}) copy-start(s32[2,4,72]{2,1,0:T(4,128)} %get-tuple-element.8.list_ref) | copy-start | bytes 6916
  25.3 13.8 %copy-start = (bf16[64,256,256]{2,1,0:T(8,128)(2,1)S(1)}, bf16[64,256,256]{2,1,0:T(8,128)(2,1)}, u32[]{:S(2)}) copy-start(bf16[64,256,256]{2,1,0:T(8,128)(2,1)} %transfer_ref.3) | copy-start | bytes 25165828
  28.7 10.4 %collective-permute-start.14 = (bf16[2,256,256]{2,1,0:T(8,128)(2,1)S(1)}, bf16[2,256,256]{2,1,0:T(8,128)(2,1)S(1)}, u32[]{:S(2)}, u32[]{:S(2)}) collective-permute-start(bf16[2,256,256]{2,1,0:T(8,128)(2,1)S(1)} %collective-permute-done.7), channel_id=1, source_target_pairs={{0,1},{1,0},{2,3},{3,2},{4,5},{5,4},{6,7},{7,6},{8,9},{9,8},{10,11... | collective-permute-start | bytes 786440 | tf_op jit(solution)/shard_map/ppermute | solution.py:134
  30.8 6.2 %collective-permute-start.10 = (bf16[1,256,256]{2,1,0:T(8,128)(2,1)S(1)}, bf16[1,256,256]{2,1,0:T(8,128)(2,1)S(1)}, u32[]{:S(2)}, u32[]{:S(2)}) collective-permute-start(bf16[1,256,256]{2,1,0:T(8,128)(2,1)S(1)} %slice.112), channel_id=1, source_target_pairs={{0,2},{1,3},{2,0},{3,1},{4,6},{5,7},{6,4},{7,5},{8,10},{9,11},{10,... | collective-permute-start | bytes 393224 | tf_op jit(solution)/shard_map/ppermute | solution.py:134
  30.9 6.2 %collective-permute-start.12 = (bf16[1,256,256]{2,1,0:T(8,128)(2,1)S(1)}, bf16[1,256,256]{2,1,0:T(8,128)(2,1)S(1)}, u32[]{:S(2)}, u32[]{:S(2)}) collective-permute-start(bf16[1,256,256]{2,1,0:T(8,128)(2,1)S(1)} %slice.113), channel_id=1, source_target_pairs={{0,4},{1,5},{2,6},{3,7},{4,0},{5,1},{6,2},{7,3},{8,12},{9,13},{10,... | collective-permute-start | bytes 393224 | tf_op jit(solution)/shard_map/ppermute | solution.py:134
  32.5 5.2 %collective-permute-start.9 = (bf16[2,256,256]{2,1,0:T(8,128)(2,1)S(1)}, bf16[2,256,256]{2,1,0:T(8,128)(2,1)S(1)}, u32[]{:S(2)}, u32[]{:S(2)}) collective-permute-start(bf16[2,256,256]{2,1,0:T(8,128)(2,1)S(1)} %collective-permute-done.8), channel_id=1, source_target_pairs={{0,1},{1,0},{2,3},{3,2},{4,5},{5,4},{6,7},{7,6},{8,9},{9,8},{10,11... | collective-permute-start | bytes 786440 | tf_op jit(solution)/shard_map/ppermute | solution.py:134
  35.7 2.0 %collective-permute-start.6 = (bf16[2,256,256]{2,1,0:T(8,128)(2,1)S(1)}, bf16[2,256,256]{2,1,0:T(8,128)(2,1)S(1)}, u32[]{:S(2)}, u32[]{:S(2)}) collective-permute-start(bf16[2,256,256]{2,1,0:T(8,128)(2,1)S(1)} %collective-permute-done.5), channel_id=1, source_target_pairs={{0,1},{1,0},{2,3},{3,2},{4,5},{5,4},{6,7},{7,6},{8,9},{9,8},{10,11... | collective-permute-start | bytes 786440 | tf_op jit(solution)/shard_map/ppermute | solution.py:134
  37.1 2.0 %collective-permute-start.15 = (bf16[2,256,256]{2,1,0:T(8,128)(2,1)S(1)}, bf16[2,256,256]{2,1,0:T(8,128)(2,1)S(1)}, u32[]{:S(2)}, u32[]{:S(2)}) collective-permute-start(bf16[2,256,256]{2,1,0:T(8,128)(2,1)S(1)} %collective-permute-done.11), channel_id=1, source_target_pairs={{0,1},{1,0},{2,3},{3,2},{4,5},{5,4},{6,7},{7,6},{8,9},{9,8},{10,11... | collective-permute-start | bytes 786440 | tf_op jit(solution)/shard_map/ppermute | solution.py:134
  37.1 1.9 %collective-permute-start.13 = (bf16[2,256,256]{2,1,0:T(8,128)(2,1)S(1)}, bf16[2,256,256]{2,1,0:T(8,128)(2,1)S(1)}, u32[]{:S(2)}, u32[]{:S(2)}) collective-permute-start(bf16[2,256,256]{2,1,0:T(8,128)(2,1)S(1)} %pad_maximum_fusion), channel_id=1, source_target_pairs={{0,1},{1,0},{2,3},{3,2},{4,5},{5,4},{6,7},{7,6},{8,9},{9,8},{10,11... | collective-permute-start | bytes 786440 | tf_op jit(solution)/shard_map/ppermute | solution.py:134
  42.3 2.0 %collective-permute-start.16 = (bf16[256,256]{1,0:T(8,128)(2,1)S(1)}, bf16[256,256]{1,0:T(8,128)(2,1)S(1)}, u32[]{:S(2)}, u32[]{:S(2)}) collective-permute-start(bf16[256,256]{1,0:T(8,128)(2,1)S(1)} %get-tuple-element.12), channel_id=1, source_target_pairs={{0,1},{1,0},{2,3},{3,2},{4,5},{5,4},{6,7},{7,6},{8,9},{9,8},{10,11... | collective-permute-start | bytes 393224 | tf_op jit(solution)/shard_map/ppermute | solution.py:134
  42.7 7.6 %collective-permute-start.17 = (bf16[256,256]{1,0:T(8,128)(2,1)S(1)}, bf16[256,256]{1,0:T(8,128)(2,1)S(1)}, u32[]{:S(2)}, u32[]{:S(2)}) collective-permute-start(bf16[256,256]{1,0:T(8,128)(2,1)S(1)} %get-tuple-element.11), channel_id=1, source_target_pairs={{0,2},{1,3},{2,0},{3,1},{4,6},{5,7},{6,4},{7,5},{8,10},{9,11},{10,... | collective-permute-start | bytes 393224 | tf_op jit(solution)/shard_map/ppermute | solution.py:134
  43.2 7.3 %collective-permute-start.18 = (bf16[256,256]{1,0:T(8,128)(2,1)S(1)}, bf16[256,256]{1,0:T(8,128)(2,1)S(1)}, u32[]{:S(2)}, u32[]{:S(2)}) collective-permute-start(bf16[256,256]{1,0:T(8,128)(2,1)S(1)} %get-tuple-element.10), channel_id=1, source_target_pairs={{0,3},{1,2},{2,1},{3,0},{4,7},{5,6},{6,5},{7,4},{8,11},{9,10},{10,... | collective-permute-start | bytes 393224 | tf_op jit(solution)/shard_map/ppermute | solution.py:134
  48.3 11.8 %copy-start.2 = (s32[2]{0:T(128)S(1)}, s32[2]{0:T(128)}, u32[]{:S(2)}) copy-start(s32[2]{0:T(128)} %size_ref.3) | copy-start | bytes 28
  48.3 6.0 %collective-permute-start.20 = (bf16[256,256]{1,0:T(8,128)(2,1)S(1)}, bf16[256,256]{1,0:T(8,128)(2,1)S(1)}, u32[]{:S(2)}, u32[]{:S(2)}) collective-permute-start(bf16[256,256]{1,0:T(8,128)(2,1)S(1)} %get-tuple-element.16), channel_id=1, source_target_pairs={{0,1},{1,0},{2,3},{3,2},{4,5},{5,4},{6,7},{7,6},{8,9},{9,8},{10,11... | collective-permute-start | bytes 393224 | tf_op jit(solution)/shard_map/ppermute | solution.py:134
  48.4 6.4 %collective-permute-start.21 = (bf16[256,256]{1,0:T(8,128)(2,1)S(1)}, bf16[256,256]{1,0:T(8,128)(2,1)S(1)}, u32[]{:S(2)}, u32[]{:S(2)}) collective-permute-start(bf16[256,256]{1,0:T(8,128)(2,1)S(1)} %get-tuple-element.15), channel_id=1, source_target_pairs={{0,2},{1,3},{2,0},{3,1},{4,6},{5,7},{6,4},{7,5},{8,10},{9,11},{10,... | collective-permute-start | bytes 393224 | tf_op jit(solution)/shard_map/ppermute | solution.py:134
  48.5 8.2 %collective-permute-start.22 = (bf16[256,256]{1,0:T(8,128)(2,1)S(1)}, bf16[256,256]{1,0:T(8,128)(2,1)S(1)}, u32[]{:S(2)}, u32[]{:S(2)}) collective-permute-start(bf16[256,256]{1,0:T(8,128)(2,1)S(1)} %get-tuple-element.14), channel_id=1, source_target_pairs={{0,3},{1,2},{2,1},{3,0},{4,7},{5,6},{6,5},{7,4},{8,11},{9,10},{10,... | collective-permute-start | bytes 393224 | tf_op jit(solution)/shard_map/ppermute | solution.py:134
  50.8 21.5 %collective-permute-start.19 = (bf16[2,256,256]{2,1,0:T(8,128)(2,1)S(1)}, bf16[2,256,256]{2,1,0:T(8,128)(2,1)S(1)}, u32[]{:S(2)}, u32[]{:S(2)}) collective-permute-start(bf16[2,256,256]{2,1,0:T(8,128)(2,1)S(1)} %add_convert_fusion.1), channel_id=1, source_target_pairs={{0,8},{1,9},{2,10},{3,11},{4,12},{5,13},{6,14},{7,15},{8,0},{9,1},... | collective-permute-start | bytes 786440 | tf_op jit(solution)/shard_map/ppermute | solution.py:137
  56.9 15.3 %collective-permute-start.23 = (bf16[2,256,256]{2,1,0:T(8,128)(2,1)S(1)}, bf16[2,256,256]{2,1,0:T(8,128)(2,1)S(1)}, u32[]{:S(2)}, u32[]{:S(2)}) collective-permute-start(bf16[2,256,256]{2,1,0:T(8,128)(2,1)S(1)} %add_convert_fusion), channel_id=1, source_target_pairs={{0,4},{1,5},{2,6},{3,7},{4,8},{5,9},{6,10},{7,11},{8,12},{9,13},{1... | collective-permute-start | bytes 786440 | tf_op jit(solution)/shard_map/ppermute | solution.py:137

commit v2 on v1

--- a/solution.py
+++ b/solution.py
@@ -38,7 +38,7 @@
 
 
 def list_kernel(
-    columns, pairs, me_ref, source_ref, owner_ref, dispatch_ref, result_ref, list_ref, pair_ref
+    columns, me_ref, place_ref, source_ref, owner_ref, dispatch_ref, result_ref, list_ref, pair_ref
 ):
     tiles = source_ref.shape[0]
     depth = columns // GROUP
@@ -57,7 +57,7 @@
         @pl.when(live)
         def _():
             list_ref[later, 0, count] = t
-            list_ref[later, 1, count] = (me ^ s) * pairs + jnp.maximum(pair, 0)
+            list_ref[later, 1, count] = place_ref[me ^ s] + jnp.maximum(pair, 0)
             list_ref[later, 2, count] = (row - later) * GROUP + (g ^ (o % GROUP))
 
         one = live.astype(jnp.int32)
@@ -146,31 +146,34 @@
         name="mask",
     )(pno_size, amplitudes)
 
-    lane, across = [masked] + [None] * (depth - 1), [None] * depth
-    for x in range(1, depth, 2):
-        lane[x] = swap(masked, x * GROUP)
-        across[x - 1 if x == 1 else x] = swap(lane[x - 1 if x == 1 else x], 2)
-    across[1] = swap(lane[1], 2)
-    for x in range(2, depth, 2):
-        lane[x] = swap(lane[x + 1], GROUP)
-        across[x] = jnp.concatenate(
+    odd, even = list(range(depth - 1, 0, -2)), list(range(2, depth, 2))
+    lane = {x: swap(masked, x * GROUP) for x in odd} | {0: masked}
+    lane |= {x: swap(lane[x + 1], GROUP) for x in even}
+    across = {x: swap(lane[x], 2) for x in [0] + odd}
+    across |= {
+        x: jnp.concatenate(
             [swap(lane[x][: pairs // 2], 2), swap(across[x + 1][pairs // 2 :], GROUP)]
         )
-    everyone = []
-    for x in range(depth):
-        everyone += [lane[x], swap(lane[x], 1), across[x], swap(across[x], 1)]
-    everyone = jnp.concatenate(everyone)
+        for x in even
+    }
+    held, places = [], []
+    for x in odd + [0] + even:
+        for m, part in ((x * GROUP, lane[x]), (x * GROUP + 2, across[x])):
+            held += [part, swap(part, 1)]
+            places += [m, m ^ 1]
+    everyone = jnp.concatenate(held)
+    place = jnp.array([places.index(m) * pairs for m in range(columns)], jnp.int32)
 
     tile_list, fed = pl.pallas_call(
-        functools.partial(list_kernel, columns, pairs),
+        functools.partial(list_kernel, columns),
         out_shape=[
             jax.ShapeDtypeStruct((2, 4, tiles + UNROLL), jnp.int32),
             jax.ShapeDtypeStruct((half + 1, GROUP), jnp.int32),
         ],
-        in_specs=[SMEM()] * 5,
+        in_specs=[SMEM()] * 6,
         out_specs=[SMEM(), SMEM()],
         name="tile_list",
-    )(me[None], tile_source, tile_owner, dispatch_table, result_list)
+    )(me[None], place, tile_source, tile_owner, dispatch_table, result_list)
 
     def sums_of(part, rows, *after):
         return pl.pallas_call(
@@ -220,8 +223,8 @@
 
     total = functools.reduce(jnp.add, [part.astype(jnp.float32) for part in coupled], base)
     lanes = jnp.arange(width, dtype=jnp.int32)
-    held = lanes[None, :] < pno_size[:, None]
-    return jnp.where(held[:, :, None] & held[:, None, :], total, 0.0)
+    live = lanes[None, :] < pno_size[:, None]
+    return jnp.where(live[:, :, None] & live[:, None, :], total, 0.0)
 
 
 def solution(mesh):

time: 75.2 us -> 73.3 us (0.975); the launches traced: 74.4 us -> 73.4 us
  starting transfers between devices: 23 us -> 29 us
  waiting for transfers between devices: 30.8 us -> 24.8 us
  local copies, waits for them, and re-layouts: 1.99 us -> 1.04 us
    ppermute x22, waiting for transfers between devices: 20.8 us -> 12.1 us  [swap(): return lax.ppermute(value, 'col', [(i, i ^ m) for i in range(columns)])]
    ppermute x22, starting transfers between devices: 16.4 us -> 22.1 us  [swap(): return lax.ppermute(value, 'col', [(i, i ^ m) for i in range(columns)])]
    ppermute x2, waiting for transfers between devices: 10.1 us -> 12.7 us  [ahead(): lax.ppermute(value, 'col', [(i, (i + steps * GROUP) % columns) for i in r...]
    unnamed x22 -> x24, local copies, waits for them, and re-layouts: 1.25 us -> 0.31 us
  transfers between devices with their start and end apart: 24 -> 24, of which waited for: 10 -> 10; matrix products, arithmetic and copies ran while one was open for 5% -> 3% of each run, Pallas kernels for 13% -> 13%
where the time goes in v2:
time: 73.3 us; the launch traced here: 73.4 us
  starting transfers between devices  29 us (40%)
  waiting for transfers between devices  24.8 us (34%)
  Pallas kernels  14.4 us (20%)
  other arithmetic  3.77 us (5%)
  local copies, waits for them, and re-layouts  1.04 us (1%)
    ppermute x22, starting transfers between devices, swap(): return lax.ppermute(value, 'col', [(i, i ^ m) for i in range(columns)])  22.1 us
    ppermute x2, waiting for transfers between devices, ahead(): lax.ppermute(value, 'col', [(i, (i + steps * GROUP) % columns) for i in r...  12.7 us
    ppermute x22, waiting for transfers between devices, swap(): return lax.ppermute(value, 'col', [(i, i ^ m) for i in range(columns)])  12.1 us
    pallas_call x2, Pallas kernels, sums_of(): pl.pallas_call(functools.partial(tiles_kernel, part), out_shape=jax.Shape...  7.01 us
    ppermute x2, starting transfers between devices, ahead(): lax.ppermute(value, 'col', [(i, (i + steps * GROUP) % columns) for i in r...  6.89 us
    pallas_call x1, Pallas kernels, shards(): pl.pallas_call(functools.partial(list_kernel, columns), out_shape=[jax.Sh...  3.64 us
    select_n x1, other arithmetic, shards(): return jnp.where(live[:, :, None] & live[:, None, :], total, 0.0)  2.16 us
    pallas_call x1, Pallas kernels, shards(): pl.pallas_call(base_kernel, out_shape=jax.ShapeDtypeStruct(amplitudes.sha...  2.05 us
  transfers between devices with their start and end apart: 24, of which 10 were waited for; matrix products, arithmetic and copies ran while one was open for 3% of the time, Pallas kernels for 13%

profile of v2, /device:TPU:0, one launch (start us, length us, event | category | flops | bytes accessed | tf_op | source)
XLA Modules:
  0.0 73.4 jit_solution(15211586047756262933)
XLA Ops:
  0.0 1.7 %mask.1.masked_ref = bf16[2,256,256]{2,1,0:T(8,128)(2,1)} custom-call(s32[2]{0:T(128)} %size_ref.3, bf16[2,256,256]{2,1,0:T(8,128)(2,1)} %amplitude_ref.1), custom_call_target="tpu_custom_call" | custom-call | tf_op jit(solution)/shard_map/mask/pallas_call | solution.py:141
  1.7 5.0 %collective-permute-start = (bf16[2,256,256]{2,1,0:T(8,128)(2,1)}, bf16[2,256,256]{2,1,0:T(8,128)(2,1)S(1)}, u32[]{:S(2)}, u32[]{:S(2)}) collective-permute-start(bf16[2,256,256]{2,1,0:T(8,128)(2,1)} %mask.1.masked_ref), channel_id=1, source_target_pairs={{0,12},{1,13},{2,14},{3,15},{4,8},{5,9},{6,10},{7,11},{8,4},{9,5},... | collective-permute-start | bytes 786440 | tf_op jit(solution)/shard_map/ppermute | solution.py:134
  6.8 0.0 collective-permute-start.4
  6.8 1.5 %collective-permute-start.9 = (bf16[2,256,256]{2,1,0:T(8,128)(2,1)}, bf16[2,256,256]{2,1,0:T(8,128)(2,1)S(1)}, u32[]{:S(2)}, u32[]{:S(2)}) collective-permute-start(bf16[2,256,256]{2,1,0:T(8,128)(2,1)} %mask.1.masked_ref), channel_id=1, source_target_pairs={{0,2},{1,3},{2,0},{3,1},{4,6},{5,7},{6,4},{7,5},{8,10},{9,11},{10,... | collective-permute-start | bytes 786440 | tf_op jit(solution)/shard_map/ppermute | solution.py:134
  8.3 3.6 %tile_list.1 = (s32[2,4,72]{2,1,0:T(4,128)}, s32[3,4]{1,0:T(4,128)}) custom-call(s32[1]{0:T(128)} %bitcast.me_ref, s32[16]{0:T(128)} %constant.23.clone.place_ref, s32[64]{0:T(128)} %source_ref.1, s32[64]{0:T(128)} %owner_ref.1, s32[16,16]{1,0:T(8,128)} %dispatch_ref.1, s32[16,16]{1,0:T(8,128)} %result_ref.1), custom_call_target="tpu_custom_call" | custom-call | tf_op jit(solution)/shard_map/tile_list/pallas_call | solution.py:167
  12.0 0.7 slice_bitcast_fusion.20
  12.6 0.7 %compare_select_fusion.1 = (s32[4]{0:T(128)S(1)}, s32[4]{0:T(128)S(1)}) fusion(s32[3,4]{1,0:T(4,128)} %get-tuple-element.7, s32[]{:T(128)S(6)} %select_n.64), kind=kLoop, calls=%fused_computation.48 | loop fusion | flops 16 | bytes 68 | tf_op jit(solution)/shard_map/jit(_where)/select_n | solution.py:200
  13.4 0.1 iota_compare_fusion.1
  13.5 0.8 %collective-permute-done = bf16[2,256,256]{2,1,0:T(8,128)(2,1)S(1)} collective-permute-done((bf16[2,256,256]{2,1,0:T(8,128)(2,1)}, bf16[2,256,256]{2,1,0:T(8,128)(2,1)S(1)}, u32[]{:S(2)}, u32[]{:S(2)}) %collective-permute-start) | collective-permute-done | bytes 262176 | tf_op jit(solution)/shard_map/ppermute | solution.py:134
  14.3 0.0 collective-permute-start.1
  14.3 1.7 %collective-permute-start.2 = (bf16[2,256,256]{2,1,0:T(8,128)(2,1)S(1)}, bf16[2,256,256]{2,1,0:T(8,128)(2,1)S(1)}, u32[]{:S(2)}, u32[]{:S(2)}) collective-permute-start(bf16[2,256,256]{2,1,0:T(8,128)(2,1)S(1)} %collective-permute-done), channel_id=1, source_target_pairs={{0,2},{1,3},{2,0},{3,1},{4,6},{5,7},{6,4},{7,5},{8,10},{9,11},{10,... | collective-permute-start | bytes 786440 | tf_op jit(solution)/shard_map/ppermute | solution.py:134
  15.9 4.2 %collective-permute-start.11 = (bf16[2,256,256]{2,1,0:T(8,128)(2,1)S(1)}, bf16[2,256,256]{2,1,0:T(8,128)(2,1)S(1)}, u32[]{:S(2)}, u32[]{:S(2)}) collective-permute-start(bf16[2,256,256]{2,1,0:T(8,128)(2,1)S(1)} %collective-permute-done), channel_id=1, source_target_pairs={{0,4},{1,5},{2,6},{3,7},{4,0},{5,1},{6,2},{7,3},{8,12},{9,13},{10,... | collective-permute-start | bytes 786440 | tf_op jit(solution)/shard_map/ppermute | solution.py:134
  20.1 0.1 iota_compare_fusion
  20.2 0.0 collective-permute-done.4
  20.3 0.6 collective-permute-start.6
  20.8 6.0 %collective-permute-done.11 = bf16[2,256,256]{2,1,0:T(8,128)(2,1)S(1)} collective-permute-done((bf16[2,256,256]{2,1,0:T(8,128)(2,1)S(1)}, bf16[2,256,256]{2,1,0:T(8,128)(2,1)S(1)}, u32[]{:S(2)}, u32[]{:S(2)}) %collective-permute-start.11) | collective-permute-done | bytes 262176 | tf_op jit(solution)/shard_map/ppermute | solution.py:134
  26.9 0.6 collective-permute-start.13
  27.4 0.0 collective-permute-done.2
  27.4 0.0 copy-start
  27.5 1.8 %collective-permute-start.14 = (bf16[1,256,256]{2,1,0:T(8,128)(2,1)S(1)}, bf16[1,256,256]{2,1,0:T(8,128)(2,1)S(1)}, u32[]{:S(2)}, u32[]{:S(2)}) collective-permute-start(bf16[1,256,256]{2,1,0:T(8,128)(2,1)S(1)} %slice.113), channel_id=1, source_target_pairs={{0,4},{1,5},{2,6},{3,7},{4,0},{5,1},{6,2},{7,3},{8,12},{9,13},{10,... | collective-permute-start | bytes 393224 | tf_op jit(solution)/shard_map/ppermute | solution.py:134
  29.3 0.0 collective-permute-done.1
  29.3 0.0 collective-permute-start.3
  29.3 0.0 collective-permute-done.9
  29.3 0.6 collective-permute-start.8
  29.9 2.1 %collective-permute-done.13 = bf16[1,256,256]{2,1,0:T(8,128)(2,1)S(1)} collective-permute-done((bf16[1,256,256]{2,1,0:T(8,128)(2,1)S(1)}, bf16[1,256,256]{2,1,0:T(8,128)(2,1)S(1)}, u32[]{:S(2)}, u32[]{:S(2)}) %collective-permute-start.13) | collective-permute-done | bytes 131104 | tf_op jit(solution)/shard_map/ppermute | solution.py:134
  32.1 0.0 collective-permute-start.5
  32.1 0.4 collective-permute-done.14
  32.5 0.1 collective-permute-start.10
  32.6 0.0 collective-permute-done.6
  32.6 0.5 collective-permute-start.12
  33.1 0.0 collective-permute-done.3
  33.1 0.1 collective-permute-start.7
  33.2 0.3 collective-permute-done.5
  33.6 0.2 collective-permute-start.15
  33.8 1.0 %collective-permute-done.7 = bf16[2,256,256]{2,1,0:T(8,128)(2,1)S(1)} collective-permute-done((bf16[2,256,256]{2,1,0:T(8,128)(2,1)S(1)}, bf16[2,256,256]{2,1,0:T(8,128)(2,1)S(1)}, u32[]{:S(2)}, u32[]{:S(2)}) %collective-permute-start.7) | collective-permute-done | bytes 262176 | tf_op jit(solution)/shard_map/ppermute | solution.py:134
  34.8 0.0 copy-done.2
  34.8 0.0 collective-permute-done.8
  34.9 0.0 collective-permute-done.10
  35.0 0.0 collective-permute-done.12
  35.0 0.1 collective-permute-done.15
  35.2 3.1 %tiles.2 = bf16[4,256,256]{2,1,0:T(8,128)(2,1)S(1)} custom-call(s32[2,4,72]{2,1,0:T(4,128)S(1)} %copy-done.1, bf16[32,256,256]{2,1,0:T(8,128)(2,1)S(1)} %constant_dynamic-update-slice_fusion.masked_ref, bf16[64,256,256]{2,1,0:T(8,128)(2,1)S(1)} %copy-done), custom_call_target="tpu_custom_call" | custom-call | flops 2147483648 | bytes 4194304 | tf_op jit(solution)/shard_map/tiles/pallas_call | solution.py:179
  38.4 0.3 collective-permute-start.16
  38.7 2.9 %collective-permute-start.17 = (bf16[256,256]{1,0:T(8,128)(2,1)S(1)}, bf16[256,256]{1,0:T(8,128)(2,1)S(1)}, u32[]{:S(2)}, u32[]{:S(2)}) collective-permute-start(bf16[256,256]{1,0:T(8,128)(2,1)S(1)} %get-tuple-element.11), channel_id=1, source_target_pairs={{0,2},{1,3},{2,0},{3,1},{4,6},{5,7},{6,4},{7,5},{8,10},{9,11},{10,... | collective-permute-start | bytes 393224 | tf_op jit(solution)/shard_map/ppermute | solution.py:134
  41.6 0.2 collective-permute-start.18
  41.8 0.0 collective-permute-done.16.refs_0_
  41.8 3.9 %tiles.3 = bf16[4,256,256]{2,1,0:T(8,128)(2,1)S(1)} custom-call(s32[2,4,72]{2,1,0:T(4,128)S(1)} %copy-done.1, bf16[32,256,256]{2,1,0:T(8,128)(2,1)S(1)} %constant_dynamic-update-slice_fusion.masked_ref, bf16[64,256,256]{2,1,0:T(8,128)(2,1)S(1)} %copy-done, bf16[256,256]{1,0:T(8,128)(2,1)S(1)} %collective-permute-done.16.refs_0_), custom_call_target="tpu_custom_call" | custom-call | flops 2147483648 | bytes 4194304 | tf_op jit(solution)/shard_map/tiles/pallas_call | solution.py:179
  45.7 0.0 copy-start.3
  45.8 0.1 collective-permute-start.20
  45.9 1.8 %collective-permute-start.21 = (bf16[256,256]{1,0:T(8,128)(2,1)S(1)}, bf16[256,256]{1,0:T(8,128)(2,1)S(1)}, u32[]{:S(2)}, u32[]{:S(2)}) collective-permute-start(bf16[256,256]{1,0:T(8,128)(2,1)S(1)} %get-tuple-element.15), channel_id=1, source_target_pairs={{0,2},{1,3},{2,0},{3,1},{4,6},{5,7},{6,4},{7,5},{8,10},{9,11},{10,... | collective-permute-start | bytes 393224 | tf_op jit(solution)/shard_map/ppermute | solution.py:134
  47.6 0.1 collective-permute-start.22
  47.7 0.0 collective-permute-done.17
  47.8 0.6 collective-permute-done.18
  48.4 0.2 add_convert_fusion.1
  48.6 4.8 %collective-permute-start.19 = (bf16[2,256,256]{2,1,0:T(8,128)(2,1)S(1)}, bf16[2,256,256]{2,1,0:T(8,128)(2,1)S(1)}, u32[]{:S(2)}, u32[]{:S(2)}) collective-permute-start(bf16[2,256,256]{2,1,0:T(8,128)(2,1)S(1)} %add_convert_fusion.1), channel_id=1, source_target_pairs={{0,8},{1,9},{2,10},{3,11},{4,12},{5,13},{6,14},{7,15},{8,0},{9,1},... | collective-permute-start | bytes 786440 | tf_op jit(solution)/shard_map/ppermute | solution.py:137
  53.4 0.0 collective-permute-done.20
  53.5 0.0 collective-permute-done.21
  53.5 0.6 collective-permute-done.22
  54.2 0.2 add_convert_fusion
  54.4 2.1 %collective-permute-start.23 = (bf16[2,256,256]{2,1,0:T(8,128)(2,1)S(1)}, bf16[2,256,256]{2,1,0:T(8,128)(2,1)S(1)}, u32[]{:S(2)}, u32[]{:S(2)}) collective-permute-start(bf16[2,256,256]{2,1,0:T(8,128)(2,1)S(1)} %add_convert_fusion), channel_id=1, source_target_pairs={{0,4},{1,5},{2,6},{3,7},{4,8},{5,9},{6,10},{7,11},{8,12},{9,13},{1... | collective-permute-start | bytes 786440 | tf_op jit(solution)/shard_map/ppermute | solution.py:137
  56.4 0.1 iota_compare_fusion.3
  56.5 2.0 %base.1 = f32[2,256,256]{2,1,0:T(8,128)} custom-call(s32[2]{0:T(128)} %size_ref.3, f32[2,256]{1,0:T(2,128)} %energy_ref.1, bf16[2,256,256]{2,1,0:T(8,128)(2,1)} %integral_ref.1, bf16[2,256,256]{2,1,0:T(8,128)(2,1)} %mask.1.masked_ref), custom_call_target="tpu_custom_call" | custom-call | tf_op jit(solution)/shard_map/base/pallas_call | solution.py:216
  58.6 12.7 %collective-permute-done.19 = bf16[2,256,256]{2,1,0:T(8,128)(2,1)S(1)} collective-permute-done((bf16[2,256,256]{2,1,0:T(8,128)(2,1)S(1)}, bf16[2,256,256]{2,1,0:T(8,128)(2,1)S(1)}, u32[]{:S(2)}, u32[]{:S(2)}) %collective-permute-start.19) | collective-permute-done | bytes 262176 | tf_op jit(solution)/shard_map/ppermute | solution.py:137
  71.2 0.0 collective-permute-done.23
  71.2 2.2 %add_select_fusion = f32[2,256,256]{2,1,0:T(8,128)} fusion(bf16[2,256,256]{2,1,0:T(8,128)(2,1)S(1)} %collective-permute-done.23, bf16[2,256,256]{2,1,0:T(8,128)(2,1)S(1)} %collective-permute-done.19, f32[2,256,256]{2,1,0:T(8,128)} %base.1, f32[256,256]{1,0:T(8,128)S(1)} %convert_element_type.50, f32[256,256]{1,0:T(8,128)S(1)} %convert_element_type.49, ...), kind=kLoop, calls=%fused_computation | loop fusion | flops 1835008 | bytes 2621960 | tf_op jit(solution)/shard_map/jit(_where)/select_n | solution.py:227
  (36 shorter events, 0.6 us)
Async XLA Ops:
  1.7 33.1 %copy-start.2 = (bf16[2,256,256]{2,1,0:T(8,128)(2,1)S(1)}, bf16[2,256,256]{2,1,0:T(8,128)(2,1)}, u32[]{:S(2)}) copy-start(bf16[2,256,256]{2,1,0:T(8,128)(2,1)} %mask.1.masked_ref) | copy-start | bytes 786436
  1.7 12.6 %collective-permute-start = (bf16[2,256,256]{2,1,0:T(8,128)(2,1)}, bf16[2,256,256]{2,1,0:T(8,128)(2,1)S(1)}, u32[]{:S(2)}, u32[]{:S(2)}) collective-permute-start(bf16[2,256,256]{2,1,0:T(8,128)(2,1)} %mask.1.masked_ref), channel_id=1, source_target_pairs={{0,12},{1,13},{2,14},{3,15},{4,8},{5,9},{6,10},{7,11},{8,4},{9,5},... | collective-permute-start | bytes 786440 | tf_op jit(solution)/shard_map/ppermute | solution.py:134
  6.8 13.5 %collective-permute-start.4 = (bf16[2,256,256]{2,1,0:T(8,128)(2,1)}, bf16[2,256,256]{2,1,0:T(8,128)(2,1)S(1)}, u32[]{:S(2)}, u32[]{:S(2)}) collective-permute-start(bf16[2,256,256]{2,1,0:T(8,128)(2,1)} %mask.1.masked_ref), channel_id=1, source_target_pairs={{0,4},{1,5},{2,6},{3,7},{4,0},{5,1},{6,2},{7,3},{8,12},{9,13},{10,... | collective-permute-start | bytes 786440 | tf_op jit(solution)/shard_map/ppermute | solution.py:134
  6.8 22.5 %collective-permute-start.9 = (bf16[2,256,256]{2,1,0:T(8,128)(2,1)}, bf16[2,256,256]{2,1,0:T(8,128)(2,1)S(1)}, u32[]{:S(2)}, u32[]{:S(2)}) collective-permute-start(bf16[2,256,256]{2,1,0:T(8,128)(2,1)} %mask.1.masked_ref), channel_id=1, source_target_pairs={{0,2},{1,3},{2,0},{3,1},{4,6},{5,7},{6,4},{7,5},{8,10},{9,11},{10,... | collective-permute-start | bytes 786440 | tf_op jit(solution)/shard_map/ppermute | solution.py:134
  14.3 15.0 %collective-permute-start.1 = (bf16[2,256,256]{2,1,0:T(8,128)(2,1)S(1)}, bf16[2,256,256]{2,1,0:T(8,128)(2,1)S(1)}, u32[]{:S(2)}, u32[]{:S(2)}) collective-permute-start(bf16[2,256,256]{2,1,0:T(8,128)(2,1)S(1)} %collective-permute-done), channel_id=1, source_target_pairs={{0,1},{1,0},{2,3},{3,2},{4,5},{5,4},{6,7},{7,6},{8,9},{9,8},{10,11... | collective-permute-start | bytes 786440 | tf_op jit(solution)/shard_map/ppermute | solution.py:134
  14.3 13.1 %collective-permute-start.2 = (bf16[2,256,256]{2,1,0:T(8,128)(2,1)S(1)}, bf16[2,256,256]{2,1,0:T(8,128)(2,1)S(1)}, u32[]{:S(2)}, u32[]{:S(2)}) collective-permute-start(bf16[2,256,256]{2,1,0:T(8,128)(2,1)S(1)} %collective-permute-done), channel_id=1, source_target_pairs={{0,2},{1,3},{2,0},{3,1},{4,6},{5,7},{6,4},{7,5},{8,10},{9,11},{10,... | collective-permute-start | bytes 786440 | tf_op jit(solution)/shard_map/ppermute | solution.py:134
  15.9 10.9 %collective-permute-start.11 = (bf16[2,256,256]{2,1,0:T(8,128)(2,1)S(1)}, bf16[2,256,256]{2,1,0:T(8,128)(2,1)S(1)}, u32[]{:S(2)}, u32[]{:S(2)}) collective-permute-start(bf16[2,256,256]{2,1,0:T(8,128)(2,1)S(1)} %collective-permute-done), channel_id=1, source_target_pairs={{0,4},{1,5},{2,6},{3,7},{4,0},{5,1},{6,2},{7,3},{8,12},{9,13},{10,... | collective-permute-start | bytes 786440 | tf_op jit(solution)/shard_map/ppermute | solution.py:134
  20.3 12.3 %collective-permute-start.6 = (bf16[2,256,256]{2,1,0:T(8,128)(2,1)S(1)}, bf16[2,256,256]{2,1,0:T(8,128)(2,1)S(1)}, u32[]{:S(2)}, u32[]{:S(2)}) collective-permute-start(bf16[2,256,256]{2,1,0:T(8,128)(2,1)S(1)} %collective-permute-done.4), channel_id=1, source_target_pairs={{0,2},{1,3},{2,0},{3,1},{4,6},{5,7},{6,4},{7,5},{8,10},{9,11},{10,... | collective-permute-start | bytes 786440 | tf_op jit(solution)/shard_map/ppermute | solution.py:134
  26.9 5.2 %collective-permute-start.13 = (bf16[1,256,256]{2,1,0:T(8,128)(2,1)S(1)}, bf16[1,256,256]{2,1,0:T(8,128)(2,1)S(1)}, u32[]{:S(2)}, u32[]{:S(2)}) collective-permute-start(bf16[1,256,256]{2,1,0:T(8,128)(2,1)S(1)} %slice.112), channel_id=1, source_target_pairs={{0,2},{1,3},{2,0},{3,1},{4,6},{5,7},{6,4},{7,5},{8,10},{9,11},{10,... | collective-permute-start | bytes 393224 | tf_op jit(solution)/shard_map/ppermute | solution.py:134
  27.4 7.7 %copy-start.1 = (s32[2,4,72]{2,1,0:T(4,128)S(1)}, s32[2,4,72]{2,1,0:T(4,128)}, u32[]{:S(2)}) copy-start(s32[2,4,72]{2,1,0:T(4,128)} %get-tuple-element.8.list_ref) | copy-start | bytes 6916
  27.4 7.7 %copy-start = (bf16[64,256,256]{2,1,0:T(8,128)(2,1)S(1)}, bf16[64,256,256]{2,1,0:T(8,128)(2,1)}, u32[]{:S(2)}) copy-start(bf16[64,256,256]{2,1,0:T(8,128)(2,1)} %transfer_ref.3) | copy-start | bytes 25165828
  27.5 5.0 %collective-permute-start.14 = (bf16[1,256,256]{2,1,0:T(8,128)(2,1)S(1)}, bf16[1,256,256]{2,1,0:T(8,128)(2,1)S(1)}, u32[]{:S(2)}, u32[]{:S(2)}) collective-permute-start(bf16[1,256,256]{2,1,0:T(8,128)(2,1)S(1)} %slice.113), channel_id=1, source_target_pairs={{0,4},{1,5},{2,6},{3,7},{4,0},{5,1},{6,2},{7,3},{8,12},{9,13},{10,... | collective-permute-start | bytes 393224 | tf_op jit(solution)/shard_map/ppermute | solution.py:134
  29.3 3.8 %collective-permute-start.3 = (bf16[2,256,256]{2,1,0:T(8,128)(2,1)S(1)}, bf16[2,256,256]{2,1,0:T(8,128)(2,1)S(1)}, u32[]{:S(2)}, u32[]{:S(2)}) collective-permute-start(bf16[2,256,256]{2,1,0:T(8,128)(2,1)S(1)} %collective-permute-done.2), channel_id=1, source_target_pairs={{0,1},{1,0},{2,3},{3,2},{4,5},{5,4},{6,7},{7,6},{8,9},{9,8},{10,11... | collective-permute-start | bytes 786440 | tf_op jit(solution)/shard_map/ppermute | solution.py:134
  29.3 5.5 %collective-permute-start.8 = (bf16[2,256,256]{2,1,0:T(8,128)(2,1)}, bf16[2,256,256]{2,1,0:T(8,128)(2,1)S(1)}, u32[]{:S(2)}, u32[]{:S(2)}) collective-permute-start(bf16[2,256,256]{2,1,0:T(8,128)(2,1)} %mask.1.masked_ref), channel_id=1, source_target_pairs={{0,1},{1,0},{2,3},{3,2},{4,5},{5,4},{6,7},{7,6},{8,9},{9,8},{10,11... | collective-permute-start | bytes 786440 | tf_op jit(solution)/shard_map/ppermute | solution.py:134
  32.1 1.5 %collective-permute-start.5 = (bf16[2,256,256]{2,1,0:T(8,128)(2,1)S(1)}, bf16[2,256,256]{2,1,0:T(8,128)(2,1)S(1)}, u32[]{:S(2)}, u32[]{:S(2)}) collective-permute-start(bf16[2,256,256]{2,1,0:T(8,128)(2,1)S(1)} %collective-permute-done.4), channel_id=1, source_target_pairs={{0,1},{1,0},{2,3},{3,2},{4,5},{5,4},{6,7},{7,6},{8,9},{9,8},{10,11... | collective-permute-start | bytes 786440 | tf_op jit(solution)/shard_map/ppermute | solution.py:134
  32.5 2.4 %collective-permute-start.10 = (bf16[2,256,256]{2,1,0:T(8,128)(2,1)S(1)}, bf16[2,256,256]{2,1,0:T(8,128)(2,1)S(1)}, u32[]{:S(2)}, u32[]{:S(2)}) collective-permute-start(bf16[2,256,256]{2,1,0:T(8,128)(2,1)S(1)} %collective-permute-done.9), channel_id=1, source_target_pairs={{0,1},{1,0},{2,3},{3,2},{4,5},{5,4},{6,7},{7,6},{8,9},{9,8},{10,11... | collective-permute-start | bytes 786440 | tf_op jit(solution)/shard_map/ppermute | solution.py:134
  32.6 2.4 %collective-permute-start.12 = (bf16[2,256,256]{2,1,0:T(8,128)(2,1)S(1)}, bf16[2,256,256]{2,1,0:T(8,128)(2,1)S(1)}, u32[]{:S(2)}, u32[]{:S(2)}) collective-permute-start(bf16[2,256,256]{2,1,0:T(8,128)(2,1)S(1)} %collective-permute-done.11), channel_id=1, source_target_pairs={{0,1},{1,0},{2,3},{3,2},{4,5},{5,4},{6,7},{7,6},{8,9},{9,8},{10,11... | collective-permute-start | bytes 786440 | tf_op jit(solution)/shard_map/ppermute | solution.py:134
  33.1 1.7 %collective-permute-start.7 = (bf16[2,256,256]{2,1,0:T(8,128)(2,1)S(1)}, bf16[2,256,256]{2,1,0:T(8,128)(2,1)S(1)}, u32[]{:S(2)}, u32[]{:S(2)}) collective-permute-start(bf16[2,256,256]{2,1,0:T(8,128)(2,1)S(1)} %collective-permute-done.6), channel_id=1, source_target_pairs={{0,1},{1,0},{2,3},{3,2},{4,5},{5,4},{6,7},{7,6},{8,9},{9,8},{10,11... | collective-permute-start | bytes 786440 | tf_op jit(solution)/shard_map/ppermute | solution.py:134
  33.6 1.6 %collective-permute-start.15 = (bf16[2,256,256]{2,1,0:T(8,128)(2,1)S(1)}, bf16[2,256,256]{2,1,0:T(8,128)(2,1)S(1)}, u32[]{:S(2)}, u32[]{:S(2)}) collective-permute-start(bf16[2,256,256]{2,1,0:T(8,128)(2,1)S(1)} %pad_maximum_fusion), channel_id=1, source_target_pairs={{0,1},{1,0},{2,3},{3,2},{4,5},{5,4},{6,7},{7,6},{8,9},{9,8},{10,11... | collective-permute-start | bytes 786440 | tf_op jit(solution)/shard_map/ppermute | solution.py:134
  38.4 3.4 %collective-permute-start.16 = (bf16[256,256]{1,0:T(8,128)(2,1)S(1)}, bf16[256,256]{1,0:T(8,128)(2,1)S(1)}, u32[]{:S(2)}, u32[]{:S(2)}) collective-permute-start(bf16[256,256]{1,0:T(8,128)(2,1)S(1)} %get-tuple-element.12), channel_id=1, source_target_pairs={{0,1},{1,0},{2,3},{3,2},{4,5},{5,4},{6,7},{7,6},{8,9},{9,8},{10,11... | collective-permute-start | bytes 393224 | tf_op jit(solution)/shard_map/ppermute | solution.py:134
  38.7 9.1 %collective-permute-start.17 = (bf16[256,256]{1,0:T(8,128)(2,1)S(1)}, bf16[256,256]{1,0:T(8,128)(2,1)S(1)}, u32[]{:S(2)}, u32[]{:S(2)}) collective-permute-start(bf16[256,256]{1,0:T(8,128)(2,1)S(1)} %get-tuple-element.11), channel_id=1, source_target_pairs={{0,2},{1,3},{2,0},{3,1},{4,6},{5,7},{6,4},{7,5},{8,10},{9,11},{10,... | collective-permute-start | bytes 393224 | tf_op jit(solution)/shard_map/ppermute | solution.py:134
  41.6 6.8 %collective-permute-start.18 = (bf16[256,256]{1,0:T(8,128)(2,1)S(1)}, bf16[256,256]{1,0:T(8,128)(2,1)S(1)}, u32[]{:S(2)}, u32[]{:S(2)}) collective-permute-start(bf16[256,256]{1,0:T(8,128)(2,1)S(1)} %get-tuple-element.10), channel_id=1, source_target_pairs={{0,3},{1,2},{2,1},{3,0},{4,7},{5,6},{6,5},{7,4},{8,11},{9,10},{10,... | collective-permute-start | bytes 393224 | tf_op jit(solution)/shard_map/ppermute | solution.py:134
  45.7 10.7 %copy-start.3 = (s32[2]{0:T(128)S(1)}, s32[2]{0:T(128)}, u32[]{:S(2)}) copy-start(s32[2]{0:T(128)} %size_ref.3) | copy-start | bytes 28
  45.8 7.7 %collective-permute-start.20 = (bf16[256,256]{1,0:T(8,128)(2,1)S(1)}, bf16[256,256]{1,0:T(8,128)(2,1)S(1)}, u32[]{:S(2)}, u32[]{:S(2)}) collective-permute-start(bf16[256,256]{1,0:T(8,128)(2,1)S(1)} %get-tuple-element.16), channel_id=1, source_target_pairs={{0,1},{1,0},{2,3},{3,2},{4,5},{5,4},{6,7},{7,6},{8,9},{9,8},{10,11... | collective-permute-start | bytes 393224 | tf_op jit(solution)/shard_map/ppermute | solution.py:134
  45.9 7.6 %collective-permute-start.21 = (bf16[256,256]{1,0:T(8,128)(2,1)S(1)}, bf16[256,256]{1,0:T(8,128)(2,1)S(1)}, u32[]{:S(2)}, u32[]{:S(2)}) collective-permute-start(bf16[256,256]{1,0:T(8,128)(2,1)S(1)} %get-tuple-element.15), channel_id=1, source_target_pairs={{0,2},{1,3},{2,0},{3,1},{4,6},{5,7},{6,4},{7,5},{8,10},{9,11},{10,... | collective-permute-start | bytes 393224 | tf_op jit(solution)/shard_map/ppermute | solution.py:134
  47.6 6.5 %collective-permute-start.22 = (bf16[256,256]{1,0:T(8,128)(2,1)S(1)}, bf16[256,256]{1,0:T(8,128)(2,1)S(1)}, u32[]{:S(2)}, u32[]{:S(2)}) collective-permute-start(bf16[256,256]{1,0:T(8,128)(2,1)S(1)} %get-tuple-element.14), channel_id=1, source_target_pairs={{0,3},{1,2},{2,1},{3,0},{4,7},{5,6},{6,5},{7,4},{8,11},{9,10},{10,... | collective-permute-start | bytes 393224 | tf_op jit(solution)/shard_map/ppermute | solution.py:134
  48.6 22.6 %collective-permute-start.19 = (bf16[2,256,256]{2,1,0:T(8,128)(2,1)S(1)}, bf16[2,256,256]{2,1,0:T(8,128)(2,1)S(1)}, u32[]{:S(2)}, u32[]{:S(2)}) collective-permute-start(bf16[2,256,256]{2,1,0:T(8,128)(2,1)S(1)} %add_convert_fusion.1), channel_id=1, source_target_pairs={{0,8},{1,9},{2,10},{3,11},{4,12},{5,13},{6,14},{7,15},{8,0},{9,1},... | collective-permute-start | bytes 786440 | tf_op jit(solution)/shard_map/ppermute | solution.py:137
  54.4 16.9 %collective-permute-start.23 = (bf16[2,256,256]{2,1,0:T(8,128)(2,1)S(1)}, bf16[2,256,256]{2,1,0:T(8,128)(2,1)S(1)}, u32[]{:S(2)}, u32[]{:S(2)}) collective-permute-start(bf16[2,256,256]{2,1,0:T(8,128)(2,1)S(1)} %add_convert_fusion), channel_id=1, source_target_pairs={{0,4},{1,5},{2,6},{3,7},{4,8},{5,9},{6,10},{7,11},{8,12},{9,13},{1... | collective-permute-start | bytes 786440 | tf_op jit(solution)/shard_map/ppermute | solution.py:137

commit v3 on v2

--- a/solution.py
+++ b/solution.py
@@ -38,35 +38,38 @@
 
 
 def list_kernel(
-    columns, me_ref, place_ref, source_ref, owner_ref, dispatch_ref, result_ref, list_ref, pair_ref
+    columns, early, me_ref, place_ref, source_ref, owner_ref, dispatch_ref, result_ref, transfer_ref, list_ref, pair_ref, held_ref, arrived
 ):
     tiles = source_ref.shape[0]
     depth = columns // GROUP
     half = depth // 2
     me = me_ref[0]
+    fetch = pltpu.make_async_copy(transfer_ref, held_ref, arrived)
+    fetch.start()
     z, g = me // GROUP, me % GROUP
 
     def visit(t, counts):
         s, o = source_ref[t], owner_ref[t]
         pair = dispatch_ref[s, me]
         live = (pair >= 0) & (result_ref[me, o] >= 0)
+        where = place_ref[me ^ s]
         row = (o // GROUP - z + depth) % half
-        later = (row > 0).astype(jnp.int32)
-        count = jnp.where(row > 0, counts[1], counts[0])
+        part = jnp.where(where < early, 0, jnp.where(row == 0, 1, 2))
+        count = jnp.where(part == 0, counts[0], jnp.where(part == 1, counts[1], counts[2]))
 
         @pl.when(live)
         def _():
-            list_ref[later, 0, count] = t
-            list_ref[later, 1, count] = place_ref[me ^ s] + jnp.maximum(pair, 0)
-            list_ref[later, 2, count] = (row - later) * GROUP + (g ^ (o % GROUP))
+            list_ref[part, 0, count] = t
+            list_ref[part, 1, count] = jnp.where(part == 0, where, where - early) + jnp.maximum(pair, 0)
+            list_ref[part, 2, count] = (row - part // 2) * GROUP + (g ^ (o % GROUP))
 
         one = live.astype(jnp.int32)
-        return counts[0] + one * (1 - later), counts[1] + one * later
-
-    counts = lax.fori_loop(0, tiles, visit, (jnp.int32(0), jnp.int32(0)))
-    for part in range(2):
+        return tuple(n + one * (part == p).astype(jnp.int32) for p, n in enumerate(counts))
+
+    counts = lax.fori_loop(0, tiles, visit, (jnp.int32(0),) * 3)
+    for part, rows in enumerate((half, 1, half - 1)):
         count = counts[part]
-        spare = GROUP * (half - 1 if part else 1)
+        spare = GROUP * rows
 
         def fill(i, _):
             list_ref[part, 0, i] = 0
@@ -79,13 +82,10 @@
     for steps in range(half + 1):
         for m in range(GROUP):
             pair_ref[steps, m] = result_ref[z * GROUP + (g ^ m), (z + steps) % depth * GROUP + g]
-
-
-def tiles_kernel(part, list_ref, masked_ref, transfer_ref, *refs):
-    block_ref, total = refs[-2:]
-    steps = (list_ref[part, 3, 0] + UNROLL - 1) // UNROLL
-    total[...] = jnp.zeros_like(total)
-
+    fetch.wait()
+
+
+def add_tiles(part, list_ref, masked_ref, transfer_ref, total):
     def step(n, _):
         places = [n * UNROLL + u for u in range(UNROLL)]
         tiles = [list_ref[part, 0, i] for i in places]
@@ -106,8 +106,20 @@
             )
         return 0
 
-    lax.fori_loop(0, steps, step, 0)
-    for b in range(block_ref.shape[0]):
+    lax.fori_loop(0, (list_ref[part, 3, 0] + UNROLL - 1) // UNROLL, step, 0)
+
+
+def early_kernel(list_ref, masked_ref, transfer_ref, total):
+    total[...] = jnp.zeros_like(total)
+    add_tiles(0, list_ref, masked_ref, transfer_ref, total)
+
+
+def late_kernel(part, list_ref, masked_ref, transfer_ref, sum_ref, *refs):
+    block_ref, total = refs[-2:]
+    blocks = block_ref.shape[0]
+    total[:blocks] = sum_ref[pl.ds(GROUP * (part - 1), blocks)]
+    add_tiles(part, list_ref, masked_ref, transfer_ref, total)
+    for b in range(blocks):
         block_ref[b] = total[b].astype(block_ref.dtype)
 
 
@@ -140,7 +152,7 @@
 
     masked = pl.pallas_call(
         mask_kernel,
-        out_shape=jax.ShapeDtypeStruct(amplitudes.shape, jnp.bfloat16),
+        out_shape=pltpu.VMEM(amplitudes.shape, jnp.bfloat16),
         in_specs=[SMEM(), VMEM()],
         out_specs=VMEM(),
         name="mask",
@@ -150,50 +162,74 @@
     lane = {x: swap(masked, x * GROUP) for x in odd} | {0: masked}
     lane |= {x: swap(lane[x + 1], GROUP) for x in even}
     across = {x: swap(lane[x], 2) for x in [0] + odd}
-    across |= {
-        x: jnp.concatenate(
+
+    def with_other(parts):
+        held = [value for part in parts.values() for value in (part, swap(part, 1))]
+        return jnp.concatenate(held), [n for m in parts for n in (m, m ^ 1)]
+
+    own = {x * GROUP: lane[x] for x in odd + [0]} | {2: across[0]}
+    early, places = with_other(own)
+    later = [x * GROUP + 2 for x in odd] + [x * GROUP + y for x in even for y in (0, 2)]
+    order = places + [n for m in later for n in (m, m ^ 1)]
+    place = jnp.array([order.index(m) * pairs for m in range(columns)], jnp.int32)
+
+    in_hbm = [
+        pltpu.with_memory_space_constraint(value, pltpu.HBM)
+        for value in (tile_source, tile_owner, dispatch_table, result_list, subspace_transfers)
+    ]
+    tile_list, fed, transfers = pl.pallas_call(
+        functools.partial(list_kernel, columns, len(places) * pairs),
+        out_shape=[
+            jax.ShapeDtypeStruct((3, 4, tiles + UNROLL), jnp.int32),
+            jax.ShapeDtypeStruct((half + 1, GROUP), jnp.int32),
+            pltpu.VMEM(subspace_transfers.shape, jnp.bfloat16),
+        ],
+        in_specs=[SMEM()] * 6 + [HBM()],
+        out_specs=[SMEM(), SMEM(), VMEM()],
+        scratch_shapes=[pltpu.SemaphoreType.DMA],
+        compiler_params=pltpu.CompilerParams(vmem_limit_bytes=16 * 2**20),
+        name="tile_list",
+    )(me[None], place, *in_hbm)
+
+    work = pl.CostEstimate(
+        flops=2 * tiles * width**3, bytes_accessed=tiles * width**2, transcendentals=0
+    )
+    totals = pl.pallas_call(
+        early_kernel,
+        out_shape=jax.ShapeDtypeStruct((columns // 2 + 1, width, width), jnp.float32),
+        in_specs=[SMEM(), VMEM(), VMEM()],
+        out_specs=VMEM(),
+        compiler_params=pltpu.CompilerParams(vmem_limit_bytes=16 * 2**20),
+        cost_estimate=work,
+        name="early_tiles",
+    )(tile_list, early, transfers)
+
+    for x in even:
+        lane[x], totals = lax.optimization_barrier((lane[x], totals))
+        across[x] = jnp.concatenate(
             [swap(lane[x][: pairs // 2], 2), swap(across[x + 1][pairs // 2 :], GROUP)]
         )
-        for x in even
-    }
-    held, places = [], []
-    for x in odd + [0] + even:
-        for m, part in ((x * GROUP, lane[x]), (x * GROUP + 2, across[x])):
-            held += [part, swap(part, 1)]
-            places += [m, m ^ 1]
-    everyone = jnp.concatenate(held)
-    place = jnp.array([places.index(m) * pairs for m in range(columns)], jnp.int32)
-
-    tile_list, fed = pl.pallas_call(
-        functools.partial(list_kernel, columns),
-        out_shape=[
-            jax.ShapeDtypeStruct((2, 4, tiles + UNROLL), jnp.int32),
-            jax.ShapeDtypeStruct((half + 1, GROUP), jnp.int32),
-        ],
-        in_specs=[SMEM()] * 6,
-        out_specs=[SMEM(), SMEM()],
-        name="tile_list",
-    )(me[None], place, tile_source, tile_owner, dispatch_table, result_list)
+    parts = {x * GROUP + 2: across[x] for x in odd}
+    parts |= {x * GROUP + y: part[x] for x in even for y, part in ((0, lane), (2, across))}
+    late, _ = with_other(parts)
 
     def sums_of(part, rows, *after):
         return pl.pallas_call(
-            functools.partial(tiles_kernel, part),
+            functools.partial(late_kernel, part),
             out_shape=jax.ShapeDtypeStruct((rows * GROUP, width, width), jnp.bfloat16),
-            in_specs=[SMEM(), VMEM(), VMEM()] + [HBM()] * len(after),
+            in_specs=[SMEM(), VMEM(), VMEM(), VMEM()] + [HBM()] * len(after),
             out_specs=VMEM(),
             scratch_shapes=[pltpu.VMEM((rows * GROUP + 1, width, width), jnp.float32)],
             compiler_params=pltpu.CompilerParams(vmem_limit_bytes=16 * 2**20),
-            cost_estimate=pl.CostEstimate(
-                flops=2 * tiles * width**3, bytes_accessed=tiles * width**2, transcendentals=0
-            ),
-            name="tiles",
-        )(tile_list, everyone, subspace_transfers, *after)
+            cost_estimate=work,
+            name="late_tiles",
+        )(tile_list, late, transfers, totals, *after)
 
     def spread(block):
         return [block[0]] + [swap(block[m], m) for m in range(1, GROUP)]
 
-    first = spread(sums_of(0, 1))
-    others = sums_of(1, half - 1, first[1])
+    first = spread(sums_of(1, 1))
+    others = sums_of(2, half - 1, first[1])
     rows = [first] + [spread(others[i * GROUP : (i + 1) * GROUP]) for i in range(half - 1)]
 
     near = (g ^ jnp.arange(GROUP, dtype=jnp.int32)) < g
@@ -215,7 +251,7 @@
 
     base = pl.pallas_call(
         base_kernel,
-        out_shape=jax.ShapeDtypeStruct(amplitudes.shape, jnp.float32),
+        out_shape=pltpu.VMEM(amplitudes.shape, jnp.float32),
         in_specs=[SMEM(), VMEM(), VMEM(), VMEM()],
         out_specs=VMEM(),
         name="base",

time: 73.3 us -> 68.8 us (0.939)
  starting transfers between devices: 29 us -> 25.3 us
  waiting for transfers between devices: 24.8 us -> 27.9 us
  Pallas kernels: 14.4 us -> 12.1 us
  other arithmetic: 3.77 us -> 1.99 us
    ppermute x22, waiting for transfers between devices: 12.1 us -> 17 us  [swap(): return lax.ppermute(value, 'col', [(i, i ^ m) for i in range(columns)])]
    pallas_call x5 -> x6, Pallas kernels: 14.4 us -> 12.1 us  [the longest x1 5.06 us: shards(): pl.pallas_call(functools.partial(list_kernel, columns, len(places) * pair...]
    ppermute x22, starting transfers between devices: 22.1 us -> 20.2 us  [swap(): return lax.ppermute(value, 'col', [(i, i ^ m) for i in range(columns)])]
    ppermute x2, starting transfers between devices: 6.89 us -> 5.08 us  [ahead(): lax.ppermute(value, 'col', [(i, (i + steps * GROUP) % columns) for i in r...]
    ppermute x2, waiting for transfers between devices: 12.7 us -> 10.9 us  [ahead(): lax.ppermute(value, 'col', [(i, (i + steps * GROUP) % columns) for i in r...]
    select_n x1, other arithmetic: 2.16 us -> 1.12 us  [shards(): return jnp.where(live[:, :, None] & live[:, None, :], total, 0.0)]
    select_n x1, other arithmetic: 0.74 us -> 0.01 us  [shards(): stays = jnp.where(near, fed[0], -1)]
  transfers between devices with their start and end apart: 24 -> 24, of which waited for: 10 -> 9; matrix products, arithmetic and copies ran while one was open for 3% -> 2% of each run, Pallas kernels for 13% -> 14%
where the time goes in v3:
time: 68.8 us; the launch traced here: 68.6 us
  waiting for transfers between devices  27.9 us (41%)
  starting transfers between devices  25.3 us (37%)
  Pallas kernels  12.1 us (18%)
  other arithmetic  1.99 us (3%)
  local copies, waits for them, and re-layouts  1.02 us (1%)
    ppermute x22, starting transfers between devices, swap(): return lax.ppermute(value, 'col', [(i, i ^ m) for i in range(columns)])  20.2 us
    ppermute x22, waiting for transfers between devices, swap(): return lax.ppermute(value, 'col', [(i, i ^ m) for i in range(columns)])  17 us
    ppermute x2, waiting for transfers between devices, ahead(): lax.ppermute(value, 'col', [(i, (i + steps * GROUP) % columns) for i in r...  10.9 us
    ppermute x2, starting transfers between devices, ahead(): lax.ppermute(value, 'col', [(i, (i + steps * GROUP) % columns) for i in r...  5.08 us
    pallas_call x1, Pallas kernels, shards(): pl.pallas_call(functools.partial(list_kernel, columns, len(places) * pair...  5.06 us
    pallas_call x2, Pallas kernels, sums_of(): pl.pallas_call(functools.partial(late_kernel, part), out_shape=jax.ShapeD...  3.11 us
    pallas_call x1, Pallas kernels, shards(): pl.pallas_call(early_kernel, out_shape=jax.ShapeDtypeStruct((columns // 2...  1.6 us
  transfers between devices with their start and end apart: 24, of which 9 were waited for; matrix products, arithmetic and copies ran while one was open for 2% of the time, Pallas kernels for 14%

profile of v3, /device:TPU:0, one launch (start us, length us, event | category | flops | bytes accessed | tf_op | source)
XLA Modules:
  0.0 68.6 jit_solution(6254950376381459810)
XLA Ops:
  0.0 1.0 %mask.1.masked_ref = bf16[2,256,256]{2,1,0:T(8,128)(2,1)S(1)} custom-call(s32[2]{0:T(128)} %size_ref.3, bf16[2,256,256]{2,1,0:T(8,128)(2,1)} %amplitude_ref.1), custom_call_target="tpu_custom_call" | custom-call | tf_op jit(solution)/shard_map/mask/pallas_call | solution.py:153
  1.0 0.0 copy-start
  1.1 5.1 %collective-permute-start = (bf16[2,256,256]{2,1,0:T(8,128)(2,1)S(1)}, bf16[2,256,256]{2,1,0:T(8,128)(2,1)S(1)}, u32[]{:S(2)}, u32[]{:S(2)}) collective-permute-start(bf16[2,256,256]{2,1,0:T(8,128)(2,1)S(1)} %mask.1.masked_ref), channel_id=1, source_target_pairs={{0,12},{1,13},{2,14},{3,15},{4,8},{5,9},{6,10},{7,11},{8,4},{9,5},... | collective-permute-start | bytes 786440 | tf_op jit(solution)/shard_map/ppermute | solution.py:146
  6.2 0.0 collective-permute-start.3
  6.2 0.0 collective-permute-start.9
  6.2 1.5 %collective-permute-start.10 = (bf16[2,256,256]{2,1,0:T(8,128)(2,1)S(1)}, bf16[2,256,256]{2,1,0:T(8,128)(2,1)S(1)}, u32[]{:S(2)}, u32[]{:S(2)}) collective-permute-start(bf16[2,256,256]{2,1,0:T(8,128)(2,1)S(1)} %mask.1.masked_ref), channel_id=1, source_target_pairs={{0,2},{1,3},{2,0},{3,1},{4,6},{5,7},{6,4},{7,5},{8,10},{9,11},{10,... | collective-permute-start | bytes 786440 | tf_op jit(solution)/shard_map/ppermute | solution.py:146
  7.7 0.7 copy-done.1
  8.4 5.1 %tile_list.1 = (s32[3,4,72]{2,1,0:T(4,128)S(1)}, s32[3,4]{1,0:T(4,128)S(1)}, bf16[64,256,256]{2,1,0:T(8,128)(2,1)S(1)}) custom-call(s32[1]{0:T(128)} %bitcast.me_ref, s32[16]{0:T(128)S(1)} %copy-done.1, s32[64]{0:T(128)} %source_ref.1, s32[64]{0:T(128)} %owner_ref.1, s32[16,16]{1,0:T(8,128)} %dispatch_ref.1, s32[16,16]{1,0:T(8,128)} %result_ref.1, ...), custom_call_target="tpu_custom_call" | custom-call | tf_op jit(solution)/shard_map/tile_list/pallas_call | solution.py:180
  13.4 0.1 iota_compare_fusion
  13.5 0.0 collective-permute-done
  13.5 0.2 collective-permute-start.7
  13.8 1.4 %collective-permute-start.1 = (bf16[2,256,256]{2,1,0:T(8,128)(2,1)S(1)}, bf16[2,256,256]{2,1,0:T(8,128)(2,1)S(1)}, u32[]{:S(2)}, u32[]{:S(2)}) collective-permute-start(bf16[2,256,256]{2,1,0:T(8,128)(2,1)S(1)} %collective-permute-done), channel_id=1, source_target_pairs={{0,2},{1,3},{2,0},{3,1},{4,6},{5,7},{6,4},{7,5},{8,10},{9,11},{10,... | collective-permute-start | bytes 786440 | tf_op jit(solution)/shard_map/ppermute | solution.py:146
  15.2 3.0 %collective-permute-done.3 = bf16[2,256,256]{2,1,0:T(8,128)(2,1)S(1)} collective-permute-done((bf16[2,256,256]{2,1,0:T(8,128)(2,1)S(1)}, bf16[2,256,256]{2,1,0:T(8,128)(2,1)S(1)}, u32[]{:S(2)}, u32[]{:S(2)}) %collective-permute-start.3) | collective-permute-done | bytes 262176 | tf_op jit(solution)/shard_map/ppermute | solution.py:146
  18.2 0.0 collective-permute-start.8
  18.2 0.0 collective-permute-done.7
  18.2 1.6 %collective-permute-start.4 = (bf16[2,256,256]{2,1,0:T(8,128)(2,1)S(1)}, bf16[2,256,256]{2,1,0:T(8,128)(2,1)S(1)}, u32[]{:S(2)}, u32[]{:S(2)}) collective-permute-start(bf16[2,256,256]{2,1,0:T(8,128)(2,1)S(1)} %collective-permute-done.3), channel_id=1, source_target_pairs={{0,2},{1,3},{2,0},{3,1},{4,6},{5,7},{6,4},{7,5},{8,10},{9,11},{10,... | collective-permute-start | bytes 786440 | tf_op jit(solution)/shard_map/ppermute | solution.py:146
  19.9 0.0 collective-permute-done.10
  19.9 1.7 %collective-permute-start.6 = (bf16[2,256,256]{2,1,0:T(8,128)(2,1)S(1)}, bf16[2,256,256]{2,1,0:T(8,128)(2,1)S(1)}, u32[]{:S(2)}, u32[]{:S(2)}) collective-permute-start(bf16[2,256,256]{2,1,0:T(8,128)(2,1)S(1)} %collective-permute-done), channel_id=1, source_target_pairs={{0,4},{1,5},{2,6},{3,7},{4,0},{5,1},{6,2},{7,3},{8,12},{9,13},{10,... | collective-permute-start | bytes 786440 | tf_op jit(solution)/shard_map/ppermute | solution.py:146
  21.6 0.0 collective-permute-done.8
  21.6 0.0 collective-permute-start.11
  21.7 0.0 copy-done
  21.7 0.0 collective-permute-done.9
  21.8 1.4 %collective-permute-done.11 = bf16[2,256,256]{2,1,0:T(8,128)(2,1)S(1)} collective-permute-done((bf16[2,256,256]{2,1,0:T(8,128)(2,1)S(1)}, bf16[2,256,256]{2,1,0:T(8,128)(2,1)S(1)}, u32[]{:S(2)}, u32[]{:S(2)}) %collective-permute-start.11) | collective-permute-done | bytes 262176 | tf_op jit(solution)/shard_map/ppermute | solution.py:146
  23.2 1.6 %early_tiles.1.sum_ref = f32[9,256,256]{2,1,0:T(8,128)S(1)} custom-call(s32[3,4,72]{2,1,0:T(4,128)S(1)} %get-tuple-element.11.list_ref, bf16[16,256,256]{2,1,0:T(8,128)(2,1)S(1)} %constant_dynamic-update-slice_fusion.masked_ref, bf16[64,256,256]{2,1,0:T(8,128)(2,1)S(1)} %get-tuple-element.12.transfer_ref), custom_call_target="tpu_custom_call" | custom-call | flops 2147483648 | bytes 4194304 | tf_op jit(solution)/shard_map/early_tiles/pallas_call | solution.py:197
  24.8 3.6 %collective-permute-done.6 = bf16[2,256,256]{2,1,0:T(8,128)(2,1)S(1)} collective-permute-done((bf16[2,256,256]{2,1,0:T(8,128)(2,1)S(1)}, bf16[2,256,256]{2,1,0:T(8,128)(2,1)S(1)}, u32[]{:S(2)}, u32[]{:S(2)}) %collective-permute-start.6) | collective-permute-done | bytes 262176 | tf_op jit(solution)/shard_map/ppermute | solution.py:146
  28.4 0.6 collective-permute-start.13
  29.0 0.0 collective-permute-done.1
  29.0 1.8 %collective-permute-start.14 = (bf16[1,256,256]{2,1,0:T(8,128)(2,1)S(1)}, bf16[1,256,256]{2,1,0:T(8,128)(2,1)S(1)}, u32[]{:S(2)}, u32[]{:S(2)}) collective-permute-start(bf16[1,256,256]{2,1,0:T(8,128)(2,1)S(1)} %slice.112), channel_id=1, source_target_pairs={{0,4},{1,5},{2,6},{3,7},{4,0},{5,1},{6,2},{7,3},{8,12},{9,13},{10,... | collective-permute-start | bytes 393224 | tf_op jit(solution)/shard_map/ppermute | solution.py:146
  30.7 0.0 collective-permute-start.2
  30.7 0.1 iota_compare_fusion.1
  30.8 0.5 collective-permute-start.12
  31.3 0.0 collective-permute-done.4
  31.3 0.1 collective-permute-start.5
  31.4 2.0 %collective-permute-done.13 = bf16[1,256,256]{2,1,0:T(8,128)(2,1)S(1)} collective-permute-done((bf16[1,256,256]{2,1,0:T(8,128)(2,1)S(1)}, bf16[1,256,256]{2,1,0:T(8,128)(2,1)S(1)}, u32[]{:S(2)}, u32[]{:S(2)}) %collective-permute-start.13) | collective-permute-done | bytes 131104 | tf_op jit(solution)/shard_map/ppermute | solution.py:146
  33.4 0.6 collective-permute-done.14
  34.0 0.1 collective-permute-start.15
  34.1 0.0 collective-permute-done.2
  34.2 0.0 collective-permute-done.5
  34.2 0.0 collective-permute-done.12
  34.3 1.3 %collective-permute-done.15 = bf16[2,256,256]{2,1,0:T(8,128)(2,1)S(1)} collective-permute-done((bf16[2,256,256]{2,1,0:T(8,128)(2,1)S(1)}, bf16[2,256,256]{2,1,0:T(8,128)(2,1)S(1)}, u32[]{:S(2)}, u32[]{:S(2)}) %collective-permute-start.15) | collective-permute-done | bytes 262176 | tf_op jit(solution)/shard_map/ppermute | solution.py:146
  35.7 1.6 %late_tiles.2 = bf16[4,256,256]{2,1,0:T(8,128)(2,1)S(1)} custom-call(s32[3,4,72]{2,1,0:T(4,128)S(1)} %get-tuple-element.11.list_ref, bf16[16,256,256]{2,1,0:T(8,128)(2,1)S(1)} %constant_dynamic-update-slice_fusion.8.masked_ref, bf16[64,256,256]{2,1,0:T(8,128)(2,1)S(1)} %get-tuple-element.12.transfer_ref, f32[9,256,256]{2,1,0:T(8,128)S(1)} %early_tiles.1.sum_ref), custom_call_target="tpu_custom_call" | custom-call | flops 2147483648 | bytes 4194304 | tf_op jit(solution)/shard_map/late_tiles/pallas_call | solution.py:217
  37.3 1.0 %collective-permute-start.16 = (bf16[256,256]{1,0:T(8,128)(2,1)S(1)}, bf16[256,256]{1,0:T(8,128)(2,1)S(1)}, u32[]{:S(2)}, u32[]{:S(2)}) collective-permute-start(bf16[256,256]{1,0:T(8,128)(2,1)S(1)} %get-tuple-element.18), channel_id=1, source_target_pairs={{0,1},{1,0},{2,3},{3,2},{4,5},{5,4},{6,7},{7,6},{8,9},{9,8},{10,11... | collective-permute-start | bytes 393224 | tf_op jit(solution)/shard_map/ppermute | solution.py:146
  38.3 1.6 %collective-permute-start.18 = (bf16[256,256]{1,0:T(8,128)(2,1)S(1)}, bf16[256,256]{1,0:T(8,128)(2,1)S(1)}, u32[]{:S(2)}, u32[]{:S(2)}) collective-permute-start(bf16[256,256]{1,0:T(8,128)(2,1)S(1)} %get-tuple-element.16), channel_id=1, source_target_pairs={{0,3},{1,2},{2,1},{3,0},{4,7},{5,6},{6,5},{7,4},{8,11},{9,10},{10,... | collective-permute-start | bytes 393224 | tf_op jit(solution)/shard_map/ppermute | solution.py:146
  39.9 0.2 collective-permute-start.17
  40.0 0.0 collective-permute-done.16.refs_0_
  40.0 1.6 %late_tiles.3 = bf16[4,256,256]{2,1,0:T(8,128)(2,1)S(1)} custom-call(s32[3,4,72]{2,1,0:T(4,128)S(1)} %get-tuple-element.11.list_ref, bf16[16,256,256]{2,1,0:T(8,128)(2,1)S(1)} %constant_dynamic-update-slice_fusion.8.masked_ref, bf16[64,256,256]{2,1,0:T(8,128)(2,1)S(1)} %get-tuple-element.12.transfer_ref, f32[9,256,256]{2,1,0:T(8,128)S(1)} %early_tiles.1.sum_ref, ...), custom_call_target="tpu_custom_call" | custom-call | flops 2147483648 | bytes 4194304 | tf_op jit(solution)/shard_map/late_tiles/pallas_call | solution.py:217
  41.6 1.3 %collective-permute-start.22 = (bf16[256,256]{1,0:T(8,128)(2,1)S(1)}, bf16[256,256]{1,0:T(8,128)(2,1)S(1)}, u32[]{:S(2)}, u32[]{:S(2)}) collective-permute-start(bf16[256,256]{1,0:T(8,128)(2,1)S(1)} %get-tuple-element.20), channel_id=1, source_target_pairs={{0,3},{1,2},{2,1},{3,0},{4,7},{5,6},{6,5},{7,4},{8,11},{9,10},{10,... | collective-permute-start | bytes 393224 | tf_op jit(solution)/shard_map/ppermute | solution.py:146
  42.9 1.5 %collective-permute-start.21 = (bf16[256,256]{1,0:T(8,128)(2,1)S(1)}, bf16[256,256]{1,0:T(8,128)(2,1)S(1)}, u32[]{:S(2)}, u32[]{:S(2)}) collective-permute-start(bf16[256,256]{1,0:T(8,128)(2,1)S(1)} %get-tuple-element.21), channel_id=1, source_target_pairs={{0,2},{1,3},{2,0},{3,1},{4,6},{5,7},{6,4},{7,5},{8,10},{9,11},{10,... | collective-permute-start | bytes 393224 | tf_op jit(solution)/shard_map/ppermute | solution.py:146
  44.4 0.0 collective-permute-start.20
  44.5 0.0 collective-permute-done.18
  44.5 0.0 copy-start.2
  44.6 2.6 %collective-permute-done.17 = bf16[256,256]{1,0:T(8,128)(2,1)S(1)} collective-permute-done((bf16[256,256]{1,0:T(8,128)(2,1)S(1)}, bf16[256,256]{1,0:T(8,128)(2,1)S(1)}, u32[]{:S(2)}, u32[]{:S(2)}) %collective-permute-start.17) | collective-permute-done | bytes 131104 | tf_op jit(solution)/shard_map/ppermute | solution.py:146
  47.2 0.2 add_convert_fusion.1
  47.4 2.7 %collective-permute-start.19 = (bf16[2,256,256]{2,1,0:T(8,128)(2,1)S(1)}, bf16[2,256,256]{2,1,0:T(8,128)(2,1)S(1)}, u32[]{:S(2)}, u32[]{:S(2)}) collective-permute-start(bf16[2,256,256]{2,1,0:T(8,128)(2,1)S(1)} %add_convert_fusion.1), channel_id=1, source_target_pairs={{0,8},{1,9},{2,10},{3,11},{4,12},{5,13},{6,14},{7,15},{8,0},{9,1},... | collective-permute-start | bytes 786440 | tf_op jit(solution)/shard_map/ppermute | solution.py:149
  50.1 0.0 collective-permute-done.22
  50.1 2.5 %collective-permute-done.21 = bf16[256,256]{1,0:T(8,128)(2,1)S(1)} collective-permute-done((bf16[256,256]{1,0:T(8,128)(2,1)S(1)}, bf16[256,256]{1,0:T(8,128)(2,1)S(1)}, u32[]{:S(2)}, u32[]{:S(2)}) %collective-permute-start.21) | collective-permute-done | bytes 131104 | tf_op jit(solution)/shard_map/ppermute | solution.py:146
  52.6 0.0 collective-permute-done.20
  52.6 0.2 add_convert_fusion
  52.9 2.4 %collective-permute-start.23 = (bf16[2,256,256]{2,1,0:T(8,128)(2,1)S(1)}, bf16[2,256,256]{2,1,0:T(8,128)(2,1)S(1)}, u32[]{:S(2)}, u32[]{:S(2)}) collective-permute-start(bf16[2,256,256]{2,1,0:T(8,128)(2,1)S(1)} %add_convert_fusion), channel_id=1, source_target_pairs={{0,4},{1,5},{2,6},{3,7},{4,8},{5,9},{6,10},{7,11},{8,12},{9,13},{1... | collective-permute-start | bytes 786440 | tf_op jit(solution)/shard_map/ppermute | solution.py:149
  55.3 0.1 iota_compare_fusion.3
  55.3 1.3 %base.1 = f32[2,256,256]{2,1,0:T(8,128)S(1)} custom-call(s32[2]{0:T(128)} %size_ref.3, f32[2,256]{1,0:T(2,128)} %energy_ref.1, bf16[2,256,256]{2,1,0:T(8,128)(2,1)} %integral_ref.1, bf16[2,256,256]{2,1,0:T(8,128)(2,1)} %copy-done), custom_call_target="tpu_custom_call" | custom-call | tf_op jit(solution)/shard_map/base/pallas_call | solution.py:252
  56.6 10.9 %collective-permute-done.19 = bf16[2,256,256]{2,1,0:T(8,128)(2,1)S(1)} collective-permute-done((bf16[2,256,256]{2,1,0:T(8,128)(2,1)S(1)}, bf16[2,256,256]{2,1,0:T(8,128)(2,1)S(1)}, u32[]{:S(2)}, u32[]{:S(2)}) %collective-permute-start.19) | collective-permute-done | bytes 262176 | tf_op jit(solution)/shard_map/ppermute | solution.py:149
  67.5 0.0 collective-permute-done.23
  67.5 1.1 %add_select_fusion = f32[2,256,256]{2,1,0:T(8,128)} fusion(bf16[2,256,256]{2,1,0:T(8,128)(2,1)S(1)} %collective-permute-done.23, bf16[2,256,256]{2,1,0:T(8,128)(2,1)S(1)} %collective-permute-done.19, f32[2,256,256]{2,1,0:T(8,128)S(1)} %base.1, f32[256,256]{1,0:T(8,128)S(1)} %convert_element_type.50, f32[256,256]{1,0:T(8,128)S(1)} %convert_element_type.49, ...), kind=kLoop, calls=%fused_computation | loop fusion | flops 1835008 | bytes 2621960 | tf_op jit(solution)/shard_map/jit(_where)/select_n | solution.py:263
  (35 shorter events, 0.6 us)
Async XLA Ops:
  1.0 20.6 %copy-start = (bf16[2,256,256]{2,1,0:T(8,128)(2,1)}, bf16[2,256,256]{2,1,0:T(8,128)(2,1)S(1)}, u32[]{:S(2)}) copy-start(bf16[2,256,256]{2,1,0:T(8,128)(2,1)S(1)} %mask.1.masked_ref) | copy-start | bytes 786436
  1.1 12.5 %collective-permute-start = (bf16[2,256,256]{2,1,0:T(8,128)(2,1)S(1)}, bf16[2,256,256]{2,1,0:T(8,128)(2,1)S(1)}, u32[]{:S(2)}, u32[]{:S(2)}) collective-permute-start(bf16[2,256,256]{2,1,0:T(8,128)(2,1)S(1)} %mask.1.masked_ref), channel_id=1, source_target_pairs={{0,12},{1,13},{2,14},{3,15},{4,8},{5,9},{6,10},{7,11},{8,4},{9,5},... | collective-permute-start | bytes 786440 | tf_op jit(solution)/shard_map/ppermute | solution.py:146
  6.2 12.0 %collective-permute-start.3 = (bf16[2,256,256]{2,1,0:T(8,128)(2,1)S(1)}, bf16[2,256,256]{2,1,0:T(8,128)(2,1)S(1)}, u32[]{:S(2)}, u32[]{:S(2)}) collective-permute-start(bf16[2,256,256]{2,1,0:T(8,128)(2,1)S(1)} %mask.1.masked_ref), channel_id=1, source_target_pairs={{0,4},{1,5},{2,6},{3,7},{4,0},{5,1},{6,2},{7,3},{8,12},{9,13},{10,... | collective-permute-start | bytes 786440 | tf_op jit(solution)/shard_map/ppermute | solution.py:146
  6.2 15.5 %collective-permute-start.9 = (bf16[2,256,256]{2,1,0:T(8,128)(2,1)S(1)}, bf16[2,256,256]{2,1,0:T(8,128)(2,1)S(1)}, u32[]{:S(2)}, u32[]{:S(2)}) collective-permute-start(bf16[2,256,256]{2,1,0:T(8,128)(2,1)S(1)} %mask.1.masked_ref), channel_id=1, source_target_pairs={{0,1},{1,0},{2,3},{3,2},{4,5},{5,4},{6,7},{7,6},{8,9},{9,8},{10,11... | collective-permute-start | bytes 786440 | tf_op jit(solution)/shard_map/ppermute | solution.py:146
  6.2 13.7 %collective-permute-start.10 = (bf16[2,256,256]{2,1,0:T(8,128)(2,1)S(1)}, bf16[2,256,256]{2,1,0:T(8,128)(2,1)S(1)}, u32[]{:S(2)}, u32[]{:S(2)}) collective-permute-start(bf16[2,256,256]{2,1,0:T(8,128)(2,1)S(1)} %mask.1.masked_ref), channel_id=1, source_target_pairs={{0,2},{1,3},{2,0},{3,1},{4,6},{5,7},{6,4},{7,5},{8,10},{9,11},{10,... | collective-permute-start | bytes 786440 | tf_op jit(solution)/shard_map/ppermute | solution.py:146
  7.7 0.7 copy-start.1
  13.5 4.7 %collective-permute-start.7 = (bf16[2,256,256]{2,1,0:T(8,128)(2,1)S(1)}, bf16[2,256,256]{2,1,0:T(8,128)(2,1)S(1)}, u32[]{:S(2)}, u32[]{:S(2)}) collective-permute-start(bf16[2,256,256]{2,1,0:T(8,128)(2,1)S(1)} %collective-permute-done), channel_id=1, source_target_pairs={{0,1},{1,0},{2,3},{3,2},{4,5},{5,4},{6,7},{7,6},{8,9},{9,8},{10,11... | collective-permute-start | bytes 786440 | tf_op jit(solution)/shard_map/ppermute | solution.py:146
  13.8 15.2 %collective-permute-start.1 = (bf16[2,256,256]{2,1,0:T(8,128)(2,1)S(1)}, bf16[2,256,256]{2,1,0:T(8,128)(2,1)S(1)}, u32[]{:S(2)}, u32[]{:S(2)}) collective-permute-start(bf16[2,256,256]{2,1,0:T(8,128)(2,1)S(1)} %collective-permute-done), channel_id=1, source_target_pairs={{0,2},{1,3},{2,0},{3,1},{4,6},{5,7},{6,4},{7,5},{8,10},{9,11},{10,... | collective-permute-start | bytes 786440 | tf_op jit(solution)/shard_map/ppermute | solution.py:146
  18.2 3.4 %collective-permute-start.8 = (bf16[2,256,256]{2,1,0:T(8,128)(2,1)S(1)}, bf16[2,256,256]{2,1,0:T(8,128)(2,1)S(1)}, u32[]{:S(2)}, u32[]{:S(2)}) collective-permute-start(bf16[2,256,256]{2,1,0:T(8,128)(2,1)S(1)} %collective-permute-done.3), channel_id=1, source_target_pairs={{0,1},{1,0},{2,3},{3,2},{4,5},{5,4},{6,7},{7,6},{8,9},{9,8},{10,11... | collective-permute-start | bytes 786440 | tf_op jit(solution)/shard_map/ppermute | solution.py:146
  18.2 13.1 %collective-permute-start.4 = (bf16[2,256,256]{2,1,0:T(8,128)(2,1)S(1)}, bf16[2,256,256]{2,1,0:T(8,128)(2,1)S(1)}, u32[]{:S(2)}, u32[]{:S(2)}) collective-permute-start(bf16[2,256,256]{2,1,0:T(8,128)(2,1)S(1)} %collective-permute-done.3), channel_id=1, source_target_pairs={{0,2},{1,3},{2,0},{3,1},{4,6},{5,7},{6,4},{7,5},{8,10},{9,11},{10,... | collective-permute-start | bytes 786440 | tf_op jit(solution)/shard_map/ppermute | solution.py:146
  19.9 8.5 %collective-permute-start.6 = (bf16[2,256,256]{2,1,0:T(8,128)(2,1)S(1)}, bf16[2,256,256]{2,1,0:T(8,128)(2,1)S(1)}, u32[]{:S(2)}, u32[]{:S(2)}) collective-permute-start(bf16[2,256,256]{2,1,0:T(8,128)(2,1)S(1)} %collective-permute-done), channel_id=1, source_target_pairs={{0,4},{1,5},{2,6},{3,7},{4,0},{5,1},{6,2},{7,3},{8,12},{9,13},{10,... | collective-permute-start | bytes 786440 | tf_op jit(solution)/shard_map/ppermute | solution.py:146
  21.6 1.5 %collective-permute-start.11 = (bf16[2,256,256]{2,1,0:T(8,128)(2,1)S(1)}, bf16[2,256,256]{2,1,0:T(8,128)(2,1)S(1)}, u32[]{:S(2)}, u32[]{:S(2)}) collective-permute-start(bf16[2,256,256]{2,1,0:T(8,128)(2,1)S(1)} %collective-permute-done.10), channel_id=1, source_target_pairs={{0,1},{1,0},{2,3},{3,2},{4,5},{5,4},{6,7},{7,6},{8,9},{9,8},{10,11... | collective-permute-start | bytes 786440 | tf_op jit(solution)/shard_map/ppermute | solution.py:146
  28.4 5.0 %collective-permute-start.13 = (bf16[1,256,256]{2,1,0:T(8,128)(2,1)S(1)}, bf16[1,256,256]{2,1,0:T(8,128)(2,1)S(1)}, u32[]{:S(2)}, u32[]{:S(2)}) collective-permute-start(bf16[1,256,256]{2,1,0:T(8,128)(2,1)S(1)} %slice.89), channel_id=1, source_target_pairs={{0,2},{1,3},{2,0},{3,1},{4,6},{5,7},{6,4},{7,5},{8,10},{9,11},{10,... | collective-permute-start | bytes 393224 | tf_op jit(solution)/shard_map/ppermute | solution.py:146
  29.0 5.0 %collective-permute-start.14 = (bf16[1,256,256]{2,1,0:T(8,128)(2,1)S(1)}, bf16[1,256,256]{2,1,0:T(8,128)(2,1)S(1)}, u32[]{:S(2)}, u32[]{:S(2)}) collective-permute-start(bf16[1,256,256]{2,1,0:T(8,128)(2,1)S(1)} %slice.112), channel_id=1, source_target_pairs={{0,4},{1,5},{2,6},{3,7},{4,0},{5,1},{6,2},{7,3},{8,12},{9,13},{10,... | collective-permute-start | bytes 393224 | tf_op jit(solution)/shard_map/ppermute | solution.py:146
  30.7 3.4 %collective-permute-start.2 = (bf16[2,256,256]{2,1,0:T(8,128)(2,1)S(1)}, bf16[2,256,256]{2,1,0:T(8,128)(2,1)S(1)}, u32[]{:S(2)}, u32[]{:S(2)}) collective-permute-start(bf16[2,256,256]{2,1,0:T(8,128)(2,1)S(1)} %collective-permute-done.1), channel_id=1, source_target_pairs={{0,1},{1,0},{2,3},{3,2},{4,5},{5,4},{6,7},{7,6},{8,9},{9,8},{10,11... | collective-permute-start | bytes 786440 | tf_op jit(solution)/shard_map/ppermute | solution.py:146
  30.8 3.4 %collective-permute-start.12 = (bf16[2,256,256]{2,1,0:T(8,128)(2,1)S(1)}, bf16[2,256,256]{2,1,0:T(8,128)(2,1)S(1)}, u32[]{:S(2)}, u32[]{:S(2)}) collective-permute-start(bf16[2,256,256]{2,1,0:T(8,128)(2,1)S(1)} %collective-permute-done.6), channel_id=1, source_target_pairs={{0,1},{1,0},{2,3},{3,2},{4,5},{5,4},{6,7},{7,6},{8,9},{9,8},{10,11... | collective-permute-start | bytes 786440 | tf_op jit(solution)/shard_map/ppermute | solution.py:146
  31.3 2.9 %collective-permute-start.5 = (bf16[2,256,256]{2,1,0:T(8,128)(2,1)S(1)}, bf16[2,256,256]{2,1,0:T(8,128)(2,1)S(1)}, u32[]{:S(2)}, u32[]{:S(2)}) collective-permute-start(bf16[2,256,256]{2,1,0:T(8,128)(2,1)S(1)} %collective-permute-done.4), channel_id=1, source_target_pairs={{0,1},{1,0},{2,3},{3,2},{4,5},{5,4},{6,7},{7,6},{8,9},{9,8},{10,11... | collective-permute-start | bytes 786440 | tf_op jit(solution)/shard_map/ppermute | solution.py:146
  34.0 1.6 %collective-permute-start.15 = (bf16[2,256,256]{2,1,0:T(8,128)(2,1)S(1)}, bf16[2,256,256]{2,1,0:T(8,128)(2,1)S(1)}, u32[]{:S(2)}, u32[]{:S(2)}) collective-permute-start(bf16[2,256,256]{2,1,0:T(8,128)(2,1)S(1)} %pad_maximum_fusion), channel_id=1, source_target_pairs={{0,1},{1,0},{2,3},{3,2},{4,5},{5,4},{6,7},{7,6},{8,9},{9,8},{10,11... | collective-permute-start | bytes 786440 | tf_op jit(solution)/shard_map/ppermute | solution.py:146
  37.3 2.7 %collective-permute-start.16 = (bf16[256,256]{1,0:T(8,128)(2,1)S(1)}, bf16[256,256]{1,0:T(8,128)(2,1)S(1)}, u32[]{:S(2)}, u32[]{:S(2)}) collective-permute-start(bf16[256,256]{1,0:T(8,128)(2,1)S(1)} %get-tuple-element.18), channel_id=1, source_target_pairs={{0,1},{1,0},{2,3},{3,2},{4,5},{5,4},{6,7},{7,6},{8,9},{9,8},{10,11... | collective-permute-start | bytes 393224 | tf_op jit(solution)/shard_map/ppermute | solution.py:146
  38.3 6.2 %collective-permute-start.18 = (bf16[256,256]{1,0:T(8,128)(2,1)S(1)}, bf16[256,256]{1,0:T(8,128)(2,1)S(1)}, u32[]{:S(2)}, u32[]{:S(2)}) collective-permute-start(bf16[256,256]{1,0:T(8,128)(2,1)S(1)} %get-tuple-element.16), channel_id=1, source_target_pairs={{0,3},{1,2},{2,1},{3,0},{4,7},{5,6},{6,5},{7,4},{8,11},{9,10},{10,... | collective-permute-start | bytes 393224 | tf_op jit(solution)/shard_map/ppermute | solution.py:146
  39.9 7.3 %collective-permute-start.17 = (bf16[256,256]{1,0:T(8,128)(2,1)S(1)}, bf16[256,256]{1,0:T(8,128)(2,1)S(1)}, u32[]{:S(2)}, u32[]{:S(2)}) collective-permute-start(bf16[256,256]{1,0:T(8,128)(2,1)S(1)} %get-tuple-element.17), channel_id=1, source_target_pairs={{0,2},{1,3},{2,0},{3,1},{4,6},{5,7},{6,4},{7,5},{8,10},{9,11},{10,... | collective-permute-start | bytes 393224 | tf_op jit(solution)/shard_map/ppermute | solution.py:146
  41.6 8.4 %collective-permute-start.22 = (bf16[256,256]{1,0:T(8,128)(2,1)S(1)}, bf16[256,256]{1,0:T(8,128)(2,1)S(1)}, u32[]{:S(2)}, u32[]{:S(2)}) collective-permute-start(bf16[256,256]{1,0:T(8,128)(2,1)S(1)} %get-tuple-element.20), channel_id=1, source_target_pairs={{0,3},{1,2},{2,1},{3,0},{4,7},{5,6},{6,5},{7,4},{8,11},{9,10},{10,... | collective-permute-start | bytes 393224 | tf_op jit(solution)/shard_map/ppermute | solution.py:146
  42.9 9.7 %collective-permute-start.21 = (bf16[256,256]{1,0:T(8,128)(2,1)S(1)}, bf16[256,256]{1,0:T(8,128)(2,1)S(1)}, u32[]{:S(2)}, u32[]{:S(2)}) collective-permute-start(bf16[256,256]{1,0:T(8,128)(2,1)S(1)} %get-tuple-element.21), channel_id=1, source_target_pairs={{0,2},{1,3},{2,0},{3,1},{4,6},{5,7},{6,4},{7,5},{8,10},{9,11},{10,... | collective-permute-start | bytes 393224 | tf_op jit(solution)/shard_map/ppermute | solution.py:146
  44.4 8.2 %collective-permute-start.20 = (bf16[256,256]{1,0:T(8,128)(2,1)S(1)}, bf16[256,256]{1,0:T(8,128)(2,1)S(1)}, u32[]{:S(2)}, u32[]{:S(2)}) collective-permute-start(bf16[256,256]{1,0:T(8,128)(2,1)S(1)} %get-tuple-element.22), channel_id=1, source_target_pairs={{0,1},{1,0},{2,3},{3,2},{4,5},{5,4},{6,7},{7,6},{8,9},{9,8},{10,11... | collective-permute-start | bytes 393224 | tf_op jit(solution)/shard_map/ppermute | solution.py:146
  44.5 10.7 %copy-start.2 = (s32[2]{0:T(128)S(1)}, s32[2]{0:T(128)}, u32[]{:S(2)}) copy-start(s32[2]{0:T(128)} %size_ref.3) | copy-start | bytes 28
  47.4 20.1 %collective-permute-start.19 = (bf16[2,256,256]{2,1,0:T(8,128)(2,1)S(1)}, bf16[2,256,256]{2,1,0:T(8,128)(2,1)S(1)}, u32[]{:S(2)}, u32[]{:S(2)}) collective-permute-start(bf16[2,256,256]{2,1,0:T(8,128)(2,1)S(1)} %add_convert_fusion.1), channel_id=1, source_target_pairs={{0,8},{1,9},{2,10},{3,11},{4,12},{5,13},{6,14},{7,15},{8,0},{9,1},... | collective-permute-start | bytes 786440 | tf_op jit(solution)/shard_map/ppermute | solution.py:149
  52.9 14.7 %collective-permute-start.23 = (bf16[2,256,256]{2,1,0:T(8,128)(2,1)S(1)}, bf16[2,256,256]{2,1,0:T(8,128)(2,1)S(1)}, u32[]{:S(2)}, u32[]{:S(2)}) collective-permute-start(bf16[2,256,256]{2,1,0:T(8,128)(2,1)S(1)} %add_convert_fusion), channel_id=1, source_target_pairs={{0,4},{1,5},{2,6},{3,7},{4,8},{5,9},{6,10},{7,11},{8,12},{9,13},{1... | collective-permute-start | bytes 786440 | tf_op jit(solution)/shard_map/ppermute | solution.py:149

commit v4 on v3

--- a/solution.py
+++ b/solution.py
@@ -8,7 +8,7 @@
 from jax.sharding import PartitionSpec as P
 
 GROUP = 4
-UNROLL = 8
+UNROLL = 10
 
 VMEM = functools.partial(pl.BlockSpec, memory_space=pltpu.VMEM)
 SMEM = functools.partial(pl.BlockSpec, memory_space=pltpu.SMEM)

time: 68.8 us -> 69.1 us (level)
  starting transfers between devices: 25.3 us -> 23.9 us
  Pallas kernels: 12.1 us -> 13.5 us
    ppermute x2, starting transfers between devices: 5.08 us -> 2.81 us  [ahead(): lax.ppermute(value, 'col', [(i, (i + steps * GROUP) % columns) for i in r...]
    ppermute x2, waiting for transfers between devices: 10.9 us -> 12.2 us  [ahead(): lax.ppermute(value, 'col', [(i, (i + steps * GROUP) % columns) for i in r...]
    pallas_call x1, Pallas kernels: 1.6 us -> 2.75 us  [shards(): pl.pallas_call(early_kernel, out_shape=jax.ShapeDtypeStruct((columns // 2...]
    ppermute x22, waiting for transfers between devices: 17 us -> 16 us  [swap(): return lax.ppermute(value, 'col', [(i, i ^ m) for i in range(columns)])]
    ppermute x22, starting transfers between devices: 20.2 us -> 21.1 us  [swap(): return lax.ppermute(value, 'col', [(i, i ^ m) for i in range(columns)])]
  transfers between devices with their start and end apart: 24 -> 24, of which waited for: 9 -> 9; matrix products, arithmetic and copies ran while one was open for 2% -> 2% of each run, Pallas kernels for 14% -> 16%
where the time goes in v4:
time: 69.1 us; the launch traced here: 69 us
  waiting for transfers between devices  28.1 us (41%)
  starting transfers between devices  23.9 us (35%)
  Pallas kernels  13.5 us (20%)
  other arithmetic  1.99 us (3%)
  local copies, waits for them, and re-layouts  1.02 us (1%)
    ppermute x22, starting transfers between devices, swap(): return lax.ppermute(value, 'col', [(i, i ^ m) for i in range(columns)])  21.1 us
    ppermute x22, waiting for transfers between devices, swap(): return lax.ppermute(value, 'col', [(i, i ^ m) for i in range(columns)])  16 us
    ppermute x2, waiting for transfers between devices, ahead(): lax.ppermute(value, 'col', [(i, (i + steps * GROUP) % columns) for i in r...  12.2 us
    pallas_call x1, Pallas kernels, shards(): pl.pallas_call(functools.partial(list_kernel, columns, len(places) * pair...  5.06 us
    pallas_call x2, Pallas kernels, sums_of(): pl.pallas_call(functools.partial(late_kernel, part), out_shape=jax.ShapeD...  3.43 us
    ppermute x2, starting transfers between devices, ahead(): lax.ppermute(value, 'col', [(i, (i + steps * GROUP) % columns) for i in r...  2.81 us
    pallas_call x1, Pallas kernels, shards(): pl.pallas_call(early_kernel, out_shape=jax.ShapeDtypeStruct((columns // 2...  2.75 us
  transfers between devices with their start and end apart: 24, of which 9 were waited for; matrix products, arithmetic and copies ran while one was open for 2% of the time, Pallas kernels for 16%

profile of v4, /device:TPU:0, one launch (start us, length us, event | category | flops | bytes accessed | tf_op | source)
XLA Modules:
  0.0 69.0 jit_solution(11109989137904285436)
XLA Ops:
  0.0 1.0 %mask.1.masked_ref = bf16[2,256,256]{2,1,0:T(8,128)(2,1)S(1)} custom-call(s32[2]{0:T(128)} %size_ref.3, bf16[2,256,256]{2,1,0:T(8,128)(2,1)} %amplitude_ref.1), custom_call_target="tpu_custom_call" | custom-call | tf_op jit(solution)/shard_map/mask/pallas_call | solution.py:153
  1.0 0.0 copy-start
  1.1 5.1 %collective-permute-start = (bf16[2,256,256]{2,1,0:T(8,128)(2,1)S(1)}, bf16[2,256,256]{2,1,0:T(8,128)(2,1)S(1)}, u32[]{:S(2)}, u32[]{:S(2)}) collective-permute-start(bf16[2,256,256]{2,1,0:T(8,128)(2,1)S(1)} %mask.1.masked_ref), channel_id=1, source_target_pairs={{0,12},{1,13},{2,14},{3,15},{4,8},{5,9},{6,10},{7,11},{8,4},{9,5},... | collective-permute-start | bytes 786440 | tf_op jit(solution)/shard_map/ppermute | solution.py:146
  6.2 0.0 collective-permute-start.3
  6.2 0.0 collective-permute-start.9
  6.2 1.5 %collective-permute-start.10 = (bf16[2,256,256]{2,1,0:T(8,128)(2,1)S(1)}, bf16[2,256,256]{2,1,0:T(8,128)(2,1)S(1)}, u32[]{:S(2)}, u32[]{:S(2)}) collective-permute-start(bf16[2,256,256]{2,1,0:T(8,128)(2,1)S(1)} %mask.1.masked_ref), channel_id=1, source_target_pairs={{0,2},{1,3},{2,0},{3,1},{4,6},{5,7},{6,4},{7,5},{8,10},{9,11},{10,... | collective-permute-start | bytes 786440 | tf_op jit(solution)/shard_map/ppermute | solution.py:146
  7.7 0.7 copy-done.1
  8.4 5.1 %tile_list.1 = (s32[3,4,74]{2,1,0:T(4,128)S(1)}, s32[3,4]{1,0:T(4,128)S(1)}, bf16[64,256,256]{2,1,0:T(8,128)(2,1)S(1)}) custom-call(s32[1]{0:T(128)} %bitcast.me_ref, s32[16]{0:T(128)S(1)} %copy-done.1, s32[64]{0:T(128)} %source_ref.1, s32[64]{0:T(128)} %owner_ref.1, s32[16,16]{1,0:T(8,128)} %dispatch_ref.1, s32[16,16]{1,0:T(8,128)} %result_ref.1, ...), custom_call_target="tpu_custom_call" | custom-call | tf_op jit(solution)/shard_map/tile_list/pallas_call | solution.py:180
  13.4 0.1 iota_compare_fusion
  13.5 0.0 collective-permute-done
  13.5 0.2 collective-permute-start.7
  13.8 1.4 %collective-permute-start.1 = (bf16[2,256,256]{2,1,0:T(8,128)(2,1)S(1)}, bf16[2,256,256]{2,1,0:T(8,128)(2,1)S(1)}, u32[]{:S(2)}, u32[]{:S(2)}) collective-permute-start(bf16[2,256,256]{2,1,0:T(8,128)(2,1)S(1)} %collective-permute-done), channel_id=1, source_target_pairs={{0,2},{1,3},{2,0},{3,1},{4,6},{5,7},{6,4},{7,5},{8,10},{9,11},{10,... | collective-permute-start | bytes 786440 | tf_op jit(solution)/shard_map/ppermute | solution.py:146
  15.2 3.0 %collective-permute-done.3 = bf16[2,256,256]{2,1,0:T(8,128)(2,1)S(1)} collective-permute-done((bf16[2,256,256]{2,1,0:T(8,128)(2,1)S(1)}, bf16[2,256,256]{2,1,0:T(8,128)(2,1)S(1)}, u32[]{:S(2)}, u32[]{:S(2)}) %collective-permute-start.3) | collective-permute-done | bytes 262176 | tf_op jit(solution)/shard_map/ppermute | solution.py:146
  18.2 0.0 collective-permute-start.8
  18.2 0.0 collective-permute-done.7
  18.2 1.6 %collective-permute-start.4 = (bf16[2,256,256]{2,1,0:T(8,128)(2,1)S(1)}, bf16[2,256,256]{2,1,0:T(8,128)(2,1)S(1)}, u32[]{:S(2)}, u32[]{:S(2)}) collective-permute-start(bf16[2,256,256]{2,1,0:T(8,128)(2,1)S(1)} %collective-permute-done.3), channel_id=1, source_target_pairs={{0,2},{1,3},{2,0},{3,1},{4,6},{5,7},{6,4},{7,5},{8,10},{9,11},{10,... | collective-permute-start | bytes 786440 | tf_op jit(solution)/shard_map/ppermute | solution.py:146
  19.9 0.0 collective-permute-done.10
  19.9 1.7 %collective-permute-start.6 = (bf16[2,256,256]{2,1,0:T(8,128)(2,1)S(1)}, bf16[2,256,256]{2,1,0:T(8,128)(2,1)S(1)}, u32[]{:S(2)}, u32[]{:S(2)}) collective-permute-start(bf16[2,256,256]{2,1,0:T(8,128)(2,1)S(1)} %collective-permute-done), channel_id=1, source_target_pairs={{0,4},{1,5},{2,6},{3,7},{4,0},{5,1},{6,2},{7,3},{8,12},{9,13},{10,... | collective-permute-start | bytes 786440 | tf_op jit(solution)/shard_map/ppermute | solution.py:146
  21.6 0.0 collective-permute-done.8
  21.6 0.0 collective-permute-start.11
  21.7 0.0 copy-done
  21.7 0.0 collective-permute-done.9
  21.8 1.4 %collective-permute-done.11 = bf16[2,256,256]{2,1,0:T(8,128)(2,1)S(1)} collective-permute-done((bf16[2,256,256]{2,1,0:T(8,128)(2,1)S(1)}, bf16[2,256,256]{2,1,0:T(8,128)(2,1)S(1)}, u32[]{:S(2)}, u32[]{:S(2)}) %collective-permute-start.11) | collective-permute-done | bytes 262176 | tf_op jit(solution)/shard_map/ppermute | solution.py:146
  23.2 2.8 %early_tiles.1.sum_ref = f32[9,256,256]{2,1,0:T(8,128)S(1)} custom-call(s32[3,4,74]{2,1,0:T(4,128)S(1)} %get-tuple-element.11.list_ref, bf16[16,256,256]{2,1,0:T(8,128)(2,1)S(1)} %constant_dynamic-update-slice_fusion.masked_ref, bf16[64,256,256]{2,1,0:T(8,128)(2,1)S(1)} %get-tuple-element.12.transfer_ref), custom_call_target="tpu_custom_call" | custom-call | flops 2147483648 | bytes 4194304 | tf_op jit(solution)/shard_map/early_tiles/pallas_call | solution.py:197
  25.9 2.4 %collective-permute-done.6 = bf16[2,256,256]{2,1,0:T(8,128)(2,1)S(1)} collective-permute-done((bf16[2,256,256]{2,1,0:T(8,128)(2,1)S(1)}, bf16[2,256,256]{2,1,0:T(8,128)(2,1)S(1)}, u32[]{:S(2)}, u32[]{:S(2)}) %collective-permute-start.6) | collective-permute-done | bytes 262176 | tf_op jit(solution)/shard_map/ppermute | solution.py:146
  28.4 0.6 collective-permute-start.13
  29.0 0.0 collective-permute-done.1
  29.0 1.8 %collective-permute-start.14 = (bf16[1,256,256]{2,1,0:T(8,128)(2,1)S(1)}, bf16[1,256,256]{2,1,0:T(8,128)(2,1)S(1)}, u32[]{:S(2)}, u32[]{:S(2)}) collective-permute-start(bf16[1,256,256]{2,1,0:T(8,128)(2,1)S(1)} %slice.112), channel_id=1, source_target_pairs={{0,4},{1,5},{2,6},{3,7},{4,0},{5,1},{6,2},{7,3},{8,12},{9,13},{10,... | collective-permute-start | bytes 393224 | tf_op jit(solution)/shard_map/ppermute | solution.py:146
  30.7 0.0 collective-permute-start.2
  30.7 0.1 iota_compare_fusion.1
  30.8 0.5 collective-permute-start.12
  31.3 0.0 collective-permute-done.4
  31.3 0.1 collective-permute-start.5
  31.4 2.0 %collective-permute-done.13 = bf16[1,256,256]{2,1,0:T(8,128)(2,1)S(1)} collective-permute-done((bf16[1,256,256]{2,1,0:T(8,128)(2,1)S(1)}, bf16[1,256,256]{2,1,0:T(8,128)(2,1)S(1)}, u32[]{:S(2)}, u32[]{:S(2)}) %collective-permute-start.13) | collective-permute-done | bytes 131104 | tf_op jit(solution)/shard_map/ppermute | solution.py:146
  33.4 0.6 collective-permute-done.14
  34.0 0.1 collective-permute-start.15
  34.1 0.0 collective-permute-done.2
  34.2 0.0 collective-permute-done.5
  34.2 0.0 collective-permute-done.12
  34.3 1.3 %collective-permute-done.15 = bf16[2,256,256]{2,1,0:T(8,128)(2,1)S(1)} collective-permute-done((bf16[2,256,256]{2,1,0:T(8,128)(2,1)S(1)}, bf16[2,256,256]{2,1,0:T(8,128)(2,1)S(1)}, u32[]{:S(2)}, u32[]{:S(2)}) %collective-permute-start.15) | collective-permute-done | bytes 262176 | tf_op jit(solution)/shard_map/ppermute | solution.py:146
  35.7 1.7 %late_tiles.2 = bf16[4,256,256]{2,1,0:T(8,128)(2,1)S(1)} custom-call(s32[3,4,74]{2,1,0:T(4,128)S(1)} %get-tuple-element.11.list_ref, bf16[16,256,256]{2,1,0:T(8,128)(2,1)S(1)} %constant_dynamic-update-slice_fusion.8.masked_ref, bf16[64,256,256]{2,1,0:T(8,128)(2,1)S(1)} %get-tuple-element.12.transfer_ref, f32[9,256,256]{2,1,0:T(8,128)S(1)} %early_tiles.1.sum_ref), custom_call_target="tpu_custom_call" | custom-call | flops 2147483648 | bytes 4194304 | tf_op jit(solution)/shard_map/late_tiles/pallas_call | solution.py:217
  37.4 1.2 %collective-permute-start.16 = (bf16[256,256]{1,0:T(8,128)(2,1)S(1)}, bf16[256,256]{1,0:T(8,128)(2,1)S(1)}, u32[]{:S(2)}, u32[]{:S(2)}) collective-permute-start(bf16[256,256]{1,0:T(8,128)(2,1)S(1)} %get-tuple-element.18), channel_id=1, source_target_pairs={{0,1},{1,0},{2,3},{3,2},{4,5},{5,4},{6,7},{7,6},{8,9},{9,8},{10,11... | collective-permute-start | bytes 393224 | tf_op jit(solution)/shard_map/ppermute | solution.py:146
  38.6 2.2 %collective-permute-start.18 = (bf16[256,256]{1,0:T(8,128)(2,1)S(1)}, bf16[256,256]{1,0:T(8,128)(2,1)S(1)}, u32[]{:S(2)}, u32[]{:S(2)}) collective-permute-start(bf16[256,256]{1,0:T(8,128)(2,1)S(1)} %get-tuple-element.16), channel_id=1, source_target_pairs={{0,3},{1,2},{2,1},{3,0},{4,7},{5,6},{6,5},{7,4},{8,11},{9,10},{10,... | collective-permute-start | bytes 393224 | tf_op jit(solution)/shard_map/ppermute | solution.py:146
  40.8 0.5 collective-permute-start.17
  41.2 0.0 collective-permute-done.16.refs_0_
  41.2 1.7 %late_tiles.3 = bf16[4,256,256]{2,1,0:T(8,128)(2,1)S(1)} custom-call(s32[3,4,74]{2,1,0:T(4,128)S(1)} %get-tuple-element.11.list_ref, bf16[16,256,256]{2,1,0:T(8,128)(2,1)S(1)} %constant_dynamic-update-slice_fusion.8.masked_ref, bf16[64,256,256]{2,1,0:T(8,128)(2,1)S(1)} %get-tuple-element.12.transfer_ref, f32[9,256,256]{2,1,0:T(8,128)S(1)} %early_tiles.1.sum_ref, ...), custom_call_target="tpu_custom_call" | custom-call | flops 2147483648 | bytes 4194304 | tf_op jit(solution)/shard_map/late_tiles/pallas_call | solution.py:217
  43.0 2.4 %collective-permute-start.22 = (bf16[256,256]{1,0:T(8,128)(2,1)S(1)}, bf16[256,256]{1,0:T(8,128)(2,1)S(1)}, u32[]{:S(2)}, u32[]{:S(2)}) collective-permute-start(bf16[256,256]{1,0:T(8,128)(2,1)S(1)} %get-tuple-element.20), channel_id=1, source_target_pairs={{0,3},{1,2},{2,1},{3,0},{4,7},{5,6},{6,5},{7,4},{8,11},{9,10},{10,... | collective-permute-start | bytes 393224 | tf_op jit(solution)/shard_map/ppermute | solution.py:146
  45.4 0.3 collective-permute-start.21
  45.7 0.0 collective-permute-start.20
  45.7 0.0 collective-permute-done.18
  45.8 0.0 copy-start.2
  45.8 2.5 %collective-permute-done.17 = bf16[256,256]{1,0:T(8,128)(2,1)S(1)} collective-permute-done((bf16[256,256]{1,0:T(8,128)(2,1)S(1)}, bf16[256,256]{1,0:T(8,128)(2,1)S(1)}, u32[]{:S(2)}, u32[]{:S(2)}) %collective-permute-start.17) | collective-permute-done | bytes 131104 | tf_op jit(solution)/shard_map/ppermute | solution.py:146
  48.3 0.2 add_convert_fusion.1
  48.5 2.0 %collective-permute-start.19 = (bf16[2,256,256]{2,1,0:T(8,128)(2,1)S(1)}, bf16[2,256,256]{2,1,0:T(8,128)(2,1)S(1)}, u32[]{:S(2)}, u32[]{:S(2)}) collective-permute-start(bf16[2,256,256]{2,1,0:T(8,128)(2,1)S(1)} %add_convert_fusion.1), channel_id=1, source_target_pairs={{0,8},{1,9},{2,10},{3,11},{4,12},{5,13},{6,14},{7,15},{8,0},{9,1},... | collective-permute-start | bytes 786440 | tf_op jit(solution)/shard_map/ppermute | solution.py:149
  50.5 0.0 collective-permute-done.22
  50.6 2.7 %collective-permute-done.21 = bf16[256,256]{1,0:T(8,128)(2,1)S(1)} collective-permute-done((bf16[256,256]{1,0:T(8,128)(2,1)S(1)}, bf16[256,256]{1,0:T(8,128)(2,1)S(1)}, u32[]{:S(2)}, u32[]{:S(2)}) %collective-permute-start.21) | collective-permute-done | bytes 131104 | tf_op jit(solution)/shard_map/ppermute | solution.py:146
  53.3 0.0 collective-permute-done.20
  53.3 0.2 add_convert_fusion
  53.5 0.8 %collective-permute-start.23 = (bf16[2,256,256]{2,1,0:T(8,128)(2,1)S(1)}, bf16[2,256,256]{2,1,0:T(8,128)(2,1)S(1)}, u32[]{:S(2)}, u32[]{:S(2)}) collective-permute-start(bf16[2,256,256]{2,1,0:T(8,128)(2,1)S(1)} %add_convert_fusion), channel_id=1, source_target_pairs={{0,4},{1,5},{2,6},{3,7},{4,8},{5,9},{6,10},{7,11},{8,12},{9,13},{1... | collective-permute-start | bytes 786440 | tf_op jit(solution)/shard_map/ppermute | solution.py:149
  54.3 0.1 iota_compare_fusion.3
  54.4 1.3 %base.1 = f32[2,256,256]{2,1,0:T(8,128)S(1)} custom-call(s32[2]{0:T(128)} %size_ref.3, f32[2,256]{1,0:T(2,128)} %energy_ref.1, bf16[2,256,256]{2,1,0:T(8,128)(2,1)} %integral_ref.1, bf16[2,256,256]{2,1,0:T(8,128)(2,1)} %copy-done), custom_call_target="tpu_custom_call" | custom-call | tf_op jit(solution)/shard_map/base/pallas_call | solution.py:252
  55.7 12.2 %collective-permute-done.19 = bf16[2,256,256]{2,1,0:T(8,128)(2,1)S(1)} collective-permute-done((bf16[2,256,256]{2,1,0:T(8,128)(2,1)S(1)}, bf16[2,256,256]{2,1,0:T(8,128)(2,1)S(1)}, u32[]{:S(2)}, u32[]{:S(2)}) %collective-permute-start.19) | collective-permute-done | bytes 262176 | tf_op jit(solution)/shard_map/ppermute | solution.py:149
  67.8 0.0 collective-permute-done.23
  67.8 1.1 %add_select_fusion = f32[2,256,256]{2,1,0:T(8,128)} fusion(bf16[2,256,256]{2,1,0:T(8,128)(2,1)S(1)} %collective-permute-done.23, bf16[2,256,256]{2,1,0:T(8,128)(2,1)S(1)} %collective-permute-done.19, f32[2,256,256]{2,1,0:T(8,128)S(1)} %base.1, f32[256,256]{1,0:T(8,128)S(1)} %convert_element_type.50, f32[256,256]{1,0:T(8,128)S(1)} %convert_element_type.49, ...), kind=kLoop, calls=%fused_computation | loop fusion | flops 1835008 | bytes 2621960 | tf_op jit(solution)/shard_map/jit(_where)/select_n | solution.py:263
  (35 shorter events, 0.6 us)
Async XLA Ops:
  1.0 20.6 %copy-start = (bf16[2,256,256]{2,1,0:T(8,128)(2,1)}, bf16[2,256,256]{2,1,0:T(8,128)(2,1)S(1)}, u32[]{:S(2)}) copy-start(bf16[2,256,256]{2,1,0:T(8,128)(2,1)S(1)} %mask.1.masked_ref) | copy-start | bytes 786436
  1.1 12.5 %collective-permute-start = (bf16[2,256,256]{2,1,0:T(8,128)(2,1)S(1)}, bf16[2,256,256]{2,1,0:T(8,128)(2,1)S(1)}, u32[]{:S(2)}, u32[]{:S(2)}) collective-permute-start(bf16[2,256,256]{2,1,0:T(8,128)(2,1)S(1)} %mask.1.masked_ref), channel_id=1, source_target_pairs={{0,12},{1,13},{2,14},{3,15},{4,8},{5,9},{6,10},{7,11},{8,4},{9,5},... | collective-permute-start | bytes 786440 | tf_op jit(solution)/shard_map/ppermute | solution.py:146
  6.2 12.0 %collective-permute-start.3 = (bf16[2,256,256]{2,1,0:T(8,128)(2,1)S(1)}, bf16[2,256,256]{2,1,0:T(8,128)(2,1)S(1)}, u32[]{:S(2)}, u32[]{:S(2)}) collective-permute-start(bf16[2,256,256]{2,1,0:T(8,128)(2,1)S(1)} %mask.1.masked_ref), channel_id=1, source_target_pairs={{0,4},{1,5},{2,6},{3,7},{4,0},{5,1},{6,2},{7,3},{8,12},{9,13},{10,... | collective-permute-start | bytes 786440 | tf_op jit(solution)/shard_map/ppermute | solution.py:146
  6.2 15.5 %collective-permute-start.9 = (bf16[2,256,256]{2,1,0:T(8,128)(2,1)S(1)}, bf16[2,256,256]{2,1,0:T(8,128)(2,1)S(1)}, u32[]{:S(2)}, u32[]{:S(2)}) collective-permute-start(bf16[2,256,256]{2,1,0:T(8,128)(2,1)S(1)} %mask.1.masked_ref), channel_id=1, source_target_pairs={{0,1},{1,0},{2,3},{3,2},{4,5},{5,4},{6,7},{7,6},{8,9},{9,8},{10,11... | collective-permute-start | bytes 786440 | tf_op jit(solution)/shard_map/ppermute | solution.py:146
  6.2 13.7 %collective-permute-start.10 = (bf16[2,256,256]{2,1,0:T(8,128)(2,1)S(1)}, bf16[2,256,256]{2,1,0:T(8,128)(2,1)S(1)}, u32[]{:S(2)}, u32[]{:S(2)}) collective-permute-start(bf16[2,256,256]{2,1,0:T(8,128)(2,1)S(1)} %mask.1.masked_ref), channel_id=1, source_target_pairs={{0,2},{1,3},{2,0},{3,1},{4,6},{5,7},{6,4},{7,5},{8,10},{9,11},{10,... | collective-permute-start | bytes 786440 | tf_op jit(solution)/shard_map/ppermute | solution.py:146
  7.7 0.7 copy-start.1
  13.5 4.7 %collective-permute-start.7 = (bf16[2,256,256]{2,1,0:T(8,128)(2,1)S(1)}, bf16[2,256,256]{2,1,0:T(8,128)(2,1)S(1)}, u32[]{:S(2)}, u32[]{:S(2)}) collective-permute-start(bf16[2,256,256]{2,1,0:T(8,128)(2,1)S(1)} %collective-permute-done), channel_id=1, source_target_pairs={{0,1},{1,0},{2,3},{3,2},{4,5},{5,4},{6,7},{7,6},{8,9},{9,8},{10,11... | collective-permute-start | bytes 786440 | tf_op jit(solution)/shard_map/ppermute | solution.py:146
  13.8 15.2 %collective-permute-start.1 = (bf16[2,256,256]{2,1,0:T(8,128)(2,1)S(1)}, bf16[2,256,256]{2,1,0:T(8,128)(2,1)S(1)}, u32[]{:S(2)}, u32[]{:S(2)}) collective-permute-start(bf16[2,256,256]{2,1,0:T(8,128)(2,1)S(1)} %collective-permute-done), channel_id=1, source_target_pairs={{0,2},{1,3},{2,0},{3,1},{4,6},{5,7},{6,4},{7,5},{8,10},{9,11},{10,... | collective-permute-start | bytes 786440 | tf_op jit(solution)/shard_map/ppermute | solution.py:146
  18.2 3.4 %collective-permute-start.8 = (bf16[2,256,256]{2,1,0:T(8,128)(2,1)S(1)}, bf16[2,256,256]{2,1,0:T(8,128)(2,1)S(1)}, u32[]{:S(2)}, u32[]{:S(2)}) collective-permute-start(bf16[2,256,256]{2,1,0:T(8,128)(2,1)S(1)} %collective-permute-done.3), channel_id=1, source_target_pairs={{0,1},{1,0},{2,3},{3,2},{4,5},{5,4},{6,7},{7,6},{8,9},{9,8},{10,11... | collective-permute-start | bytes 786440 | tf_op jit(solution)/shard_map/ppermute | solution.py:146
  18.2 13.1 %collective-permute-start.4 = (bf16[2,256,256]{2,1,0:T(8,128)(2,1)S(1)}, bf16[2,256,256]{2,1,0:T(8,128)(2,1)S(1)}, u32[]{:S(2)}, u32[]{:S(2)}) collective-permute-start(bf16[2,256,256]{2,1,0:T(8,128)(2,1)S(1)} %collective-permute-done.3), channel_id=1, source_target_pairs={{0,2},{1,3},{2,0},{3,1},{4,6},{5,7},{6,4},{7,5},{8,10},{9,11},{10,... | collective-permute-start | bytes 786440 | tf_op jit(solution)/shard_map/ppermute | solution.py:146
  19.9 8.5 %collective-permute-start.6 = (bf16[2,256,256]{2,1,0:T(8,128)(2,1)S(1)}, bf16[2,256,256]{2,1,0:T(8,128)(2,1)S(1)}, u32[]{:S(2)}, u32[]{:S(2)}) collective-permute-start(bf16[2,256,256]{2,1,0:T(8,128)(2,1)S(1)} %collective-permute-done), channel_id=1, source_target_pairs={{0,4},{1,5},{2,6},{3,7},{4,0},{5,1},{6,2},{7,3},{8,12},{9,13},{10,... | collective-permute-start | bytes 786440 | tf_op jit(solution)/shard_map/ppermute | solution.py:146
  21.6 1.5 %collective-permute-start.11 = (bf16[2,256,256]{2,1,0:T(8,128)(2,1)S(1)}, bf16[2,256,256]{2,1,0:T(8,128)(2,1)S(1)}, u32[]{:S(2)}, u32[]{:S(2)}) collective-permute-start(bf16[2,256,256]{2,1,0:T(8,128)(2,1)S(1)} %collective-permute-done.10), channel_id=1, source_target_pairs={{0,1},{1,0},{2,3},{3,2},{4,5},{5,4},{6,7},{7,6},{8,9},{9,8},{10,11... | collective-permute-start | bytes 786440 | tf_op jit(solution)/shard_map/ppermute | solution.py:146
  28.4 5.0 %collective-permute-start.13 = (bf16[1,256,256]{2,1,0:T(8,128)(2,1)S(1)}, bf16[1,256,256]{2,1,0:T(8,128)(2,1)S(1)}, u32[]{:S(2)}, u32[]{:S(2)}) collective-permute-start(bf16[1,256,256]{2,1,0:T(8,128)(2,1)S(1)} %slice.89), channel_id=1, source_target_pairs={{0,2},{1,3},{2,0},{3,1},{4,6},{5,7},{6,4},{7,5},{8,10},{9,11},{10,... | collective-permute-start | bytes 393224 | tf_op jit(solution)/shard_map/ppermute | solution.py:146
  29.0 5.0 %collective-permute-start.14 = (bf16[1,256,256]{2,1,0:T(8,128)(2,1)S(1)}, bf16[1,256,256]{2,1,0:T(8,128)(2,1)S(1)}, u32[]{:S(2)}, u32[]{:S(2)}) collective-permute-start(bf16[1,256,256]{2,1,0:T(8,128)(2,1)S(1)} %slice.112), channel_id=1, source_target_pairs={{0,4},{1,5},{2,6},{3,7},{4,0},{5,1},{6,2},{7,3},{8,12},{9,13},{10,... | collective-permute-start | bytes 393224 | tf_op jit(solution)/shard_map/ppermute | solution.py:146
  30.7 3.4 %collective-permute-start.2 = (bf16[2,256,256]{2,1,0:T(8,128)(2,1)S(1)}, bf16[2,256,256]{2,1,0:T(8,128)(2,1)S(1)}, u32[]{:S(2)}, u32[]{:S(2)}) collective-permute-start(bf16[2,256,256]{2,1,0:T(8,128)(2,1)S(1)} %collective-permute-done.1), channel_id=1, source_target_pairs={{0,1},{1,0},{2,3},{3,2},{4,5},{5,4},{6,7},{7,6},{8,9},{9,8},{10,11... | collective-permute-start | bytes 786440 | tf_op jit(solution)/shard_map/ppermute | solution.py:146
  30.8 3.4 %collective-permute-start.12 = (bf16[2,256,256]{2,1,0:T(8,128)(2,1)S(1)}, bf16[2,256,256]{2,1,0:T(8,128)(2,1)S(1)}, u32[]{:S(2)}, u32[]{:S(2)}) collective-permute-start(bf16[2,256,256]{2,1,0:T(8,128)(2,1)S(1)} %collective-permute-done.6), channel_id=1, source_target_pairs={{0,1},{1,0},{2,3},{3,2},{4,5},{5,4},{6,7},{7,6},{8,9},{9,8},{10,11... | collective-permute-start | bytes 786440 | tf_op jit(solution)/shard_map/ppermute | solution.py:146
  31.3 2.9 %collective-permute-start.5 = (bf16[2,256,256]{2,1,0:T(8,128)(2,1)S(1)}, bf16[2,256,256]{2,1,0:T(8,128)(2,1)S(1)}, u32[]{:S(2)}, u32[]{:S(2)}) collective-permute-start(bf16[2,256,256]{2,1,0:T(8,128)(2,1)S(1)} %collective-permute-done.4), channel_id=1, source_target_pairs={{0,1},{1,0},{2,3},{3,2},{4,5},{5,4},{6,7},{7,6},{8,9},{9,8},{10,11... | collective-permute-start | bytes 786440 | tf_op jit(solution)/shard_map/ppermute | solution.py:146
  34.0 1.6 %collective-permute-start.15 = (bf16[2,256,256]{2,1,0:T(8,128)(2,1)S(1)}, bf16[2,256,256]{2,1,0:T(8,128)(2,1)S(1)}, u32[]{:S(2)}, u32[]{:S(2)}) collective-permute-start(bf16[2,256,256]{2,1,0:T(8,128)(2,1)S(1)} %pad_maximum_fusion), channel_id=1, source_target_pairs={{0,1},{1,0},{2,3},{3,2},{4,5},{5,4},{6,7},{7,6},{8,9},{9,8},{10,11... | collective-permute-start | bytes 786440 | tf_op jit(solution)/shard_map/ppermute | solution.py:146
  37.4 3.8 %collective-permute-start.16 = (bf16[256,256]{1,0:T(8,128)(2,1)S(1)}, bf16[256,256]{1,0:T(8,128)(2,1)S(1)}, u32[]{:S(2)}, u32[]{:S(2)}) collective-permute-start(bf16[256,256]{1,0:T(8,128)(2,1)S(1)} %get-tuple-element.18), channel_id=1, source_target_pairs={{0,1},{1,0},{2,3},{3,2},{4,5},{5,4},{6,7},{7,6},{8,9},{9,8},{10,11... | collective-permute-start | bytes 393224 | tf_op jit(solution)/shard_map/ppermute | solution.py:146
  38.6 7.1 %collective-permute-start.18 = (bf16[256,256]{1,0:T(8,128)(2,1)S(1)}, bf16[256,256]{1,0:T(8,128)(2,1)S(1)}, u32[]{:S(2)}, u32[]{:S(2)}) collective-permute-start(bf16[256,256]{1,0:T(8,128)(2,1)S(1)} %get-tuple-element.16), channel_id=1, source_target_pairs={{0,3},{1,2},{2,1},{3,0},{4,7},{5,6},{6,5},{7,4},{8,11},{9,10},{10,... | collective-permute-start | bytes 393224 | tf_op jit(solution)/shard_map/ppermute | solution.py:146
  40.8 7.5 %collective-permute-start.17 = (bf16[256,256]{1,0:T(8,128)(2,1)S(1)}, bf16[256,256]{1,0:T(8,128)(2,1)S(1)}, u32[]{:S(2)}, u32[]{:S(2)}) collective-permute-start(bf16[256,256]{1,0:T(8,128)(2,1)S(1)} %get-tuple-element.17), channel_id=1, source_target_pairs={{0,2},{1,3},{2,0},{3,1},{4,6},{5,7},{6,4},{7,5},{8,10},{9,11},{10,... | collective-permute-start | bytes 393224 | tf_op jit(solution)/shard_map/ppermute | solution.py:146
  43.0 7.5 %collective-permute-start.22 = (bf16[256,256]{1,0:T(8,128)(2,1)S(1)}, bf16[256,256]{1,0:T(8,128)(2,1)S(1)}, u32[]{:S(2)}, u32[]{:S(2)}) collective-permute-start(bf16[256,256]{1,0:T(8,128)(2,1)S(1)} %get-tuple-element.20), channel_id=1, source_target_pairs={{0,3},{1,2},{2,1},{3,0},{4,7},{5,6},{6,5},{7,4},{8,11},{9,10},{10,... | collective-permute-start | bytes 393224 | tf_op jit(solution)/shard_map/ppermute | solution.py:146
  45.4 7.8 %collective-permute-start.21 = (bf16[256,256]{1,0:T(8,128)(2,1)S(1)}, bf16[256,256]{1,0:T(8,128)(2,1)S(1)}, u32[]{:S(2)}, u32[]{:S(2)}) collective-permute-start(bf16[256,256]{1,0:T(8,128)(2,1)S(1)} %get-tuple-element.21), channel_id=1, source_target_pairs={{0,2},{1,3},{2,0},{3,1},{4,6},{5,7},{6,4},{7,5},{8,10},{9,11},{10,... | collective-permute-start | bytes 393224 | tf_op jit(solution)/shard_map/ppermute | solution.py:146
  45.7 7.6 %collective-permute-start.20 = (bf16[256,256]{1,0:T(8,128)(2,1)S(1)}, bf16[256,256]{1,0:T(8,128)(2,1)S(1)}, u32[]{:S(2)}, u32[]{:S(2)}) collective-permute-start(bf16[256,256]{1,0:T(8,128)(2,1)S(1)} %get-tuple-element.22), channel_id=1, source_target_pairs={{0,1},{1,0},{2,3},{3,2},{4,5},{5,4},{6,7},{7,6},{8,9},{9,8},{10,11... | collective-permute-start | bytes 393224 | tf_op jit(solution)/shard_map/ppermute | solution.py:146
  45.8 8.5 %copy-start.2 = (s32[2]{0:T(128)S(1)}, s32[2]{0:T(128)}, u32[]{:S(2)}) copy-start(s32[2]{0:T(128)} %size_ref.3) | copy-start | bytes 28
  48.5 19.3 %collective-permute-start.19 = (bf16[2,256,256]{2,1,0:T(8,128)(2,1)S(1)}, bf16[2,256,256]{2,1,0:T(8,128)(2,1)S(1)}, u32[]{:S(2)}, u32[]{:S(2)}) collective-permute-start(bf16[2,256,256]{2,1,0:T(8,128)(2,1)S(1)} %add_convert_fusion.1), channel_id=1, source_target_pairs={{0,8},{1,9},{2,10},{3,11},{4,12},{5,13},{6,14},{7,15},{8,0},{9,1},... | collective-permute-start | bytes 786440 | tf_op jit(solution)/shard_map/ppermute | solution.py:149
  53.5 14.3 %collective-permute-start.23 = (bf16[2,256,256]{2,1,0:T(8,128)(2,1)S(1)}, bf16[2,256,256]{2,1,0:T(8,128)(2,1)S(1)}, u32[]{:S(2)}, u32[]{:S(2)}) collective-permute-start(bf16[2,256,256]{2,1,0:T(8,128)(2,1)S(1)} %add_convert_fusion), channel_id=1, source_target_pairs={{0,4},{1,5},{2,6},{3,7},{4,8},{5,9},{6,10},{7,11},{8,12},{9,13},{1... | collective-permute-start | bytes 786440 | tf_op jit(solution)/shard_map/ppermute | solution.py:149
